TPU v7x, 512 devices: a whole 4x8x8 slice. The times are simulated.
512 devices in a mesh: cols: 128 (over x, z_lo, y), rows: 4 (over z_hi, core).
Axes of the slice: x: 4, y: 8, z: 8 (z_hi: 2, z_lo: 4; z = z_hi * 4 + z_lo), core: 2. Of those that a mesh axis runs over, the one named last changes fastest.
Arguments:
- tokens: bfloat16 [64, 1024, 256], P('rows', 'cols'), may hold values from -600 to 600
- edge_tokens: bfloat16 [2, 3, 1024, 256], P(None, None, 'cols'), may hold values from -18 to 18
- output_grad: bfloat16 [64, 1024, 256], P('rows', 'cols'), may hold values from -24 to 24
- norm_gain: float32 [256], replicated, may hold values from 0.1 to 1.9
- qkv_weight: bfloat16 [256, 768], replicated, may hold values from -0.4 to 0.4
- out_weight: bfloat16 [256, 256], replicated, may hold values from -0.375 to 0.375
- head_scale: float32 [4], replicated, may hold values from 1 to 256
Outputs:
- token_grad: bfloat16 [64, 1024, 256], P('rows', 'cols')
- qkv_grad: float32 [256, 768], P(None, 'cols')
- proj_grad: float32 [256, 256], P(None, 'cols')
- gain_grad: float32 [256], P('cols')
All inputs are finite; a program needn't handle non-finite values.
Results may differ from a plain program's by a relative error of at most 0.0087.
Values may be sent and summed in bfloat16 or wider, within the bound.
No kernel may reach another device: no remote copies, remote signals or barrier semaphores. Data moves between devices by JAX's collectives and lax.ppermute only.
A program may use at most 64 MiB of HBM per device.

v0:
```python
import jax
import jax.numpy as jnp
from jax import lax
from jax.sharding import PartitionSpec as P

HEAD_DIM = 64
RADIUS = 3


EPSILON = 1e-06
PRECISE = lax.Precision.HIGHEST


def padded_2(cells, sides, width, closed):
    for axis, dim in sides:
        count = lax.axis_size(axis)
        ends = count if closed else count - 1
        head = lax.slice_in_dim(cells, 0, width, axis=dim)
        tail = lax.slice_in_dim(cells, cells.shape[dim] - width, cells.shape[dim], axis=dim)
        cells = jnp.concatenate(
            [
                lax.ppermute(tail, axis, [(i, (i + 1) % count) for i in range(ends)]),
                cells,
                lax.ppermute(head, axis, [((i + 1) % count, i) for i in range(ends)]),
            ],
            axis=dim,
        )
    return cells


def head_norm(raw_values):
    heads_view = raw_values.reshape(raw_values.shape[0], -1, HEAD_DIM)
    reciprocal = lax.rsqrt(jnp.mean(heads_view * heads_view, axis=-1, keepdims=True) + EPSILON)
    return (heads_view * reciprocal, reciprocal)


def head_back(grad_hat, unit_rows, reciprocal):
    return reciprocal * (
        grad_hat - unit_rows * jnp.mean(grad_hat * unit_rows, axis=-1, keepdims=True)
    )


def project_in(tokens, norm_gain, qkv_weight):
    feature_width = tokens.shape[-1]
    flat_rows = tokens.reshape(-1, feature_width).astype(jnp.float32)
    reciprocal = lax.rsqrt(jnp.mean(flat_rows * flat_rows, axis=-1, keepdims=True) + EPSILON)
    unit_rows = flat_rows * reciprocal
    normed = (unit_rows * norm_gain).astype(jnp.bfloat16)
    projected = jnp.dot(normed, qkv_weight, preferred_element_type=jnp.float32)
    queries, query_recip = head_norm(projected[:, :feature_width])
    key_rows, key_recip = head_norm(projected[:, feature_width : 2 * feature_width])
    values = projected[:, 2 * feature_width :]
    return (unit_rows, reciprocal, normed, queries, query_recip, key_rows, key_recip, values)


def key_value(stored, row_count, col_count):
    values = stored[7]
    feature_width = values.shape[1]
    joined = jnp.concatenate([stored[5].reshape(-1, feature_width), values], axis=1)
    return joined.astype(jnp.bfloat16).reshape(row_count, col_count, 2 * feature_width)


def project_back(stored, query_grad, key_grad, value_grad, norm_gain, qkv_weight):
    unit_rows, reciprocal, normed, queries, query_recip, key_rows, key_recip, values = stored
    token_count, feature_width = unit_rows.shape
    raw_query = head_back(query_grad.reshape(queries.shape), queries, query_recip).reshape(
        token_count, feature_width
    )
    raw_key = head_back(key_grad.reshape(key_rows.shape), key_rows, key_recip).reshape(
        token_count, feature_width
    )
    projected_grad = jnp.concatenate([raw_query, raw_key, value_grad], axis=1)
    weight_grad = jnp.dot(normed.astype(jnp.float32).T, projected_grad, precision=PRECISE)
    normed_grad = jnp.dot(projected_grad, qkv_weight.astype(jnp.float32).T, precision=PRECISE)
    gain_part = jnp.sum(normed_grad * unit_rows, axis=0)
    scaled = normed_grad * norm_gain
    token_part = reciprocal * (
        scaled - unit_rows * jnp.mean(scaled * unit_rows, axis=-1, keepdims=True)
    )
    return (token_part, weight_grad, gain_part)


def attend(query_b, padded, upstream, head_scale):
    row_count, col_count, feature_width = query_b.shape
    head_count = feature_width // HEAD_DIM
    reach = 2 * RADIUS
    band = 16
    wide_cols = col_count + reach
    factor = head_scale / HEAD_DIM
    query_pos = jnp.arange(band * col_count, dtype=jnp.int32)
    key_pos = jnp.arange((band + reach) * wide_cols, dtype=jnp.int32)
    row_gap = (key_pos // wide_cols)[None, :] - (query_pos // col_count)[:, None]
    col_gap = (key_pos % wide_cols)[None, :] - (query_pos % col_count)[:, None]
    inside = (row_gap >= 0) & (row_gap <= reach) & (col_gap >= 0) & (col_gap <= reach)
    grad_pad = jnp.zeros((row_count + reach, wide_cols, 2 * feature_width), jnp.float32)
    queries = query_b.reshape(-1, head_count, HEAD_DIM).astype(jnp.float32)
    incoming = upstream.reshape(-1, head_count, HEAD_DIM).astype(jnp.float32)
    kv_band = padded.reshape(-1, 2, head_count, HEAD_DIM).astype(jnp.float32)
    attended_heads = []
    query_heads = []
    key_heads = []
    value_heads = []
    for head in range(head_count):
        query_h = queries[:, head]
        income_h = incoming[:, head]
        key_h = kv_band[:, 0, head]
        value_h = kv_band[:, 1, head]
        scores = jnp.dot(query_h, key_h.T, precision=PRECISE) * factor[head]
        scores = jnp.where(inside, scores, -1e30)
        maximum = jnp.max(scores, axis=1, keepdims=True)
        exponent = jnp.where(inside, jnp.exp(scores - maximum), 0.0)
        prob = exponent / jnp.sum(exponent, axis=1, keepdims=True)
        attended_heads.append(jnp.dot(prob, value_h, precision=PRECISE))
        dots = jnp.dot(income_h, value_h.T, precision=PRECISE)
        mean_dot = jnp.sum(prob * dots, axis=1, keepdims=True)
        weighted = prob * (dots - mean_dot) * factor[head]
        query_heads.append(jnp.dot(weighted, key_h, precision=PRECISE))
        key_heads.append(jnp.dot(weighted.T, query_h, precision=PRECISE))
        value_heads.append(jnp.dot(prob.T, income_h, precision=PRECISE))
    attended_bands = jnp.concatenate(attended_heads, axis=1)
    query_bands = jnp.stack(query_heads, axis=1)
    block = jnp.concatenate(key_heads + value_heads, axis=1).reshape(
        band + reach, wide_cols, 2 * feature_width
    )
    grad_pad = grad_pad.at[0 : band + reach].add(block)
    attended = attended_bands.reshape(row_count, col_count, feature_width)
    return (attended.astype(jnp.bfloat16), query_bands, grad_pad)


def fold_back(grid, send_cols, send_rows):
    row_count = grid.shape[0] - 2 * RADIUS
    col_count = grid.shape[1] - 2 * RADIUS
    side_strips = jnp.concatenate([grid[:, :RADIUS], grid[:, col_count + RADIUS :]], axis=1)
    returned = send_cols(side_strips)
    middle = grid[:, RADIUS : col_count + RADIUS]
    middle = middle.at[:, :RADIUS].add(returned[:, :RADIUS])
    middle = middle.at[:, col_count - RADIUS :].add(returned[:, 3 * RADIUS :])
    end_strips = jnp.concatenate([middle[:RADIUS], middle[row_count + RADIUS :]], axis=0)
    arrived = send_rows(end_strips)
    interior = middle[RADIUS : row_count + RADIUS]
    interior = interior.at[:RADIUS].add(arrived[:RADIUS])
    interior = interior.at[row_count - RADIUS :].add(arrived[3 * RADIUS :])
    return (middle, interior)


def own_columns(whole):
    share_width = whole.shape[1] // lax.axis_size("cols")
    return lax.dynamic_slice_in_dim(whole, lax.axis_index("cols") * share_width, share_width, 1)


def on_device(tokens, edge_tokens, output_grad, norm_gain, qkv_weight, out_weight, head_scale):
    row_count, col_count, feature_width = tokens.shape
    top_device = lax.axis_index("rows") == 0
    bottom_device = lax.axis_index("rows") == lax.axis_size("rows") - 1
    token_total = row_count * lax.axis_size("rows") * col_count * lax.axis_size("cols")
    grad_scale = token_total ** (-0.5)
    flat_grad = output_grad.reshape(-1, feature_width)
    upstream = jnp.dot(flat_grad, out_weight.T, preferred_element_type=jnp.float32).astype(
        jnp.bfloat16
    )
    upstream = upstream.reshape(row_count, col_count, feature_width)
    stored = project_in(tokens, norm_gain, qkv_weight)
    edge_stored = project_in(edge_tokens, norm_gain, qkv_weight)
    local_kv = key_value(stored, row_count, col_count)
    edge_kv = key_value(edge_stored, 2 * RADIUS, col_count)
    tall_grid = padded_2(local_kv, (("rows", 0),), RADIUS, False)
    upper = jnp.where(top_device, edge_kv[:RADIUS], tall_grid[:RADIUS])
    lower = jnp.where(bottom_device, edge_kv[RADIUS:], tall_grid[row_count + RADIUS :])
    tall_grid = jnp.concatenate([upper, tall_grid[RADIUS : row_count + RADIUS], lower], axis=0)
    padded = padded_2(tall_grid, (("cols", 1),), RADIUS, True)
    queries = stored[3].reshape(row_count, col_count, feature_width).astype(jnp.bfloat16)
    attended, query_grad, grad_pad = attend(queries, padded, upstream, head_scale)

    def send_key_cols(strips):
        return padded_2(strips.astype(jnp.bfloat16), (("cols", 1),), RADIUS, True).astype(
            strips.dtype
        )

    def send_key_rows(strips):
        return padded_2(strips.astype(jnp.bfloat16), (("rows", 0),), RADIUS, False).astype(
            strips.dtype
        )

    middle, interior = fold_back(grad_pad, send_key_cols, send_key_rows)
    kv_grad = interior.reshape(-1, 2 * feature_width)
    token_part, qkv_sum, gain_sum = project_back(
        stored,
        query_grad.reshape(-1, feature_width),
        kv_grad[:, :feature_width],
        kv_grad[:, feature_width:],
        norm_gain,
        qkv_weight,
    )
    upper_grad = jnp.where(top_device, middle[:RADIUS], 0.0)
    lower_grad = jnp.where(bottom_device, middle[row_count + RADIUS :], 0.0)
    edge_grad = jnp.concatenate([upper_grad, lower_grad], axis=0).reshape(-1, 2 * feature_width)
    edge_zero = jnp.zeros((edge_grad.shape[0], feature_width), jnp.float32)
    edge_part, edge_qkv, edge_gain = project_back(
        edge_stored,
        edge_zero,
        edge_grad[:, :feature_width],
        edge_grad[:, feature_width:],
        norm_gain,
        qkv_weight,
    )
    qkv_sum = qkv_sum + edge_qkv
    gain_sum = gain_sum + edge_gain
    branch_grad = token_part.reshape(row_count, col_count, feature_width)
    token_grad = (output_grad.astype(jnp.float32) + branch_grad).astype(jnp.bfloat16)
    proj_sum = jnp.dot(
        attended.reshape(-1, feature_width).T, flat_grad, preferred_element_type=jnp.float32
    )
    gain_row = gain_sum[None, :]
    qkv_whole, proj_whole, gain_whole = lax.psum((qkv_sum, proj_sum, gain_row), ("cols", "rows"))
    qkv_part = own_columns(qkv_whole)
    proj_part = own_columns(proj_whole)
    gain_part = own_columns(gain_whole)
    return (
        token_grad,
        qkv_part * grad_scale,
        proj_part * grad_scale,
        (gain_part * grad_scale).reshape(-1),
    )


def solution(mesh):
    return jax.shard_map(
        on_device,
        mesh=mesh,
        in_specs=(
            P("rows", "cols", None),
            P(None, None, "cols", None),
            P("rows", "cols", None),
            P(),
            P(),
            P(),
            P(),
        ),
        out_specs=(P("rows", "cols", None), P(None, "cols"), P(None, "cols"), P("cols")),
        check_vma=False,
    )
```

profile of v0, /device:TPU:1, one launch (start us, length us, event | category | flops | bytes accessed | tf_op | source)
XLA Modules:
  0.0 489.4 jit_solution(4403459563142128915)
XLA Ops:
  7.2 1.0 fusion.10
  9.5 12.0 %collective-permute-start = (bf16[3,8,512]{2,1,0:T(8,128)(2,1)S(1)}, bf16[3,8,512]{2,1,0:T(8,128)(2,1)S(1)}, u32[]{:S(2)}, u32[]{:S(2)}) collective-permute-start(bf16[3,8,512]{2,1,0:T(8,128)(2,1)S(1)} %get-tuple-element.111), channel_id=1, source_target_pairs={{0,1},{1,2},{2,3},{4,5},{5,6},{6,7},{8,9},{9,10},{10,11},{12,13},{... | collective-permute-start | bytes 73736 | tf_op jit(solution)/shard_map/ppermute | solution.py:22
  21.5 1.9 collective-permute-start.1
  32.4 10.0 %collective-permute-start.3 = (bf16[22,3,512]{2,1,0:T(4,128)(2,1)S(1)}, bf16[22,3,512]{2,1,0:T(4,128)(2,1)S(1)}, u32[]{:S(2)}, u32[]{:S(2)}) collective-permute-start(bf16[22,3,512]{2,1,0:T(4,128)(2,1)S(1)} %get-tuple-element.104), channel_id=1, source_target_pairs={{4,0},{8,4},{12,8},{16,12},{20,16},{24,20},{28,24},{32,28},{36,32}... | collective-permute-start | bytes 202760 | tf_op jit(solution)/shard_map/ppermute | solution.py:24
  42.4 1.9 collective-permute-start.2
  44.4 9.3 %collective-permute-done.2 = bf16[22,3,512]{2,1,0:T(4,128)(2,1)S(1)} collective-permute-done((bf16[22,3,512]{2,1,0:T(4,128)(2,1)S(1)}, bf16[22,3,512]{2,1,0:T(4,128)(2,1)S(1)}, u32[]{:S(2)}, u32[]{:S(2)}) %collective-permute-start.2) | collective-permute-done | bytes 67616 | tf_op jit(solution)/shard_map/ppermute | solution.py:22
  60.3 0.9 fusion.123
  61.9 1.0 convolution_bitcast_fusion.4
  62.9 1.6 convolution_dynamic-update-slice_fusion.7
  64.5 1.0 convolution_bitcast_fusion.3
  65.5 1.6 convolution_dynamic-update-slice_fusion.6
  67.1 1.0 convolution_bitcast_fusion.2
  68.1 1.6 convolution_dynamic-update-slice_fusion.5
  69.7 1.0 convolution_bitcast_fusion.1
  70.7 1.6 convolution_dynamic-update-slice_fusion.4
  72.4 1.0 convolution_dynamic-update-slice_fusion.3
  73.3 1.0 convolution_dynamic-update-slice_fusion.2
  74.3 1.0 convolution_dynamic-update-slice_fusion.1
  75.3 1.0 convolution_dynamic-update-slice_fusion
  76.3 1.4 copy.38
  81.6 1.9 collective-permute-start.5
  83.6 3.4 collective-permute-start.4
  87.1 7.8 %collective-permute-done.4 = bf16[22,3,512]{2,1,0:T(4,128)(2,1)S(1)} collective-permute-done((bf16[22,3,512]{2,1,0:T(4,128)(2,1)S(1)}, bf16[22,3,512]{2,1,0:T(4,128)(2,1)S(1)}, u32[]{:S(2)}, u32[]{:S(2)}) %collective-permute-start.4) | collective-permute-done | bytes 67616 | tf_op jit(solution)/shard_map/ppermute | solution.py:22
  95.0 1.2 scatter-add.14
  96.5 1.2 scatter-add.15
  97.7 1.9 collective-permute-start.7
  99.6 10.4 %collective-permute-start.6 = (bf16[3,8,512]{2,1,0:T(8,128)(2,1)S(1)}, bf16[3,8,512]{2,1,0:T(8,128)(2,1)S(1)}, u32[]{:S(2)}, u32[]{:S(2)}) collective-permute-start(bf16[3,8,512]{2,1,0:T(8,128)(2,1)S(1)} %get-tuple-element.98), channel_id=1, source_target_pairs={{0,1},{1,2},{2,3},{4,5},{5,6},{6,7},{8,9},{9,10},{10,11},{12,13},{... | collective-permute-start | bytes 73736 | tf_op jit(solution)/shard_map/ppermute | solution.py:22
  116.2 1.4 convolution_add_fusion
  117.6 93.2 %psum.23 = f32[1,256]{1,0:T(1,128)S(1)} all-reduce(f32[1,256]{1,0:T(1,128)S(1)} %bitcast.213), channel_id=1, replica_groups=mesh['cols'=128,'rows'=4] {'cols','rows'}, use_global_device_ids=true, to_apply=%region_27.28 | all-reduce | flops 256 | bytes 2048 | tf_op jit(solution)/shard_map/psum | solution.py:214
  212.2 267.8 %all-reduce.3.cloned.1.call-done = (f32[256,768]{0,1:T(8,128)}, f32[256,256]{0,1:T(8,128)}) async-done(((f32[256,768]{0,1:T(8,128)}, f32[256,256]{0,1:T(8,128)}), (f32[256,768]{0,1:T(8,128)}, f32[256,256]{0,1:T(8,128)})) %all-reduce.3.cloned.1.call-update) | async-done | bytes 1048592 | tf_op jit(solution)/shard_map/psum | solution.py:214
  480.0 1.3 dynamic-slice_multiply_fusion.1
  481.2 1.3 dynamic-slice_multiply_fusion
  (177 shorter events, 28.8 us)
Async XLA Ops:
  7.2 1.2 copy-start
  7.2 1.2 copy-start.1
  7.2 472.8 %all-reduce.3.cloned.1.call-start = ((), (), s32[]{:S(2)}) async-start(), calls=%async_computation | async-start | bytes 2097152 | tf_op jit(solution)/shard_map/psum | solution.py:214
  8.2 0.7 copy-start.14
  9.5 22.8 %collective-permute-start = (bf16[3,8,512]{2,1,0:T(8,128)(2,1)S(1)}, bf16[3,8,512]{2,1,0:T(8,128)(2,1)S(1)}, u32[]{:S(2)}, u32[]{:S(2)}) collective-permute-start(bf16[3,8,512]{2,1,0:T(8,128)(2,1)S(1)} %get-tuple-element.111), channel_id=1, source_target_pairs={{0,1},{1,2},{2,3},{4,5},{5,6},{6,7},{8,9},{9,10},{10,11},{12,13},{... | collective-permute-start | bytes 73736 | tf_op jit(solution)/shard_map/ppermute | solution.py:22
  21.5 10.8 %collective-permute-start.1 = (bf16[3,8,512]{2,1,0:T(8,128)(2,1)S(1)}, bf16[3,8,512]{2,1,0:T(8,128)(2,1)S(1)}, u32[]{:S(2)}, u32[]{:S(2)}) collective-permute-start(bf16[3,8,512]{2,1,0:T(8,128)(2,1)S(1)} %get-tuple-element.112), channel_id=1, source_target_pairs={{1,0},{2,1},{3,2},{5,4},{6,5},{7,6},{9,8},{10,9},{11,10},{13,12},{... | collective-permute-start | bytes 73736 | tf_op jit(solution)/shard_map/ppermute | solution.py:24
  23.6 1.4 copy-start.12
  28.0 0.9 copy-start.11
  28.0 0.9 copy-start.2
  32.4 12.0 %collective-permute-start.3 = (bf16[22,3,512]{2,1,0:T(4,128)(2,1)S(1)}, bf16[22,3,512]{2,1,0:T(4,128)(2,1)S(1)}, u32[]{:S(2)}, u32[]{:S(2)}) collective-permute-start(bf16[22,3,512]{2,1,0:T(4,128)(2,1)S(1)} %get-tuple-element.104), channel_id=1, source_target_pairs={{4,0},{8,4},{12,8},{16,12},{20,16},{24,20},{28,24},{32,28},{36,32}... | collective-permute-start | bytes 202760 | tf_op jit(solution)/shard_map/ppermute | solution.py:24
  42.4 11.3 %collective-permute-start.2 = (bf16[22,3,512]{2,1,0:T(4,128)(2,1)S(1)}, bf16[22,3,512]{2,1,0:T(4,128)(2,1)S(1)}, u32[]{:S(2)}, u32[]{:S(2)}) collective-permute-start(bf16[22,3,512]{2,1,0:T(4,128)(2,1)S(1)} %get-tuple-element.103), channel_id=1, source_target_pairs={{0,4},{4,8},{8,12},{12,16},{16,20},{20,24},{24,28},{28,32},{32,36}... | collective-permute-start | bytes 202760 | tf_op jit(solution)/shard_map/ppermute | solution.py:22
  44.4 30.9 %copy-start.17 = (s32[128]{0:T(128)}, s32[128]{0:T(128)S(1)}, u32[]{:S(2)}) copy-start(s32[128]{0:T(128)S(1)} %get-tuple-element.133) | copy-start | bytes 1540
  44.4 30.9 %copy-start.19 = (s32[128]{0:T(128)}, s32[128]{0:T(128)S(1)}, u32[]{:S(2)}) copy-start(s32[128]{0:T(128)S(1)} %get-tuple-element.134) | copy-start | bytes 1540
  56.5 0.9 copy-start.13
  56.5 0.8 copy-start.16
  56.7 0.7 copy-start.15
  59.4 13.0 %copy-start.22 = (f32[128,308]{0,1:T(8,128)}, f32[128,308]{0,1:T(8,128)S(1)}, u32[]{:S(2)}) copy-start(f32[128,308]{0,1:T(8,128)S(1)} %get-tuple-element.123) | copy-start | bytes 473092
  60.3 13.0 %copy-start.24 = (f32[128,308]{0,1:T(8,128)}, f32[128,308]{0,1:T(8,128)S(1)}, u32[]{:S(2)}) copy-start(f32[128,308]{0,1:T(8,128)S(1)} %get-tuple-element.125) | copy-start | bytes 473092
  61.3 13.0 %copy-start.26 = (f32[128,308]{0,1:T(8,128)}, f32[128,308]{0,1:T(8,128)S(1)}, u32[]{:S(2)}) copy-start(f32[128,308]{0,1:T(8,128)S(1)} %get-tuple-element.127) | copy-start | bytes 473092
  78.4 0.9 copy-start.27
  79.3 0.9 copy-start.25
  80.3 0.9 copy-start.23
  81.6 5.4 %collective-permute-start.5 = (bf16[22,3,512]{2,1,0:T(4,128)(2,1)S(1)}, bf16[22,3,512]{2,1,0:T(4,128)(2,1)S(1)}, u32[]{:S(2)}, u32[]{:S(2)}) collective-permute-start(bf16[22,3,512]{2,1,0:T(4,128)(2,1)S(1)} %get-tuple-element.101), channel_id=1, source_target_pairs={{4,0},{8,4},{12,8},{16,12},{20,16},{24,20},{28,24},{32,28},{36,32}... | collective-permute-start | bytes 202760 | tf_op jit(solution)/shard_map/ppermute | solution.py:24
  83.6 11.3 %collective-permute-start.4 = (bf16[22,3,512]{2,1,0:T(4,128)(2,1)S(1)}, bf16[22,3,512]{2,1,0:T(4,128)(2,1)S(1)}, u32[]{:S(2)}, u32[]{:S(2)}) collective-permute-start(bf16[22,3,512]{2,1,0:T(4,128)(2,1)S(1)} %get-tuple-element.100), channel_id=1, source_target_pairs={{0,4},{4,8},{8,12},{12,16},{16,20},{20,24},{24,28},{28,32},{32,36}... | collective-permute-start | bytes 202760 | tf_op jit(solution)/shard_map/ppermute | solution.py:22
  97.7 12.4 %copy-start.3 = (bf16[16,8,256]{2,1,0:T(8,128)(2,1)S(1)}, bf16[16,8,256]{2,1,0:T(8,128)(2,1)}, u32[]{:S(2)}) copy-start(bf16[16,8,256]{2,1,0:T(8,128)(2,1)} %param.21) | copy-start | bytes 196612
  97.7 13.5 %collective-permute-start.7 = (bf16[3,8,512]{2,1,0:T(8,128)(2,1)S(1)}, bf16[3,8,512]{2,1,0:T(8,128)(2,1)S(1)}, u32[]{:S(2)}, u32[]{:S(2)}) collective-permute-start(bf16[3,8,512]{2,1,0:T(8,128)(2,1)S(1)} %get-tuple-element.99), channel_id=1, source_target_pairs={{1,0},{2,1},{3,2},{5,4},{6,5},{7,6},{9,8},{10,9},{11,10},{13,12},{... | collective-permute-start | bytes 73736 | tf_op jit(solution)/shard_map/ppermute | solution.py:24
  99.6 11.6 %collective-permute-start.6 = (bf16[3,8,512]{2,1,0:T(8,128)(2,1)S(1)}, bf16[3,8,512]{2,1,0:T(8,128)(2,1)S(1)}, u32[]{:S(2)}, u32[]{:S(2)}) collective-permute-start(bf16[3,8,512]{2,1,0:T(8,128)(2,1)S(1)} %get-tuple-element.98), channel_id=1, source_target_pairs={{0,1},{1,2},{2,3},{4,5},{5,6},{6,7},{8,9},{9,10},{10,11},{12,13},{... | collective-permute-start | bytes 73736 | tf_op jit(solution)/shard_map/ppermute | solution.py:22
  111.5 0.9 copy-start.4
  113.7 0.7 copy-start.8
  114.8 0.8 copy-start.6
  114.8 0.8 copy-start.9
  114.8 0.8 copy-start.10
  (5 other events, 3.1 us)
Sparse Core Ops, SparseCore 0:
  211.0 268.9 all-reduce.2
where the time goes:
time: 491 us; the launch traced here: 489 us
  waiting for transfers between devices  285 us (58%)
  blocking collectives  93.2 us (19%)
  starting transfers between devices  43.5 us (9%)
  matrix products  25.2 us (5%)
  local copies, waits for them, and re-layouts  19.5 us (4%)
  between operations  14.9 us (3%)
  other arithmetic  8.16 us (2%)
    psum x1, waiting for transfers between devices, on_device(): lax.psum((qkv_sum, proj_sum, gain_row), ('cols', 'rows'))  268 us
    psum x1, blocking collectives, on_device(): lax.psum((qkv_sum, proj_sum, gain_row), ('cols', 'rows'))  93.2 us
    ppermute x4, starting transfers between devices, padded_2(): lax.ppermute(tail, axis, [(i, (i + 1) % count) for i in range(ends)])  27.7 us
    ppermute x4, waiting for transfers between devices, padded_2(): lax.ppermute(tail, axis, [(i, (i + 1) % count) for i in range(ends)])  17.1 us
    ppermute x4, starting transfers between devices, padded_2(): lax.ppermute(head, axis, [((i + 1) % count, i) for i in range(ends)])  15.8 us
  transfers between devices with their start and end apart: 9, of which 3 were waited for; matrix products, arithmetic and copies ran while one was open for 2% of the time, Pallas kernels for 0%

commit v1 on v0

v1 whole, which is shorter than its diff:
```python
import jax
import jax.numpy as jnp
from jax import lax
from jax.experimental import pallas as pl
from jax.experimental.pallas import tpu as pltpu
from jax.sharding import PartitionSpec as P

HEAD_DIM = 64
HEADS = 4
RADIUS = 3
EPSILON = 1e-06

SPAN = 32
REACH = 2 * RADIUS
BAND = 4
LOWEST = -1e30
F32 = jnp.float32
BF16 = jnp.bfloat16


def dot(left, right, left_dim=1, right_dim=0):
    return lax.dot_general(
        left, right, (((left_dim,), (right_dim,)), ((), ())), preferred_element_type=F32
    )


def head_mean(values, group):
    high = values.astype(BF16)
    low = (values - high.astype(F32)).astype(BF16)
    return (dot(high, group) + dot(low, group)) * (1.0 / HEAD_DIM)


def unit_norm(cells):
    rows = cells.astype(F32)
    reciprocal = lax.rsqrt(jnp.mean(rows * rows, axis=-1, keepdims=True) + EPSILON)
    return rows * reciprocal, reciprocal


def head_norm(raw, group):
    reciprocal = lax.rsqrt(head_mean(raw * raw, group) + EPSILON)
    return raw * reciprocal, reciprocal


def head_back(grad, hat, reciprocal, group):
    return reciprocal * (grad - hat * head_mean(grad * hat, group))


def block_kernel(
    place_ref, scale_ref, own_ref, own_grad_ref, west_ref, east_ref, gain_ref, qkv_ref, out_ref,
    token_ref, qkv_grad_ref, proj_grad_ref, gain_grad_ref,
    key_ref, value_ref, key_grad_ref, value_grad_ref,
):
    width = own_ref.shape[1]
    own_count = own_ref.shape[0]
    strip = REACH * SPAN
    top = place_ref[0] == 0
    bottom = place_ref[0] == place_ref[1] - 1
    gain = gain_ref[...]
    weight = qkv_ref[...]
    lane_head = lax.broadcasted_iota(jnp.int32, (width, width), 0) // HEAD_DIM
    group = (lane_head == lax.broadcasted_iota(jnp.int32, (width, width), 1) // HEAD_DIM).astype(BF16)

    def row_in(count):
        return lax.broadcasted_iota(jnp.int32, (count, 1), 0) & (SPAN - 1)

    def query_rows(count):
        row = row_in(count)
        own = row < 16
        below = (row >= 16) & (row < 16 + RADIUS) & jnp.logical_not(bottom)
        above = (row >= SPAN - RADIUS) & jnp.logical_not(top)
        return own | below | above

    def keys_of(cells, start):
        unit, reciprocal = unit_norm(cells)
        normed = (unit * gain).astype(BF16)
        keys, key_recip = head_norm(dot(normed, weight[:, width : 2 * width]), group)
        values = dot(normed, weight[:, 2 * width :])
        key_ref[start : start + cells.shape[0]] = keys.astype(BF16)
        value_ref[start : start + cells.shape[0]] = values.astype(BF16)
        return unit, reciprocal, normed, keys, key_recip

    def queries_of(normed):
        return head_norm(dot(normed, weight[:, :width]), group)

    unit, reciprocal, normed, keys, key_recip = keys_of(own_ref[...], strip)
    queries, query_recip = queries_of(normed)
    west_normed = keys_of(west_ref[:strip], 0)[2]
    east_normed = keys_of(east_ref[:strip], strip + own_count)[2]
    band = BAND * SPAN
    west_query = queries_of(west_normed[strip - band :])[0]
    east_query = queries_of(east_normed[:band])[0]

    own_grad = own_grad_ref[...]
    out_weight = out_ref[...]
    own_up = dot(own_grad, out_weight, 1, 1)
    west_up = dot(west_ref[strip:], out_weight, 1, 1)
    east_up = dot(east_ref[strip:], out_weight, 1, 1)
    empty = jnp.zeros((SPAN, width), F32)

    lane = lax.broadcasted_iota(jnp.int32, (1, width), 1) // HEAD_DIM
    zero = jnp.zeros((), BF16)

    def spread(cells, valid):
        cells = jnp.where(valid, cells, 0.0).astype(BF16)
        return jnp.concatenate([jnp.where(lane == head, cells, zero) for head in range(HEADS)], axis=0)

    rows_ok = query_rows(band)
    strip_col = lax.broadcasted_iota(jnp.int32, (band, 1), 0) // SPAN
    bands = (
        (spread(west_query, rows_ok & (strip_col > 0)), jnp.concatenate([empty, west_up], axis=0)),
        (spread(queries[:band], rows_ok), own_up[:band]),
        (spread(queries[band:], rows_ok), own_up[band:]),
        (spread(east_query, rows_ok & (strip_col < RADIUS)), jnp.concatenate([east_up, empty], axis=0)),
    )

    deep = (BAND + REACH) * SPAN
    key_at = lax.broadcasted_iota(jnp.int32, (deep, band), 0)
    query_at = lax.broadcasted_iota(jnp.int32, (deep, band), 1)
    col_gap = key_at // SPAN - query_at // SPAN
    row_gap = (key_at - query_at + RADIUS) & (SPAN - 1)
    inside = (col_gap >= 0) & (col_gap <= REACH) & (row_gap <= REACH)
    bias = jnp.where(inside, 0.0, LOWEST)
    bias = jnp.concatenate([bias] * HEADS, axis=1)
    factor = jnp.concatenate(
        [jnp.full((1, band), scale_ref[head] * (1.0 / HEAD_DIM), F32) for head in range(HEADS)], axis=1
    )

    def merge(stacked):
        half = width // 2
        low = lax.broadcasted_iota(jnp.int32, (1, half), 1) < HEAD_DIM
        parts = [stacked[head * band : (head + 1) * band] for head in range(HEADS)]
        return jnp.concatenate(
            [
                jnp.where(low, parts[0][:, :half], parts[1][:, :half]),
                jnp.where(low, parts[2][:, half:], parts[3][:, half:]),
            ],
            axis=1,
        )

    key_grad_ref[...] = jnp.zeros_like(key_grad_ref)
    value_grad_ref[...] = jnp.zeros_like(value_grad_ref)
    attended = []
    query_grads = []
    own_end = strip + own_count
    for index, (query_big, upstream) in enumerate(bands):
        up_big = spread(upstream, rows_ok)
        first = (2 + BAND * index - RADIUS) * SPAN
        last = first + deep
        lower, upper = max(first, 0), min(last, own_end + strip)
        key_band = key_ref[lower:upper]
        value_band = value_ref[lower:upper]
        scores = dot(key_band, query_big, 1, 1) * factor + bias[lower - first : upper - first]
        exponent = jnp.exp(scores - jnp.max(scores, axis=0, keepdims=True))
        prob = exponent * (1.0 / jnp.sum(exponent, axis=0, keepdims=True))
        dots = dot(value_band, up_big, 1, 1)
        mean_dot = jnp.sum(prob * dots, axis=0, keepdims=True)
        weighted = (prob * (dots - mean_dot) * factor).astype(BF16)
        prob = prob.astype(BF16)
        near, far = max(lower, strip), min(upper, own_end)
        key_grad_ref[near - strip : far - strip] += dot(weighted[near - lower : far - lower], query_big)
        value_grad_ref[near - strip : far - strip] += dot(prob[near - lower : far - lower], up_big)
        if index in (1, 2):
            attended.append(merge(dot(prob, value_band, 0, 0)))
            query_grads.append(merge(dot(weighted, key_band, 0, 0)))

    row = row_in(own_count)
    own_rows = row < 16
    key_rows = own_rows | (top & (row >= SPAN - RADIUS)) | (bottom & (row >= 16) & (row < 16 + RADIUS))
    query_grad = jnp.concatenate(query_grads, axis=0)
    raw_query = head_back(query_grad, queries, query_recip, group)
    raw_key = head_back(key_grad_ref[...], keys, key_recip, group)
    projected_grad = jnp.concatenate(
        [
            jnp.where(own_rows, raw_query, 0.0),
            jnp.where(key_rows, raw_key, 0.0),
            jnp.where(key_rows, value_grad_ref[...], 0.0),
        ],
        axis=1,
    ).astype(BF16)
    normed_grad = dot(projected_grad, weight, 1, 1)
    gain_grad_ref[...] = jnp.sum(normed_grad * unit, axis=0, keepdims=True)
    scaled = normed_grad * gain
    token_part = reciprocal * (scaled - unit * jnp.mean(scaled * unit, axis=-1, keepdims=True))
    token_ref[...] = (own_grad.astype(F32) + token_part).astype(BF16)
    qkv_grad_ref[...] = dot(projected_grad, normed, 0, 0).astype(BF16)
    attended = jnp.where(own_rows, jnp.concatenate(attended, axis=0), 0.0).astype(BF16)
    proj_grad_ref[...] = dot(own_grad, attended, 0, 0).astype(BF16)


def exchange(axis, count, closed, to_next, to_back):
    ends = count if closed else count - 1
    from_back = lax.ppermute(to_next, axis, [(i, (i + 1) % count) for i in range(ends)])
    from_next = lax.ppermute(to_back, axis, [((i + 1) % count, i) for i in range(ends)])
    return from_back, from_next


def on_device(tokens, edge_tokens, output_grad, norm_gain, qkv_weight, out_weight, head_scale):
    row_count, col_count, width = tokens.shape
    row_devices = lax.axis_size("rows")
    col_devices = lax.axis_size("cols")
    place = lax.axis_index("rows")
    grad_scale = (row_count * row_devices * col_count * col_devices) ** (-0.5)
    own = tokens.transpose(1, 0, 2)
    grad = output_grad.transpose(1, 0, 2)
    edges = edge_tokens.transpose(2, 0, 1, 3)
    above, below = exchange(
        "rows",
        row_devices,
        False,
        jnp.concatenate([own[:, row_count - REACH :], grad[:, row_count - RADIUS :]], axis=1),
        jnp.concatenate([own[:, :REACH], grad[:, :RADIUS]], axis=1),
    )
    blank = jnp.zeros((col_count, RADIUS, width), BF16)
    upper = jnp.where(place == 0, jnp.concatenate([blank, edges[:, 0]], axis=1), above[:, :REACH])
    lower = jnp.where(
        place == row_devices - 1, jnp.concatenate([edges[:, 1], blank], axis=1), below[:, :REACH]
    )
    gap = jnp.zeros((col_count, SPAN - row_count - 2 * REACH, width), BF16)
    slab = jnp.concatenate([own, lower, gap, upper], axis=1)
    grad_gap = jnp.zeros((col_count, SPAN - row_count - 2 * RADIUS, width), BF16)
    grad_slab = jnp.concatenate([grad, below[:, REACH:], grad_gap, above[:, REACH:]], axis=1)
    west, east = exchange(
        "cols",
        col_devices,
        True,
        jnp.concatenate([slab[col_count - REACH :], grad_slab[col_count - RADIUS :]], axis=0),
        jnp.concatenate([slab[:REACH], grad_slab[:RADIUS]], axis=0),
    )
    cells = col_count * SPAN
    whole = pl.BlockSpec(memory_space=pltpu.VMEM)
    scalars = pl.BlockSpec(memory_space=pltpu.SMEM)
    token_grad, qkv_grad, proj_grad, gain_grad = pl.pallas_call(
        block_kernel,
        out_shape=(
            jax.ShapeDtypeStruct((cells, width), BF16),
            jax.ShapeDtypeStruct((3 * width, width), BF16),
            jax.ShapeDtypeStruct((width, width), BF16),
            jax.ShapeDtypeStruct((1, width), F32),
        ),
        in_specs=[scalars, scalars] + [whole] * 7,
        out_specs=(whole,) * 4,
        scratch_shapes=[
            pltpu.VMEM((cells + 2 * REACH * SPAN, width), BF16),
            pltpu.VMEM((cells + 2 * REACH * SPAN, width), BF16),
            pltpu.VMEM((cells, width), F32),
            pltpu.VMEM((cells, width), F32),
        ],
        compiler_params=pltpu.CompilerParams(vmem_limit_bytes=40 * 2**20),
    )(
        jnp.stack([place, row_devices]).astype(jnp.int32),
        head_scale,
        slab.reshape(cells, width),
        grad_slab.reshape(cells, width),
        west.reshape(-1, width),
        east.reshape(-1, width),
        norm_gain[None, :],
        qkv_weight,
        out_weight,
    )
    token_grad = token_grad.reshape(col_count, SPAN, width)[:, :row_count].transpose(1, 0, 2)
    share = width // col_devices
    chunks = jnp.concatenate(
        [
            qkv_grad.reshape(col_devices, 3 * share, width),
            proj_grad.reshape(col_devices, share, width),
        ],
        axis=1,
    )
    gains = jnp.pad(
        gain_grad.astype(BF16).reshape(col_devices, 1, share),
        ((0, 0), (0, 4 * share - 1), (0, 128 - share)),
    )
    chunks = jnp.concatenate([chunks, gains], axis=2)
    chunks = lax.all_to_all(chunks, "cols", 0, 0)
    part = jnp.sum(chunks.astype(F32), axis=0)
    part = jnp.sum(lax.all_gather(part, "rows", axis=0), axis=0) * grad_scale
    return (
        token_grad,
        part[: 3 * share, :width].T,
        part[3 * share :, :width].T,
        part[0, width : width + share],
    )


def solution(mesh):
    return jax.shard_map(
        on_device,
        mesh=mesh,
        in_specs=(
            P("rows", "cols", None),
            P(None, None, "cols", None),
            P("rows", "cols", None),
            P(),
            P(),
            P(),
            P(),
        ),
        out_specs=(P("rows", "cols", None), P(None, "cols"), P(None, "cols"), P("cols")),
        check_vma=False,
    )
```

time: 491 us -> 91.7 us (0.19)
  waiting for transfers between devices: 285 us -> 31.8 us
  blocking collectives: 93.2 us -> 7.98 us
  matrix products: 25.2 us -> 0 us
  local copies, waits for them, and re-layouts: 19.5 us -> 5.39 us
  between operations: 14.9 us -> 0.88 us
  starting transfers between devices: 43.5 us -> 37.4 us
  other arithmetic: 8.16 us -> 2.75 us
  Pallas kernels: 0 us -> 4.92 us
    psum x1 -> x0, waiting for transfers between devices: 268 us -> none  [on_device(): lax.psum((qkv_sum, proj_sum, gain_row), ('cols', 'rows'))]
    psum x1 -> x0, blocking collectives: 93.2 us -> none  [on_device(): lax.psum((qkv_sum, proj_sum, gain_row), ('cols', 'rows'))]
    dot_general x32 -> x0, matrix products: 25.2 us -> none  [the longest x4 6.53 us: attend(): key_heads.append(jnp.dot(weighted.T, query_h, precision=PRECISE))]
    all_to_all x0 -> x1, waiting for transfers between devices: none -> 22.3 us  [on_device(): chunks = lax.all_to_all(chunks, 'cols', 0, 0)]
    ppermute x8 -> x4, starting transfers between devices: 43.5 us -> 26 us  [the longest x2 15.2 us: exchange(): lax.ppermute(to_next, axis, [(i, (i + 1) % count) for i in range(ends)])]
    all_to_all x0 -> x1, starting transfers between devices: none -> 11.4 us  [on_device(): chunks = lax.all_to_all(chunks, 'cols', 0, 0)]
    all_gather x0 -> x1, blocking collectives: none -> 7.98 us  [on_device(): part = jnp.sum(lax.all_gather(part, 'rows', axis=0), axis=0) * grad_scale]
    ppermute x8 -> x4, waiting for transfers between devices: 17.1 us -> 9.5 us  [the longest x2 8.09 us: exchange(): lax.ppermute(to_back, axis, [((i + 1) % count, i) for i in range(ends)])]
  transfers between devices with their start and end apart: 9 -> 5, of which waited for: 3 -> 4; matrix products, arithmetic and copies ran while one was open for 2% -> 2% of each run, Pallas kernels for 0% -> 0%
where the time goes in v1:
time: 91.7 us; the launch traced here: 91.1 us
  starting transfers between devices  37.4 us (41%)
  waiting for transfers between devices  31.8 us (35%)
  blocking collectives  7.98 us (9%)
  local copies, waits for them, and re-layouts  5.39 us (6%)
  Pallas kernels  4.92 us (5%)
  other arithmetic  2.75 us (3%)
    all_to_all x1, waiting for transfers between devices, on_device(): chunks = lax.all_to_all(chunks, 'cols', 0, 0)  22.3 us
    ppermute x2, starting transfers between devices, exchange(): lax.ppermute(to_next, axis, [(i, (i + 1) % count) for i in range(ends)])  15.2 us
    all_to_all x1, starting transfers between devices, on_device(): chunks = lax.all_to_all(chunks, 'cols', 0, 0)  11.4 us
    ppermute x2, starting transfers between devices, exchange(): lax.ppermute(to_back, axis, [((i + 1) % count, i) for i in range(ends)])  10.8 us
    ppermute x2, waiting for transfers between devices, exchange(): lax.ppermute(to_back, axis, [((i + 1) % count, i) for i in range(ends)])  8.09 us
    all_gather x1, blocking collectives, on_device(): part = jnp.sum(lax.all_gather(part, 'rows', axis=0), axis=0) * grad_scale  7.98 us
    pallas_call x1, Pallas kernels, on_device(): pl.pallas_call(block_kernel, out_shape=(jax.ShapeDtypeStruct((cells, widt...  4.92 us
  transfers between devices with their start and end apart: 5, of which 4 were waited for; matrix products, arithmetic and copies ran while one was open for 2% of the time, Pallas kernels for 0%

profile of v1, /device:TPU:1, one launch (start us, length us, event | category | flops | bytes accessed | tf_op | source)
XLA Modules:
  0.0 91.1 jit_solution(17612689261374315236)
XLA Ops:
  0.6 0.8 fusion.5
  1.4 0.8 fusion.4
  2.2 12.0 %collective-permute-start.1 = (bf16[8,9,256]{2,0,1:T(8,128)(2,1)S(1)}, bf16[8,9,256]{2,0,1:T(8,128)(2,1)S(1)}, u32[]{:S(2)}, u32[]{:S(2)}) collective-permute-start(bf16[8,9,256]{2,0,1:T(8,128)(2,1)S(1)} %pad_maximum_fusion.5), channel_id=1, source_target_pairs={{0,1},{1,2},{2,3},{4,5},{5,6},{6,7},{8,9},{9,10},{10,11},{12,13},{... | collective-permute-start | bytes 110600 | tf_op jit(solution)/shard_map/ppermute | solution.py:192
  14.2 1.9 %collective-permute-start = (bf16[8,9,256]{2,0,1:T(8,128)(2,1)S(1)}, bf16[8,9,256]{2,0,1:T(8,128)(2,1)S(1)}, u32[]{:S(2)}, u32[]{:S(2)}) collective-permute-start(bf16[8,9,256]{2,0,1:T(8,128)(2,1)S(1)} %pad_maximum_fusion.4), channel_id=1, source_target_pairs={{1,0},{2,1},{3,2},{5,4},{6,5},{7,6},{9,8},{10,9},{11,10},{13,12},{... | collective-permute-start | bytes 110600 | tf_op jit(solution)/shard_map/ppermute | solution.py:193
  16.1 0.7 slice_bitcast_fusion.1
  16.9 0.1 pad.20.clone
  17.0 0.1 pad.16.clone
  17.0 6.4 %collective-permute-done = bf16[8,9,256]{2,0,1:T(8,128)(2,1)S(1)} collective-permute-done((bf16[8,9,256]{2,0,1:T(8,128)(2,1)S(1)}, bf16[8,9,256]{2,0,1:T(8,128)(2,1)S(1)}, u32[]{:S(2)}, u32[]{:S(2)}) %collective-permute-start) | collective-permute-done | bytes 36896 | tf_op jit(solution)/shard_map/ppermute | solution.py:193
  23.4 0.9 %pad_maximum_fusion.3 = bf16[8,32,256]{2,0,1:T(8,128)(2,1)S(1)} fusion(bf16[8,3,256]{2,0,1:T(8,128)(2,1)S(1)} %slice.81, bf16[8,3,256]{2,0,1:T(8,128)(2,1)S(1)} %slice.80, bf16[8,16,256]{2,0,1:T(8,128)(2,1)} %bitcast.34, bf16[32]{0:T(256)(128)(2,1)S(1)} %pad.16.clone), kind=kLoop, calls=%fused_computation.7 | loop fusion | flops 196608 | bytes 221248 | tf_op jit(solution)/shard_map/concatenate | solution.py:221
  24.5 0.1 pad_maximum_fusion.2
  24.6 0.1 pad_maximum_fusion
  24.7 3.2 %collective-permute-start.2 = (bf16[9,32,256]{2,0,1:T(8,128)(2,1)S(1)}, bf16[9,32,256]{2,0,1:T(8,128)(2,1)S(1)}, u32[]{:S(2)}, u32[]{:S(2)}) collective-permute-start(bf16[9,32,256]{2,0,1:T(8,128)(2,1)S(1)} %pad_maximum_fusion), channel_id=1, source_target_pairs={{0,4},{4,8},{8,12},{12,16},{16,20},{20,24},{24,28},{28,32},{32,36}... | collective-permute-start | bytes 442376 | tf_op jit(solution)/shard_map/ppermute | solution.py:192
  27.9 0.1 pad_maximum_fusion.1
  28.1 8.8 %collective-permute-start.3 = (bf16[9,32,256]{2,0,1:T(8,128)(2,1)S(1)}, bf16[9,32,256]{2,0,1:T(8,128)(2,1)S(1)}, u32[]{:S(2)}, u32[]{:S(2)}) collective-permute-start(bf16[9,32,256]{2,0,1:T(8,128)(2,1)S(1)} %pad_maximum_fusion.1), channel_id=1, source_target_pairs={{4,0},{8,4},{12,8},{16,12},{20,16},{24,20},{28,24},{32,28},{36,32}... | collective-permute-start | bytes 442376 | tf_op jit(solution)/shard_map/ppermute | solution.py:193
  36.9 0.1 pad_add_fusion.place_ref
  37.1 1.4 %collective-permute-done.2 = bf16[9,32,256]{2,0,1:T(8,128)(2,1)S(1)} collective-permute-done((bf16[9,32,256]{2,0,1:T(8,128)(2,1)S(1)}, bf16[9,32,256]{2,0,1:T(8,128)(2,1)S(1)}, u32[]{:S(2)}, u32[]{:S(2)}) %collective-permute-start.2) | collective-permute-done | bytes 147488 | tf_op jit(solution)/shard_map/ppermute | solution.py:192
  38.5 0.1 copy.25
  38.5 1.7 %collective-permute-done.3 = bf16[9,32,256]{2,0,1:T(8,128)(2,1)S(1)} collective-permute-done((bf16[9,32,256]{2,0,1:T(8,128)(2,1)S(1)}, bf16[9,32,256]{2,0,1:T(8,128)(2,1)S(1)}, u32[]{:S(2)}, u32[]{:S(2)}) %collective-permute-start.3) | collective-permute-done | bytes 147488 | tf_op jit(solution)/shard_map/ppermute | solution.py:193
  40.2 0.1 copy.26
  40.3 4.9 %shard_map.102 = (bf16[256,256]{1,0:T(8,128)(2,1)S(1)}, bf16[768,256]{1,0:T(8,128)(2,1)S(1)}, bf16[256,256]{1,0:T(8,128)(2,1)S(1)}, f32[1,256]{1,0:T(1,128)S(1)}) custom-call(s32[2]{0:T(128)S(1)} %pad_add_fusion.place_ref, f32[4]{0:T(128)S(1)} %copy-done.3, bf16[256,256]{1,0:T(8,128)(2,1)S(1)} %bitcast.28, bf16[256,256]{1,0:T(8,128)(2,1)S(1)} %bitcast.27, ...), custom_call_target="tpu_custom_call" | custom-call | tf_op jit(solution)/shard_map/pallas_call | solution.py:232
  45.3 0.2 reshape.41
  45.4 0.1 reshape.38
  45.5 0.1 reshape.37
  45.6 1.2 %fusion.1 = bf16[128,8,384]{2,1,0:T(8,128)(2,1)} fusion(bf16[128,1,2]{2,1,0:T(2,128)(2,1)S(1)} %reshape.41, bf16[128,2,256]{2,1,0:T(2,128)(2,1)S(1)} %reshape.38, bf16[128,6,256]{2,1,0:T(8,128)(2,1)S(1)} %reshape.37), kind=kLoop, calls=%fused_computation.3 | loop fusion | flops 3145728 | bytes 1311232 | tf_op jit(solution)/shard_map/concatenate | solution.py:273
  46.9 11.4 %all-to-all-start = ((bf16[128,8,384]{2,1,0:T(8,128)(2,1)}), bf16[128,8,384]{2,1,0:T(8,128)(2,1)S(1)}, u32[]{:S(2)}, u32[]{:S(2)}) async-start(bf16[128,8,384]{2,1,0:T(8,128)(2,1)} %fusion.1), calls=%async_computation | async-start | bytes 1572864 | tf_op jit(solution)/shard_map/all_to_all | solution.py:274
  58.3 0.7 copy.31
  59.0 22.3 %all-to-all-done = bf16[128,8,384]{2,1,0:T(8,128)(2,1)S(1)} async-done(((bf16[128,8,384]{2,1,0:T(8,128)(2,1)}), bf16[128,8,384]{2,1,0:T(8,128)(2,1)S(1)}, u32[]{:S(2)}, u32[]{:S(2)}) %all-to-all-start) | async-done | bytes 786464 | tf_op jit(solution)/shard_map/all_to_all | solution.py:274
  81.3 0.2 convert_reduce_fusion
  81.5 8.0 %all-gather = f32[32,384]{1,0:T(8,128)S(1)} all-gather(f32[8,384]{1,0:T(8,128)S(1)} %convert_reduce_fusion), channel_id=2, replica_groups=mesh['cols'=128,'rows'=4] {'rows'}, dimensions={0}, use_global_device_ids=true | all-gather | bytes 61440 | tf_op jit(solution)/shard_map/all_gather | solution.py:276
  89.4 0.5 slice_bitcast_fusion.4
  90.0 0.6 slice_bitcast_fusion.3
  90.5 0.6 slice_bitcast_fusion.2
  (27 shorter events, 0.3 us)
Async XLA Ops:
  0.6 23.8 %copy-start.4 = (bf16[16,8,256]{2,1,0:T(8,128)(2,1)S(1)}, bf16[16,8,256]{2,1,0:T(8,128)(2,1)}, u32[]{:S(2)}) copy-start(bf16[16,8,256]{2,1,0:T(8,128)(2,1)} %param.7) | copy-start | bytes 196612
  2.2 14.9 %collective-permute-start.1 = (bf16[8,9,256]{2,0,1:T(8,128)(2,1)S(1)}, bf16[8,9,256]{2,0,1:T(8,128)(2,1)S(1)}, u32[]{:S(2)}, u32[]{:S(2)}) collective-permute-start(bf16[8,9,256]{2,0,1:T(8,128)(2,1)S(1)} %pad_maximum_fusion.5), channel_id=1, source_target_pairs={{0,1},{1,2},{2,3},{4,5},{5,6},{6,7},{8,9},{9,10},{10,11},{12,13},{... | collective-permute-start | bytes 110600 | tf_op jit(solution)/shard_map/ppermute | solution.py:192
  14.2 9.2 %collective-permute-start = (bf16[8,9,256]{2,0,1:T(8,128)(2,1)S(1)}, bf16[8,9,256]{2,0,1:T(8,128)(2,1)S(1)}, u32[]{:S(2)}, u32[]{:S(2)}) collective-permute-start(bf16[8,9,256]{2,0,1:T(8,128)(2,1)S(1)} %pad_maximum_fusion.4), channel_id=1, source_target_pairs={{1,0},{2,1},{3,2},{5,4},{6,5},{7,6},{9,8},{10,9},{11,10},{13,12},{... | collective-permute-start | bytes 110600 | tf_op jit(solution)/shard_map/ppermute | solution.py:193
  24.7 13.7 %collective-permute-start.2 = (bf16[9,32,256]{2,0,1:T(8,128)(2,1)S(1)}, bf16[9,32,256]{2,0,1:T(8,128)(2,1)S(1)}, u32[]{:S(2)}, u32[]{:S(2)}) collective-permute-start(bf16[9,32,256]{2,0,1:T(8,128)(2,1)S(1)} %pad_maximum_fusion), channel_id=1, source_target_pairs={{0,4},{4,8},{8,12},{12,16},{16,20},{20,24},{24,28},{28,32},{32,36}... | collective-permute-start | bytes 442376 | tf_op jit(solution)/shard_map/ppermute | solution.py:192
  28.0 12.2 %copy-start = (bf16[256,768]{1,0:T(8,128)(2,1)S(1)}, bf16[256,768]{1,0:T(8,128)(2,1)}, u32[]{:S(2)}) copy-start(bf16[256,768]{1,0:T(8,128)(2,1)} %qkv_ref.1) | copy-start | bytes 1179652
  28.1 12.2 %copy-start.1 = (bf16[256,256]{1,0:T(8,128)(2,1)S(1)}, bf16[256,256]{1,0:T(8,128)(2,1)}, u32[]{:S(2)}) copy-start(bf16[256,256]{1,0:T(8,128)(2,1)} %out_ref.1) | copy-start | bytes 393220
  28.1 12.2 %copy-start.2 = (f32[256]{0:T(256)S(1)}, f32[256]{0:T(256)}, u32[]{:S(2)}) copy-start(f32[256]{0:T(256)} %param.10) | copy-start | bytes 3076
  28.1 12.2 %copy-start.3 = (f32[4]{0:T(128)S(1)}, f32[4]{0:T(128)}, u32[]{:S(2)}) copy-start(f32[4]{0:T(128)} %scale_ref.1) | copy-start | bytes 52
  28.1 12.1 %collective-permute-start.3 = (bf16[9,32,256]{2,0,1:T(8,128)(2,1)S(1)}, bf16[9,32,256]{2,0,1:T(8,128)(2,1)S(1)}, u32[]{:S(2)}, u32[]{:S(2)}) collective-permute-start(bf16[9,32,256]{2,0,1:T(8,128)(2,1)S(1)} %pad_maximum_fusion.1), channel_id=1, source_target_pairs={{4,0},{8,4},{12,8},{16,12},{20,16},{24,20},{28,24},{32,28},{36,32}... | collective-permute-start | bytes 442376 | tf_op jit(solution)/shard_map/ppermute | solution.py:193
  46.9 34.4 %all-to-all-start = ((bf16[128,8,384]{2,1,0:T(8,128)(2,1)}), bf16[128,8,384]{2,1,0:T(8,128)(2,1)S(1)}, u32[]{:S(2)}, u32[]{:S(2)}) async-start(bf16[128,8,384]{2,1,0:T(8,128)(2,1)} %fusion.1), calls=%async_computation | async-start | bytes 1572864 | tf_op jit(solution)/shard_map/all_to_all | solution.py:274

commit v2 on v1

--- a/solution.py
+++ b/solution.py
@@ -1,5 +1,7 @@
 import jax
 import jax.numpy as jnp
+import ml_dtypes
+import numpy as np
 from jax import lax
 from jax.experimental import pallas as pl
 from jax.experimental.pallas import tpu as pltpu
@@ -13,6 +15,7 @@
 SPAN = 32
 REACH = 2 * RADIUS
 BAND = 4
+LANES = 128
 LOWEST = -1e30
 F32 = jnp.float32
 BF16 = jnp.bfloat16
@@ -46,8 +49,8 @@
 
 
 def block_kernel(
-    place_ref, scale_ref, own_ref, own_grad_ref, west_ref, east_ref, gain_ref, qkv_ref, out_ref,
-    token_ref, qkv_grad_ref, proj_grad_ref, gain_grad_ref,
+    place_ref, scale_ref, own_ref, own_grad_ref, west_ref, east_ref, gain_ref, qkv_ref, out_ref, pick_ref,
+    token_ref, keep_ref, send_ref,
     key_ref, value_ref, key_grad_ref, value_grad_ref,
 ):
     width = own_ref.shape[1]
@@ -178,13 +181,37 @@
         axis=1,
     ).astype(BF16)
     normed_grad = dot(projected_grad, weight, 1, 1)
-    gain_grad_ref[...] = jnp.sum(normed_grad * unit, axis=0, keepdims=True)
+    gain_grad = jnp.sum(normed_grad * unit, axis=0, keepdims=True)
     scaled = normed_grad * gain
     token_part = reciprocal * (scaled - unit * jnp.mean(scaled * unit, axis=-1, keepdims=True))
     token_ref[...] = (own_grad.astype(F32) + token_part).astype(BF16)
-    qkv_grad_ref[...] = dot(projected_grad, normed, 0, 0).astype(BF16)
     attended = jnp.where(own_rows, jnp.concatenate(attended, axis=0), 0.0).astype(BF16)
-    proj_grad_ref[...] = dot(own_grad, attended, 0, 0).astype(BF16)
+    factors = jnp.concatenate([normed, attended], axis=0)
+    gain_rows = jnp.broadcast_to(gain_grad, (LANES, width)).astype(BF16)
+    for half, half_ref in enumerate((keep_ref, send_ref)):
+        pick = pick_ref[(place_ref[0] + half) % 2]
+        columns = jnp.concatenate(
+            [
+                dot(projected_grad, pick[: 3 * width]).astype(BF16),
+                dot(own_grad, pick[3 * width : 4 * width]).astype(BF16),
+            ],
+            axis=0,
+        )
+        half_ref[:, :width] = dot(columns, factors, 0, 0).astype(BF16)
+        half_ref[:, width:] = dot(pick[4 * width :], gain_rows, 0, 1).astype(BF16)
+
+
+def picks(width, col_devices):
+    share = width // col_devices
+    part = share // 2
+    rows = 4 * part
+    half, source, target = np.ogrid[:2, : 5 * width, : col_devices * rows]
+    chunk, row = target // rows, target % rows
+    weight = chunk * 3 * share + half * 3 * part + row
+    output = 3 * width + chunk * share + half * part + row - 3 * part
+    gain = 4 * width + chunk * share + half * part + row
+    chosen = (source == np.where(row < 3 * part, weight, output)) | ((source == gain) & (row < part))
+    return chosen.astype(ml_dtypes.bfloat16)
 
 
 def exchange(axis, count, closed, to_next, to_back):
@@ -229,16 +256,15 @@
     cells = col_count * SPAN
     whole = pl.BlockSpec(memory_space=pltpu.VMEM)
     scalars = pl.BlockSpec(memory_space=pltpu.SMEM)
-    token_grad, qkv_grad, proj_grad, gain_grad = pl.pallas_call(
+    token_grad, keep, send = pl.pallas_call(
         block_kernel,
         out_shape=(
             jax.ShapeDtypeStruct((cells, width), BF16),
-            jax.ShapeDtypeStruct((3 * width, width), BF16),
-            jax.ShapeDtypeStruct((width, width), BF16),
-            jax.ShapeDtypeStruct((1, width), F32),
+            jax.ShapeDtypeStruct((2 * width, width + LANES), BF16),
+            jax.ShapeDtypeStruct((2 * width, width + LANES), BF16),
         ),
-        in_specs=[scalars, scalars] + [whole] * 7,
-        out_specs=(whole,) * 4,
+        in_specs=[scalars, scalars] + [whole] * 8,
+        out_specs=(whole,) * 3,
         scratch_shapes=[
             pltpu.VMEM((cells + 2 * REACH * SPAN, width), BF16),
             pltpu.VMEM((cells + 2 * REACH * SPAN, width), BF16),
@@ -256,29 +282,24 @@
         norm_gain[None, :],
         qkv_weight,
         out_weight,
+        picks(width, col_devices),
     )
     token_grad = token_grad.reshape(col_count, SPAN, width)[:, :row_count].transpose(1, 0, 2)
+    received = lax.ppermute(send, "rows", [(i, i ^ 1) for i in range(row_devices)])
+    chunks = (keep.astype(F32) + received.astype(F32)).astype(BF16)
     share = width // col_devices
-    chunks = jnp.concatenate(
-        [
-            qkv_grad.reshape(col_devices, 3 * share, width),
-            proj_grad.reshape(col_devices, share, width),
-        ],
-        axis=1,
-    )
-    gains = jnp.pad(
-        gain_grad.astype(BF16).reshape(col_devices, 1, share),
-        ((0, 0), (0, 4 * share - 1), (0, 128 - share)),
-    )
-    chunks = jnp.concatenate([chunks, gains], axis=2)
-    chunks = lax.all_to_all(chunks, "cols", 0, 0)
-    part = jnp.sum(chunks.astype(F32), axis=0)
-    part = jnp.sum(lax.all_gather(part, "rows", axis=0), axis=0) * grad_scale
+    part = share // 2
+    chunks = lax.all_to_all(chunks.reshape(col_devices, 4 * part, width + LANES), "cols", 0, 0)
+    blocks = jnp.sum(chunks.astype(F32), axis=0).reshape(4 * part, -1, LANES).transpose(1, 0, 2)
+    blocks = jnp.pad(blocks.reshape(-1, LANES), ((0, 4 * part), (0, 0)))
+    blocks = lax.all_gather(blocks, "rows", axis=0, tiled=True)
+    blocks = blocks.reshape(2, 2, -1, 4 * part, LANES)[:, :, :-1]
+    halves = (blocks[0] + blocks[1]).transpose(0, 2, 1, 3).reshape(2, 4 * part, -1) * grad_scale
     return (
         token_grad,
-        part[: 3 * share, :width].T,
-        part[3 * share :, :width].T,
-        part[0, width : width + share],
+        halves[:, : 3 * part, :width].reshape(3 * share, width).T,
+        halves[:, 3 * part :, :width].reshape(share, width).T,
+        halves[:, :part, width].reshape(share),
     )
 
 

time: 91.7 us -> 94.1 us (1.026)
  waiting for transfers between devices: 31.8 us -> 28 us
  blocking collectives: 7.98 us -> 10.8 us
  starting transfers between devices: 37.4 us -> 39.2 us
  Pallas kernels: 4.92 us -> 5.97 us
    all_to_all x1, waiting for transfers between devices: 22.3 us -> 16.8 us  [on_device(): lax.all_to_all(chunks.reshape(col_devices, 4 * part, width + LANES), 'col...]
    all_gather x1, blocking collectives: 7.98 us -> 10.8 us  [on_device(): blocks = lax.all_gather(blocks, 'rows', axis=0, tiled=True)]
    ppermute x0 -> x1, starting transfers between devices: none -> 1.92 us  [on_device(): lax.ppermute(send, 'rows', [(i, i ^ 1) for i in range(row_devices)])]
    ppermute x0 -> x1, waiting for transfers between devices: none -> 1.69 us  [on_device(): lax.ppermute(send, 'rows', [(i, i ^ 1) for i in range(row_devices)])]
    concatenate x1 -> x0, other arithmetic: 1.23 us -> none  [on_device(): chunks = jnp.concatenate([chunks, gains], axis=2)]
    transpose x2 -> x0, local copies, waits for them, and re-layouts: 1.18 us -> none  [the longest x1 0.6 us: on_device(): part[:3 * share, :width]]
    reshape x3, local copies, waits for them, and re-layouts: 0.36 us -> 1.46 us  [the longest x1 0.84 us: on_device(): chunks.reshape(col_devices, 4 * part, width + LANES)]
    pallas_call x1, Pallas kernels: 4.92 us -> 5.97 us  [on_device(): pl.pallas_call(block_kernel, out_shape=(jax.ShapeDtypeStruct((cells, widt...]
  transfers between devices with their start and end apart: 5 -> 6, of which waited for: 4 -> 5; matrix products, arithmetic and copies ran while one was open for 2% -> 2% of each run, Pallas kernels for 0% -> 0%
where the time goes in v2:
time: 94.1 us; the launch traced here: 93.6 us
  starting transfers between devices  39.2 us (42%)
  waiting for transfers between devices  28 us (30%)
  blocking collectives  10.8 us (11%)
  local copies, waits for them, and re-layouts  6.2 us (7%)
  Pallas kernels  5.97 us (6%)
  other arithmetic  2.5 us (3%)
    all_to_all x1, waiting for transfers between devices, on_device(): lax.all_to_all(chunks.reshape(col_devices, 4 * part, width + LANES), 'col...  16.8 us
    ppermute x2, starting transfers between devices, exchange(): lax.ppermute(to_next, axis, [(i, (i + 1) % count) for i in range(ends)])  15.2 us
    all_to_all x1, starting transfers between devices, on_device(): lax.all_to_all(chunks.reshape(col_devices, 4 * part, width + LANES), 'col...  11.4 us
    all_gather x1, blocking collectives, on_device(): blocks = lax.all_gather(blocks, 'rows', axis=0, tiled=True)  10.8 us
    ppermute x2, starting transfers between devices, exchange(): lax.ppermute(to_back, axis, [((i + 1) % count, i) for i in range(ends)])  10.6 us
    ppermute x2, waiting for transfers between devices, exchange(): lax.ppermute(to_back, axis, [((i + 1) % count, i) for i in range(ends)])  7.91 us
    pallas_call x1, Pallas kernels, on_device(): pl.pallas_call(block_kernel, out_shape=(jax.ShapeDtypeStruct((cells, widt...  5.97 us
    ppermute x1, starting transfers between devices, on_device(): lax.ppermute(send, 'rows', [(i, i ^ 1) for i in range(row_devices)])  1.92 us
  transfers between devices with their start and end apart: 6, of which 5 were waited for; matrix products, arithmetic and copies ran while one was open for 2% of the time, Pallas kernels for 0%

profile of v2, /device:TPU:1, one launch (start us, length us, event | category | flops | bytes accessed | tf_op | source)
XLA Modules:
  0.0 93.6 jit_solution(9985353239424248366)
XLA Ops:
  0.7 0.9 fusion.5
  1.6 0.8 fusion.4
  2.4 12.0 %collective-permute-start.1 = (bf16[8,9,256]{2,0,1:T(8,128)(2,1)S(1)}, bf16[8,9,256]{2,0,1:T(8,128)(2,1)S(1)}, u32[]{:S(2)}, u32[]{:S(2)}) collective-permute-start(bf16[8,9,256]{2,0,1:T(8,128)(2,1)S(1)} %pad_maximum_fusion.5), channel_id=1, source_target_pairs={{0,1},{1,2},{2,3},{4,5},{5,6},{6,7},{8,9},{9,10},{10,11},{12,13},{... | collective-permute-start | bytes 110600 | tf_op jit(solution)/shard_map/ppermute | solution.py:219
  14.5 1.9 %collective-permute-start = (bf16[8,9,256]{2,0,1:T(8,128)(2,1)S(1)}, bf16[8,9,256]{2,0,1:T(8,128)(2,1)S(1)}, u32[]{:S(2)}, u32[]{:S(2)}) collective-permute-start(bf16[8,9,256]{2,0,1:T(8,128)(2,1)S(1)} %pad_maximum_fusion.4), channel_id=1, source_target_pairs={{1,0},{2,1},{3,2},{5,4},{6,5},{7,6},{9,8},{10,9},{11,10},{13,12},{... | collective-permute-start | bytes 110600 | tf_op jit(solution)/shard_map/ppermute | solution.py:220
  16.4 0.7 slice_bitcast_fusion.1
  17.1 0.1 pad.17.clone
  17.2 0.1 pad.13.clone
  17.3 6.4 %collective-permute-done = bf16[8,9,256]{2,0,1:T(8,128)(2,1)S(1)} collective-permute-done((bf16[8,9,256]{2,0,1:T(8,128)(2,1)S(1)}, bf16[8,9,256]{2,0,1:T(8,128)(2,1)S(1)}, u32[]{:S(2)}, u32[]{:S(2)}) %collective-permute-start) | collective-permute-done | bytes 36896 | tf_op jit(solution)/shard_map/ppermute | solution.py:220
  23.7 0.9 pad_maximum_fusion.3
  24.7 0.9 %pad_maximum_fusion.2 = bf16[8,32,256]{2,0,1:T(8,128)(2,1)S(1)} fusion(bf16[8,6,256]{2,0,1:T(8,128)(2,1)S(1)} %slice_select_fusion, bf16[8,6,256]{2,0,1:T(8,128)(2,1)S(1)} %slice_select_fusion.1, bf16[8,16,256]{2,0,1:T(8,128)(2,1)} %bitcast.40, bf16[32]{0:T(256)(128)(2,1)S(1)} %pad.17.clone), kind=kLoop, calls=%fused_computation.4 | loop fusion | flops 196608 | bytes 245824 | tf_op jit(solution)/shard_map/concatenate | solution.py:246
  25.7 0.1 pad_maximum_fusion
  25.8 3.2 %collective-permute-start.2 = (bf16[9,32,256]{2,0,1:T(8,128)(2,1)S(1)}, bf16[9,32,256]{2,0,1:T(8,128)(2,1)S(1)}, u32[]{:S(2)}, u32[]{:S(2)}) collective-permute-start(bf16[9,32,256]{2,0,1:T(8,128)(2,1)S(1)} %pad_maximum_fusion), channel_id=1, source_target_pairs={{0,4},{4,8},{8,12},{12,16},{16,20},{20,24},{24,28},{28,32},{32,36}... | collective-permute-start | bytes 442376 | tf_op jit(solution)/shard_map/ppermute | solution.py:219
  29.0 0.1 pad_maximum_fusion.1
  29.1 8.7 %collective-permute-start.3 = (bf16[9,32,256]{2,0,1:T(8,128)(2,1)S(1)}, bf16[9,32,256]{2,0,1:T(8,128)(2,1)S(1)}, u32[]{:S(2)}, u32[]{:S(2)}) collective-permute-start(bf16[9,32,256]{2,0,1:T(8,128)(2,1)S(1)} %pad_maximum_fusion.1), channel_id=1, source_target_pairs={{4,0},{8,4},{12,8},{16,12},{20,16},{24,20},{28,24},{32,28},{36,32}... | collective-permute-start | bytes 442376 | tf_op jit(solution)/shard_map/ppermute | solution.py:220
  37.8 0.1 pad_add_fusion.place_ref
  38.0 1.6 %collective-permute-done.2 = bf16[9,32,256]{2,0,1:T(8,128)(2,1)S(1)} collective-permute-done((bf16[9,32,256]{2,0,1:T(8,128)(2,1)S(1)}, bf16[9,32,256]{2,0,1:T(8,128)(2,1)S(1)}, u32[]{:S(2)}, u32[]{:S(2)}) %collective-permute-start.2) | collective-permute-done | bytes 147488 | tf_op jit(solution)/shard_map/ppermute | solution.py:219
  39.5 0.1 copy.19
  39.6 1.5 %collective-permute-done.3 = bf16[9,32,256]{2,0,1:T(8,128)(2,1)S(1)} collective-permute-done((bf16[9,32,256]{2,0,1:T(8,128)(2,1)S(1)}, bf16[9,32,256]{2,0,1:T(8,128)(2,1)S(1)}, u32[]{:S(2)}, u32[]{:S(2)}) %collective-permute-start.3) | collective-permute-done | bytes 147488 | tf_op jit(solution)/shard_map/ppermute | solution.py:220
  41.1 0.1 copy.20
  41.2 6.0 %shard_map.111 = (bf16[256,256]{1,0:T(8,128)(2,1)S(1)}, bf16[512,384]{1,0:T(8,128)(2,1)S(1)}, bf16[512,384]{1,0:T(8,128)(2,1)S(1)}) custom-call(s32[2]{0:T(128)S(1)} %pad_add_fusion.place_ref, f32[4]{0:T(128)S(1)} %copy-done.4, bf16[256,256]{1,0:T(8,128)(2,1)S(1)} %bitcast.36, bf16[256,256]{1,0:T(8,128)(2,1)S(1)} %bitcast.35, bf16[288,256]{1,0:T(8,128)(2,1)S(1)} %bitcast.33, ...), custom_call_target="tpu_custom_call" | custom-call | tf_op jit(solution)/shard_map/pallas_call | solution.py:259
  47.2 1.9 %collective-permute-start.4 = (bf16[512,384]{1,0:T(8,128)(2,1)S(1)}, bf16[512,384]{1,0:T(8,128)(2,1)S(1)}, u32[]{:S(2)}, u32[]{:S(2)}) collective-permute-start(bf16[512,384]{1,0:T(8,128)(2,1)S(1)} %get-tuple-element.9), channel_id=1, source_target_pairs={{0,1},{1,0},{2,3},{3,2},{4,5},{5,4},{6,7},{7,6},{8,9},{9,8},{10,11... | collective-permute-start | bytes 1179656 | tf_op jit(solution)/shard_map/ppermute | solution.py:288
  49.1 1.7 %collective-permute-done.4 = bf16[512,384]{1,0:T(8,128)(2,1)S(1)} collective-permute-done((bf16[512,384]{1,0:T(8,128)(2,1)S(1)}, bf16[512,384]{1,0:T(8,128)(2,1)S(1)}, u32[]{:S(2)}, u32[]{:S(2)}) %collective-permute-start.4) | collective-permute-done | bytes 393248 | tf_op jit(solution)/shard_map/ppermute | solution.py:288
  50.8 0.1 add_convert_fusion
  50.9 0.8 reshape.52
  51.8 11.4 %all-to-all-start = ((bf16[128,4,384]{2,1,0:T(4,128)(2,1)}), bf16[128,4,384]{2,1,0:T(4,128)(2,1)S(1)}, u32[]{:S(2)}, u32[]{:S(2)}) async-start(bf16[128,4,384]{2,1,0:T(4,128)(2,1)} %reshape.52), calls=%async_computation | async-start | bytes 786432 | tf_op jit(solution)/shard_map/all_to_all | solution.py:292
  63.2 0.7 copy.26
  63.9 16.8 %all-to-all-done = bf16[128,4,384]{2,1,0:T(4,128)(2,1)S(1)} async-done(((bf16[128,4,384]{2,1,0:T(4,128)(2,1)}), bf16[128,4,384]{2,1,0:T(4,128)(2,1)S(1)}, u32[]{:S(2)}, u32[]{:S(2)}) %all-to-all-start) | async-done | bytes 393248 | tf_op jit(solution)/shard_map/all_to_all | solution.py:292
  80.7 0.2 convert_reduce_fusion
  80.9 10.8 %all_gather.3 = f32[64,128]{1,0:T(8,128)S(1)} all-gather(f32[16,128]{1,0:T(8,128)S(1)} %pad.6), channel_id=1, replica_groups=mesh['cols'=128,'rows'=4] {'rows'}, dimensions={0}, use_global_device_ids=true | all-gather | bytes 40960 | tf_op jit(solution)/shard_map/all_gather | solution.py:295
  91.8 0.6 slice_reduce_fusion
  92.4 0.6 reshape.56
  93.0 0.6 copy.27
  (29 shorter events, 0.2 us)
Async XLA Ops:
  0.6 40.5 %copy-start = (bf16[2,1280,512]{2,1,0:T(8,128)(2,1)S(1)}, bf16[2,1280,512]{2,1,0:T(8,128)(2,1)}, u32[]{:S(2)}) copy-start(bf16[2,1280,512]{2,1,0:T(8,128)(2,1)} %constant.7.clone.pick_ref) | copy-start | bytes 7864324
  0.6 40.5 %copy-start.4 = (f32[4]{0:T(128)S(1)}, f32[4]{0:T(128)}, u32[]{:S(2)}) copy-start(f32[4]{0:T(128)} %scale_ref.1) | copy-start | bytes 52
  0.7 40.5 %copy-start.2 = (bf16[256,256]{1,0:T(8,128)(2,1)S(1)}, bf16[256,256]{1,0:T(8,128)(2,1)}, u32[]{:S(2)}) copy-start(bf16[256,256]{1,0:T(8,128)(2,1)} %out_ref.1) | copy-start | bytes 393220
  0.7 40.5 %copy-start.1 = (bf16[256,768]{1,0:T(8,128)(2,1)S(1)}, bf16[256,768]{1,0:T(8,128)(2,1)}, u32[]{:S(2)}) copy-start(bf16[256,768]{1,0:T(8,128)(2,1)} %qkv_ref.1) | copy-start | bytes 1179652
  0.7 40.5 %copy-start.3 = (f32[256]{0:T(256)S(1)}, f32[256]{0:T(256)}, u32[]{:S(2)}) copy-start(f32[256]{0:T(256)} %param.11) | copy-start | bytes 3076
  2.4 14.9 %collective-permute-start.1 = (bf16[8,9,256]{2,0,1:T(8,128)(2,1)S(1)}, bf16[8,9,256]{2,0,1:T(8,128)(2,1)S(1)}, u32[]{:S(2)}, u32[]{:S(2)}) collective-permute-start(bf16[8,9,256]{2,0,1:T(8,128)(2,1)S(1)} %pad_maximum_fusion.5), channel_id=1, source_target_pairs={{0,1},{1,2},{2,3},{4,5},{5,6},{6,7},{8,9},{9,10},{10,11},{12,13},{... | collective-permute-start | bytes 110600 | tf_op jit(solution)/shard_map/ppermute | solution.py:219
  14.5 9.2 %collective-permute-start = (bf16[8,9,256]{2,0,1:T(8,128)(2,1)S(1)}, bf16[8,9,256]{2,0,1:T(8,128)(2,1)S(1)}, u32[]{:S(2)}, u32[]{:S(2)}) collective-permute-start(bf16[8,9,256]{2,0,1:T(8,128)(2,1)S(1)} %pad_maximum_fusion.4), channel_id=1, source_target_pairs={{1,0},{2,1},{3,2},{5,4},{6,5},{7,6},{9,8},{10,9},{11,10},{13,12},{... | collective-permute-start | bytes 110600 | tf_op jit(solution)/shard_map/ppermute | solution.py:220
  25.8 13.7 %collective-permute-start.2 = (bf16[9,32,256]{2,0,1:T(8,128)(2,1)S(1)}, bf16[9,32,256]{2,0,1:T(8,128)(2,1)S(1)}, u32[]{:S(2)}, u32[]{:S(2)}) collective-permute-start(bf16[9,32,256]{2,0,1:T(8,128)(2,1)S(1)} %pad_maximum_fusion), channel_id=1, source_target_pairs={{0,4},{4,8},{8,12},{12,16},{16,20},{20,24},{24,28},{28,32},{32,36}... | collective-permute-start | bytes 442376 | tf_op jit(solution)/shard_map/ppermute | solution.py:219
  29.1 12.0 %collective-permute-start.3 = (bf16[9,32,256]{2,0,1:T(8,128)(2,1)S(1)}, bf16[9,32,256]{2,0,1:T(8,128)(2,1)S(1)}, u32[]{:S(2)}, u32[]{:S(2)}) collective-permute-start(bf16[9,32,256]{2,0,1:T(8,128)(2,1)S(1)} %pad_maximum_fusion.1), channel_id=1, source_target_pairs={{4,0},{8,4},{12,8},{16,12},{20,16},{24,20},{28,24},{32,28},{36,32}... | collective-permute-start | bytes 442376 | tf_op jit(solution)/shard_map/ppermute | solution.py:220
  47.2 3.6 %collective-permute-start.4 = (bf16[512,384]{1,0:T(8,128)(2,1)S(1)}, bf16[512,384]{1,0:T(8,128)(2,1)S(1)}, u32[]{:S(2)}, u32[]{:S(2)}) collective-permute-start(bf16[512,384]{1,0:T(8,128)(2,1)S(1)} %get-tuple-element.9), channel_id=1, source_target_pairs={{0,1},{1,0},{2,3},{3,2},{4,5},{5,4},{6,7},{7,6},{8,9},{9,8},{10,11... | collective-permute-start | bytes 1179656 | tf_op jit(solution)/shard_map/ppermute | solution.py:288
  51.8 28.9 %all-to-all-start = ((bf16[128,4,384]{2,1,0:T(4,128)(2,1)}), bf16[128,4,384]{2,1,0:T(4,128)(2,1)S(1)}, u32[]{:S(2)}, u32[]{:S(2)}) async-start(bf16[128,4,384]{2,1,0:T(4,128)(2,1)} %reshape.52), calls=%async_computation | async-start | bytes 786432 | tf_op jit(solution)/shard_map/all_to_all | solution.py:292

commit v3 on v1

--- a/solution.py
+++ b/solution.py
@@ -1,3 +1,5 @@
+import functools
+
 import jax
 import jax.numpy as jnp
 from jax import lax
@@ -13,6 +15,7 @@
 SPAN = 32
 REACH = 2 * RADIUS
 BAND = 4
+LANES = 128
 LOWEST = -1e30
 F32 = jnp.float32
 BF16 = jnp.bfloat16
@@ -46,15 +49,19 @@
 
 
 def block_kernel(
-    place_ref, scale_ref, own_ref, own_grad_ref, west_ref, east_ref, gain_ref, qkv_ref, out_ref,
-    token_ref, qkv_grad_ref, proj_grad_ref, gain_grad_ref,
-    key_ref, value_ref, key_grad_ref, value_grad_ref,
+    place_ref, scale_ref, own_ref, own_grad_ref, odd_ref, even_ref, gain_ref, qkv_ref, out_ref,
+    token_ref, chunk_ref,
+    key_ref, value_ref, key_grad_ref, value_grad_ref, weight_grad_ref,
 ):
     width = own_ref.shape[1]
     own_count = own_ref.shape[0]
     strip = REACH * SPAN
     top = place_ref[0] == 0
     bottom = place_ref[0] == place_ref[1] - 1
+    parity = place_ref[2]
+    odd_strip, even_strip = odd_ref[...], even_ref[1 - parity]
+    west = jnp.where(parity == 0, odd_strip, even_strip)
+    east = jnp.where(parity == 0, even_strip, odd_strip)
     gain = gain_ref[...]
     weight = qkv_ref[...]
     lane_head = lax.broadcasted_iota(jnp.int32, (width, width), 0) // HEAD_DIM
@@ -84,8 +91,8 @@
 
     unit, reciprocal, normed, keys, key_recip = keys_of(own_ref[...], strip)
     queries, query_recip = queries_of(normed)
-    west_normed = keys_of(west_ref[:strip], 0)[2]
-    east_normed = keys_of(east_ref[:strip], strip + own_count)[2]
+    west_normed = keys_of(west[:strip], 0)[2]
+    east_normed = keys_of(east[:strip], strip + own_count)[2]
     band = BAND * SPAN
     west_query = queries_of(west_normed[strip - band :])[0]
     east_query = queries_of(east_normed[:band])[0]
@@ -93,8 +100,8 @@
     own_grad = own_grad_ref[...]
     out_weight = out_ref[...]
     own_up = dot(own_grad, out_weight, 1, 1)
-    west_up = dot(west_ref[strip:], out_weight, 1, 1)
-    east_up = dot(east_ref[strip:], out_weight, 1, 1)
+    west_up = dot(west[strip:], out_weight, 1, 1)
+    east_up = dot(east[strip:], out_weight, 1, 1)
     empty = jnp.zeros((SPAN, width), F32)
 
     lane = lax.broadcasted_iota(jnp.int32, (1, width), 1) // HEAD_DIM
@@ -178,20 +185,42 @@
         axis=1,
     ).astype(BF16)
     normed_grad = dot(projected_grad, weight, 1, 1)
-    gain_grad_ref[...] = jnp.sum(normed_grad * unit, axis=0, keepdims=True)
+    gain_grad = jnp.sum(normed_grad * unit, axis=0, keepdims=True)
     scaled = normed_grad * gain
     token_part = reciprocal * (scaled - unit * jnp.mean(scaled * unit, axis=-1, keepdims=True))
     token_ref[...] = (own_grad.astype(F32) + token_part).astype(BF16)
-    qkv_grad_ref[...] = dot(projected_grad, normed, 0, 0).astype(BF16)
+    weight_grad = dot(projected_grad, normed, 0, 0)
+    blocks = range(width // LANES)
+    for block in blocks:
+        weight_grad_ref[block] = weight_grad[:, block * LANES : (block + 1) * LANES]
     attended = jnp.where(own_rows, jnp.concatenate(attended, axis=0), 0.0).astype(BF16)
-    proj_grad_ref[...] = dot(own_grad, attended, 0, 0).astype(BF16)
-
-
-def exchange(axis, count, closed, to_next, to_back):
-    ends = count if closed else count - 1
-    from_back = lax.ppermute(to_next, axis, [(i, (i + 1) % count) for i in range(ends)])
-    from_next = lax.ppermute(to_back, axis, [((i + 1) % count, i) for i in range(ends)])
-    return from_back, from_next
+    for part in range(3):
+        for block in blocks:
+            third = weight_grad_ref.at[block][pl.ds(part, width, stride=3), :]
+            at = part * width + block * LANES
+            chunk_ref[:, at : at + LANES] = third.astype(BF16)
+    chunk_ref[:, 3 * width : 4 * width] = dot(own_grad, attended, 0, 0).astype(BF16)
+    chunk_ref[:, 4 * width :] = jnp.broadcast_to(gain_grad, (LANES, width)).T.astype(BF16)
+
+
+def final_kernel(scale, parts_ref, qkv_ref, proj_ref, gain_ref):
+    share, width = proj_ref.shape
+    rows = parts_ref.shape[0] // 4
+    total = sum(parts_ref[part * rows : (part + 1) * rows] for part in range(4)) * scale
+    lane = lax.broadcasted_iota(jnp.int32, (1, LANES), 1)
+    gain = jnp.zeros((1, LANES), F32)
+    step = 4 * (width // LANES) + 1
+    for side in range(share):
+        at = side * step
+        for part in range(4):
+            row = jnp.concatenate([total[at : at + 1], total[at + 1 : at + 2]], axis=1)
+            if part < 3:
+                qkv_ref[3 * side + part : 3 * side + part + 1, :] = row
+            else:
+                proj_ref[side : side + 1, :] = row
+            at += 2
+        gain = jnp.where(lane == side, total[at : at + 1], gain)
+    gain_ref[...] = gain[:, :share]
 
 
 def on_device(tokens, edge_tokens, output_grad, norm_gain, qkv_weight, out_weight, head_scale):
@@ -200,86 +229,100 @@
     col_devices = lax.axis_size("cols")
     place = lax.axis_index("rows")
     grad_scale = (row_count * row_devices * col_count * col_devices) ** (-0.5)
+    parity = lax.axis_index("cols") & 1
+    strips = jnp.concatenate(
+        [
+            tokens[:REACH],
+            tokens[row_count - REACH :],
+            output_grad[:RADIUS],
+            output_grad[row_count - RADIUS :],
+        ],
+        axis=0,
+    )
+    strips = lax.all_gather(strips, "rows", axis=0).transpose(0, 2, 1, 3)
+    above = strips[jnp.maximum(place - 1, 0)]
+    below = strips[jnp.minimum(place + 1, row_devices - 1)]
     own = tokens.transpose(1, 0, 2)
     grad = output_grad.transpose(1, 0, 2)
     edges = edge_tokens.transpose(2, 0, 1, 3)
-    above, below = exchange(
-        "rows",
-        row_devices,
-        False,
-        jnp.concatenate([own[:, row_count - REACH :], grad[:, row_count - RADIUS :]], axis=1),
-        jnp.concatenate([own[:, :REACH], grad[:, :RADIUS]], axis=1),
-    )
     blank = jnp.zeros((col_count, RADIUS, width), BF16)
-    upper = jnp.where(place == 0, jnp.concatenate([blank, edges[:, 0]], axis=1), above[:, :REACH])
+    upper = jnp.where(
+        place == 0, jnp.concatenate([blank, edges[:, 0]], axis=1), above[:, REACH : 2 * REACH]
+    )
     lower = jnp.where(
         place == row_devices - 1, jnp.concatenate([edges[:, 1], blank], axis=1), below[:, :REACH]
     )
     gap = jnp.zeros((col_count, SPAN - row_count - 2 * REACH, width), BF16)
     slab = jnp.concatenate([own, lower, gap, upper], axis=1)
     grad_gap = jnp.zeros((col_count, SPAN - row_count - 2 * RADIUS, width), BF16)
-    grad_slab = jnp.concatenate([grad, below[:, REACH:], grad_gap, above[:, REACH:]], axis=1)
-    west, east = exchange(
+    grad_slab = jnp.concatenate(
+        [
+            grad,
+            below[:, 2 * REACH : 2 * REACH + RADIUS],
+            grad_gap,
+            above[:, 2 * REACH + RADIUS :],
+        ],
+        axis=1,
+    )
+    facing_west = jnp.concatenate([slab[:REACH], grad_slab[:RADIUS]], axis=0)
+    facing_east = jnp.concatenate([slab[col_count - REACH :], grad_slab[col_count - RADIUS :]], axis=0)
+    first = [i for i in range(1, col_devices, 2)]
+    pairs = [(i, (i + 1) % col_devices) for i in first]
+    odd = lax.ppermute(
+        jnp.where(parity == 0, facing_west, facing_east), "cols", pairs + [(b, a) for a, b in pairs]
+    )
+    even = lax.all_gather(
+        jnp.where(parity == 0, facing_east, facing_west),
         "cols",
-        col_devices,
-        True,
-        jnp.concatenate([slab[col_count - REACH :], grad_slab[col_count - RADIUS :]], axis=0),
-        jnp.concatenate([slab[:REACH], grad_slab[:RADIUS]], axis=0),
+        axis=0,
+        axis_index_groups=[[i, i + 1] for i in range(0, col_devices, 2)],
     )
     cells = col_count * SPAN
     whole = pl.BlockSpec(memory_space=pltpu.VMEM)
     scalars = pl.BlockSpec(memory_space=pltpu.SMEM)
-    token_grad, qkv_grad, proj_grad, gain_grad = pl.pallas_call(
+    token_grad, chunks = pl.pallas_call(
         block_kernel,
         out_shape=(
             jax.ShapeDtypeStruct((cells, width), BF16),
-            jax.ShapeDtypeStruct((3 * width, width), BF16),
-            jax.ShapeDtypeStruct((width, width), BF16),
-            jax.ShapeDtypeStruct((1, width), F32),
+            jax.ShapeDtypeStruct((width, 4 * width + LANES), BF16),
         ),
         in_specs=[scalars, scalars] + [whole] * 7,
-        out_specs=(whole,) * 4,
+        out_specs=(whole,) * 2,
         scratch_shapes=[
             pltpu.VMEM((cells + 2 * REACH * SPAN, width), BF16),
             pltpu.VMEM((cells + 2 * REACH * SPAN, width), BF16),
             pltpu.VMEM((cells, width), F32),
             pltpu.VMEM((cells, width), F32),
+            pltpu.VMEM((width // LANES, 3 * width, LANES), F32),
         ],
         compiler_params=pltpu.CompilerParams(vmem_limit_bytes=40 * 2**20),
     )(
-        jnp.stack([place, row_devices]).astype(jnp.int32),
+        jnp.stack([place, row_devices, parity]).astype(jnp.int32),
         head_scale,
         slab.reshape(cells, width),
         grad_slab.reshape(cells, width),
-        west.reshape(-1, width),
-        east.reshape(-1, width),
+        odd.reshape(-1, width),
+        even.reshape(2, -1, width),
         norm_gain[None, :],
         qkv_weight,
         out_weight,
     )
     token_grad = token_grad.reshape(col_count, SPAN, width)[:, :row_count].transpose(1, 0, 2)
     share = width // col_devices
-    chunks = jnp.concatenate(
-        [
-            qkv_grad.reshape(col_devices, 3 * share, width),
-            proj_grad.reshape(col_devices, share, width),
-        ],
-        axis=1,
-    )
-    gains = jnp.pad(
-        gain_grad.astype(BF16).reshape(col_devices, 1, share),
-        ((0, 0), (0, 4 * share - 1), (0, 128 - share)),
-    )
-    chunks = jnp.concatenate([chunks, gains], axis=2)
-    chunks = lax.all_to_all(chunks, "cols", 0, 0)
-    part = jnp.sum(chunks.astype(F32), axis=0)
-    part = jnp.sum(lax.all_gather(part, "rows", axis=0), axis=0) * grad_scale
-    return (
-        token_grad,
-        part[: 3 * share, :width].T,
-        part[3 * share :, :width].T,
-        part[0, width : width + share],
-    )
+    chunks = lax.all_to_all(chunks.reshape(col_devices, share, -1), "cols", 0, 0)
+    part = jnp.sum(chunks.astype(F32), axis=0).reshape(-1, LANES)
+    part = jnp.pad(part, ((0, -part.shape[0] % 8), (0, 0)))
+    qkv_grad, proj_grad, gain_grad = pl.pallas_call(
+        functools.partial(final_kernel, grad_scale),
+        out_shape=(
+            jax.ShapeDtypeStruct((3 * share, width), F32),
+            jax.ShapeDtypeStruct((share, width), F32),
+            jax.ShapeDtypeStruct((1, share), F32),
+        ),
+        in_specs=[whole],
+        out_specs=(whole,) * 3,
+    )(lax.all_gather(part, "rows", axis=0, tiled=True))
+    return token_grad, qkv_grad.T, proj_grad.T, gain_grad.reshape(share)
 
 
 def solution(mesh):

time: 91.7 us -> 86.7 us (0.945)
  blocking collectives: 7.98 us -> 34.6 us
  starting transfers between devices: 37.4 us -> 17.5 us
  waiting for transfers between devices: 31.8 us -> 19.9 us
  other arithmetic: 2.75 us -> 0.89 us
  Pallas kernels: 4.92 us -> 6.39 us
    all_gather x1 -> x3, blocking collectives: 7.98 us -> 34.6 us  [the longest x1 16.5 us: on_device(): strips = lax.all_gather(strips, 'rows', axis=0).transpose(0, 2, 1, 3)]
    ppermute x4 -> x1, starting transfers between devices: 26 us -> 8.43 us  [on_device(): lax.ppermute(jnp.where(parity == 0, facing_west, facing_east), 'cols', pa...]
    ppermute x4 -> x1, waiting for transfers between devices: 9.5 us -> 0.01 us  [on_device(): lax.ppermute(jnp.where(parity == 0, facing_west, facing_east), 'cols', pa...]
    unnamed x11 -> x12, local copies, waits for them, and re-layouts: 0.68 us -> 3.13 us
    all_to_all x1, starting transfers between devices: 11.4 us -> 9.02 us  [on_device(): lax.all_to_all(chunks.reshape(col_devices, share, -1), 'cols', 0, 0)]
    all_to_all x1, waiting for transfers between devices: 22.3 us -> 19.9 us  [on_device(): lax.all_to_all(chunks.reshape(col_devices, share, -1), 'cols', 0, 0)]
    concatenate x6 -> x2, other arithmetic: 2.36 us -> 0.1 us  [the longest x1 0.09 us: on_device(): jnp.concatenate([grad, below[:, 2 * REACH:2 * REACH + RADIUS], grad_gap,...]
    pallas_call x0 -> x1, Pallas kernels: none -> 1.41 us  [on_device(): pl.pallas_call(functools.partial(final_kernel, grad_scale), out_shape=(ja...]
  transfers between devices with their start and end apart: 5 -> 2, of which waited for: 4 -> 1; matrix products, arithmetic and copies ran while one was open for 2% -> 1% of each run, Pallas kernels for 0% -> 0%
where the time goes in v3:
time: 86.7 us; the launch traced here: 86.1 us
  blocking collectives  34.6 us (40%)
  waiting for transfers between devices  19.9 us (23%)
  starting transfers between devices  17.5 us (20%)
  Pallas kernels  6.39 us (7%)
  local copies, waits for them, and re-layouts  5.99 us (7%)
  other arithmetic  0.89 us (1%)
    all_to_all x1, waiting for transfers between devices, on_device(): lax.all_to_all(chunks.reshape(col_devices, share, -1), 'cols', 0, 0)  19.9 us
    all_gather x1, blocking collectives, on_device(): strips = lax.all_gather(strips, 'rows', axis=0).transpose(0, 2, 1, 3)  16.5 us
    all_gather x1, blocking collectives, on_device(): lax.all_gather(part, 'rows', axis=0, tiled=True)  12.4 us
    all_to_all x1, starting transfers between devices, on_device(): lax.all_to_all(chunks.reshape(col_devices, share, -1), 'cols', 0, 0)  9.02 us
    ppermute x1, starting transfers between devices, on_device(): lax.ppermute(jnp.where(parity == 0, facing_west, facing_east), 'cols', pa...  8.43 us
    all_gather x1, blocking collectives, on_device(): lax.all_gather(jnp.where(parity == 0, facing_east, facing_west), 'cols',...  5.66 us
    pallas_call x1, Pallas kernels, on_device(): pl.pallas_call(block_kernel, out_shape=(jax.ShapeDtypeStruct((cells, widt...  4.98 us
    unnamed x12, local copies, waits for them, and re-layouts  3.13 us
  transfers between devices with their start and end apart: 2, of which 1 were waited for; matrix products, arithmetic and copies ran while one was open for 1% of the time, Pallas kernels for 0%

profile of v3, /device:TPU:1, one launch (start us, length us, event | category | flops | bytes accessed | tf_op | source)
XLA Modules:
  0.0 86.1 jit_solution(2595551629907523772)
XLA Ops:
  0.6 0.8 fusion
  1.4 0.9 copy.33
  2.3 0.7 fusion.1
  3.0 0.9 copy.32
  3.9 0.1 pad.21.clone
  3.9 0.1 pad.17.clone
  4.0 0.8 copy.34
  4.8 16.5 %all-gather = bf16[72,8,256]{2,1,0:T(8,128)(2,1)S(1)} all-gather(bf16[18,8,256]{2,1,0:T(8,128)(2,1)S(1)} %pad_maximum_fusion.2), channel_id=2, replica_groups=mesh['cols'=128,'rows'=4] {'rows'}, dimensions={0}, use_global_device_ids=true | all-gather | bytes 368640 | tf_op jit(solution)/shard_map/all_gather | solution.py:242
  21.4 0.1 pad_maximum_fusion.1
  21.6 0.1 pad_maximum_fusion
  21.7 0.0 copy-start
  21.7 0.0 copy-start.1
  21.8 0.0 copy-start.2
  21.8 0.0 copy-start.3
  21.8 8.4 %collective-permute-start = (bf16[9,32,256]{2,1,0:T(8,128)(2,1)S(1)}, bf16[9,32,256]{2,1,0:T(8,128)(2,1)S(1)}, u32[]{:S(2)}, u32[]{:S(2)}) collective-permute-start(bf16[9,32,256]{2,1,0:T(8,128)(2,1)S(1)} %maximum_select_fusion), channel_id=1, source_target_pairs={{4,8},{12,16},{20,24},{28,32},{36,40},{44,48},{52,56},{60,64},{68,... | collective-permute-start | bytes 442376 | tf_op jit(solution)/shard_map/ppermute | solution.py:271
  30.3 5.7 %all_gather.15 = bf16[2,9,32,256]{3,2,1,0:T(8,128)(2,1)S(1)} all-gather(bf16[1,9,32,256]{3,2,1,0:T(8,128)(2,1)S(1)} %maximum_select_fusion.1), channel_id=1, replica_groups={{0,4},{8,12},{16,20},{24,28},{32,36},{40,44},{48,52},{56,60},{64,68},{7..., dimensions={0}, use_global_device_ids=true | all-gather | bytes 442368 | tf_op jit(solution)/shard_map/all_gather | solution.py:274
  36.0 0.1 pad_add_fusion.place_ref
  36.0 0.0 collective-permute-done
  36.0 0.0 copy-done
  36.0 0.0 copy-done.1
  36.0 0.0 copy-done.2
  36.0 0.0 copy-done.3
  36.1 5.0 %shard_map.102 = (bf16[256,256]{1,0:T(8,128)(2,1)S(1)}, bf16[256,1152]{1,0:T(8,128)(2,1)S(1)}) custom-call(s32[3]{0:T(128)S(1)} %pad_add_fusion.place_ref, f32[4]{0:T(128)S(1)} %copy-done.3, bf16[256,256]{1,0:T(8,128)(2,1)S(1)} %bitcast.44, bf16[256,256]{1,0:T(8,128)(2,1)S(1)} %bitcast.46, bf16[288,256]{1,0:T(8,128)(2,1)S(1)} %bitcast.47, ...), custom_call_target="tpu_custom_call" | custom-call | tf_op jit(solution)/shard_map/pallas_call | solution.py:283
  41.0 1.0 %reshape.92 = bf16[128,2,1152]{2,1,0:T(2,128)(2,1)} reshape(bf16[256,1152]{1,0:T(8,128)(2,1)S(1)} %get-tuple-element.10) | data formatting | bytes 1179648 | tf_op jit(solution)/shard_map/reshape | solution.py:312
  42.1 9.0 %all-to-all-start = ((bf16[128,2,1152]{2,1,0:T(2,128)(2,1)}), bf16[128,2,1152]{2,1,0:T(2,128)(2,1)S(1)}, u32[]{:S(2)}, u32[]{:S(2)}) async-start(bf16[128,2,1152]{2,1,0:T(2,128)(2,1)} %reshape.92), calls=%async_computation | async-start | bytes 1179648 | tf_op jit(solution)/shard_map/all_to_all | solution.py:312
  51.1 0.7 copy.31
  51.8 19.9 %all-to-all-done = bf16[128,2,1152]{2,1,0:T(2,128)(2,1)S(1)} async-done(((bf16[128,2,1152]{2,1,0:T(2,128)(2,1)}), bf16[128,2,1152]{2,1,0:T(2,128)(2,1)S(1)}, u32[]{:S(2)}, u32[]{:S(2)}) %all-to-all-start) | async-done | bytes 589856 | tf_op jit(solution)/shard_map/all_to_all | solution.py:312
  71.7 0.5 convert_reduce_fusion
  72.3 12.4 %all_gather.16.parts_ref = f32[96,128]{1,0:T(8,128)} all-gather(f32[24,128]{1,0:T(8,128)S(1)} %pad.6), channel_id=1, replica_groups=mesh['cols'=128,'rows'=4] {'rows'}, dimensions={0}, use_global_device_ids=true | all-gather | bytes 61440 | tf_op jit(solution)/shard_map/all_gather | solution.py:324
  84.7 1.4 %shard_map.103 = (f32[6,256]{1,0:T(8,128)}, f32[2,256]{1,0:T(2,128)}, f32[1,2]{1,0:T(1,128)}) custom-call(f32[96,128]{1,0:T(8,128)} %all_gather.16.parts_ref), custom_call_target="tpu_custom_call" | custom-call | tf_op jit(solution)/shard_map/pallas_call | solution.py:315
  (17 shorter events, 0.3 us)
Async XLA Ops:
  21.7 14.3 %copy-start = (bf16[256,768]{1,0:T(8,128)(2,1)S(1)}, bf16[256,768]{1,0:T(8,128)(2,1)}, u32[]{:S(2)}) copy-start(bf16[256,768]{1,0:T(8,128)(2,1)} %qkv_ref.1) | copy-start | bytes 1179652
  21.7 14.3 %copy-start.1 = (bf16[256,256]{1,0:T(8,128)(2,1)S(1)}, bf16[256,256]{1,0:T(8,128)(2,1)}, u32[]{:S(2)}) copy-start(bf16[256,256]{1,0:T(8,128)(2,1)} %out_ref.1) | copy-start | bytes 393220
  21.8 14.3 %copy-start.2 = (f32[256]{0:T(256)S(1)}, f32[256]{0:T(256)}, u32[]{:S(2)}) copy-start(f32[256]{0:T(256)} %param.10) | copy-start | bytes 3076
  21.8 14.3 %copy-start.3 = (f32[4]{0:T(128)S(1)}, f32[4]{0:T(128)}, u32[]{:S(2)}) copy-start(f32[4]{0:T(128)} %scale_ref.1) | copy-start | bytes 52
  21.8 14.2 %collective-permute-start = (bf16[9,32,256]{2,1,0:T(8,128)(2,1)S(1)}, bf16[9,32,256]{2,1,0:T(8,128)(2,1)S(1)}, u32[]{:S(2)}, u32[]{:S(2)}) collective-permute-start(bf16[9,32,256]{2,1,0:T(8,128)(2,1)S(1)} %maximum_select_fusion), channel_id=1, source_target_pairs={{4,8},{12,16},{20,24},{28,32},{36,40},{44,48},{52,56},{60,64},{68,... | collective-permute-start | bytes 442376 | tf_op jit(solution)/shard_map/ppermute | solution.py:271
  42.1 29.6 %all-to-all-start = ((bf16[128,2,1152]{2,1,0:T(2,128)(2,1)}), bf16[128,2,1152]{2,1,0:T(2,128)(2,1)S(1)}, u32[]{:S(2)}, u32[]{:S(2)}) async-start(bf16[128,2,1152]{2,1,0:T(2,128)(2,1)} %reshape.92), calls=%async_computation | async-start | bytes 1179648 | tf_op jit(solution)/shard_map/all_to_all | solution.py:312

commit v4 on v3

--- a/solution.py
+++ b/solution.py
@@ -16,6 +16,10 @@
 REACH = 2 * RADIUS
 BAND = 4
 LANES = 128
+TAIL = 16
+COLS = ("x", "l", "y")
+ROWS = ("h", "c")
+SPLIT = (4, 4, 8)
 LOWEST = -1e30
 F32 = jnp.float32
 BF16 = jnp.bfloat16
@@ -51,7 +55,7 @@
 def block_kernel(
     place_ref, scale_ref, own_ref, own_grad_ref, odd_ref, even_ref, gain_ref, qkv_ref, out_ref,
     token_ref, chunk_ref,
-    key_ref, value_ref, key_grad_ref, value_grad_ref, weight_grad_ref,
+    key_ref, value_ref, key_grad_ref, value_grad_ref, weight_grad_ref, proj_grad_ref,
 ):
     width = own_ref.shape[1]
     own_count = own_ref.shape[0]
@@ -189,47 +193,67 @@
     scaled = normed_grad * gain
     token_part = reciprocal * (scaled - unit * jnp.mean(scaled * unit, axis=-1, keepdims=True))
     token_ref[...] = (own_grad.astype(F32) + token_part).astype(BF16)
+    attended = jnp.where(own_rows, jnp.concatenate(attended, axis=0), 0.0).astype(BF16)
     weight_grad = dot(projected_grad, normed, 0, 0)
-    blocks = range(width // LANES)
-    for block in blocks:
-        weight_grad_ref[block] = weight_grad[:, block * LANES : (block + 1) * LANES]
-    attended = jnp.where(own_rows, jnp.concatenate(attended, axis=0), 0.0).astype(BF16)
-    for part in range(3):
-        for block in blocks:
-            third = weight_grad_ref.at[block][pl.ds(part, width, stride=3), :]
-            at = part * width + block * LANES
-            chunk_ref[:, at : at + LANES] = third.astype(BF16)
-    chunk_ref[:, 3 * width : 4 * width] = dot(own_grad, attended, 0, 0).astype(BF16)
-    chunk_ref[:, 4 * width :] = jnp.broadcast_to(gain_grad, (LANES, width)).T.astype(BF16)
-
-
-def final_kernel(scale, parts_ref, qkv_ref, proj_ref, gain_ref):
-    share, width = proj_ref.shape
-    rows = parts_ref.shape[0] // 4
-    total = sum(parts_ref[part * rows : (part + 1) * rows] for part in range(4)) * scale
+    proj_grad = dot(own_grad, attended, 0, 0)
+    for block in range(width // LANES):
+        at = slice(block * LANES, (block + 1) * LANES)
+        weight_grad_ref[block] = weight_grad[:, at]
+        proj_grad_ref[block] = proj_grad[:, at]
+    blocks, rows = chunk_ref.shape[:2]
+    group = (rows - TAIL) // 8
+    for peer in range(blocks):
+        line, side = peer // 2, peer % 2
+        for part in range(4):
+            for block in range(width // LANES):
+                if part < 3:
+                    start = 6 * group * line + 3 * side + part
+                    cells = weight_grad_ref.at[block][pl.ds(start, group, stride=6), :]
+                else:
+                    start = 2 * group * line + side
+                    cells = proj_grad_ref.at[block][pl.ds(start, group, stride=2), :]
+                at = (2 * part + block) * group
+                chunk_ref[peer, at : at + group] = cells.astype(BF16)
+        lanes = gain_grad[:, 2 * group * line // LANES * LANES :][:, :LANES]
+        chunk_ref[peer, rows - TAIL :] = jnp.broadcast_to(lanes, (TAIL, LANES)).astype(BF16)
+
+
+def middle_kernel(chunk_ref, part_ref, sum_ref):
+    group = sum_ref.shape[0] // 8
+    copies = part_ref.shape[0] // group
+    total = sum(chunk_ref[peer].astype(F32) for peer in range(chunk_ref.shape[0]))
+    sum_ref[...] = total[: 8 * group]
+    gains = total[8 * group : 8 * group + TAIL - 8]
+    for column in range(group):
+        rows = jnp.concatenate([sum_ref[pl.ds(column, 8, stride=group), :], gains], axis=0).astype(BF16)
+        for copy in range(copies):
+            part_ref[copies * column + copy] = rows
+
+
+def final_kernel(scale, place_ref, parts_ref, qkv_ref, proj_ref, gain_ref):
+    total = parts_ref[...] * scale
     lane = lax.broadcasted_iota(jnp.int32, (1, LANES), 1)
-    gain = jnp.zeros((1, LANES), F32)
-    step = 4 * (width // LANES) + 1
-    for side in range(share):
-        at = side * step
+    gains = []
+    for side in range(2):
         for part in range(4):
+            at = side * TAIL + 2 * part
             row = jnp.concatenate([total[at : at + 1], total[at + 1 : at + 2]], axis=1)
             if part < 3:
                 qkv_ref[3 * side + part : 3 * side + part + 1, :] = row
             else:
                 proj_ref[side : side + 1, :] = row
-            at += 2
-        gain = jnp.where(lane == side, total[at : at + 1], gain)
-    gain_ref[...] = gain[:, :share]
+        here = lane == 2 * place_ref[0] % LANES + side
+        gains.append(jnp.sum(jnp.where(here, total[at + 2 : at + 3], 0.0), axis=1, keepdims=True))
+    gain_ref[...] = jnp.concatenate(gains, axis=1)
 
 
 def on_device(tokens, edge_tokens, output_grad, norm_gain, qkv_weight, out_weight, head_scale):
     row_count, col_count, width = tokens.shape
-    row_devices = lax.axis_size("rows")
-    col_devices = lax.axis_size("cols")
-    place = lax.axis_index("rows")
+    row_devices = lax.axis_size(ROWS)
+    col_devices = lax.axis_size(COLS)
+    place = lax.axis_index(ROWS)
     grad_scale = (row_count * row_devices * col_count * col_devices) ** (-0.5)
-    parity = lax.axis_index("cols") & 1
+    parity = lax.axis_index(COLS) & 1
     strips = jnp.concatenate(
         [
             tokens[:REACH],
@@ -239,7 +263,7 @@
         ],
         axis=0,
     )
-    strips = lax.all_gather(strips, "rows", axis=0).transpose(0, 2, 1, 3)
+    strips = lax.all_gather(strips, ROWS, axis=0).transpose(0, 2, 1, 3)
     above = strips[jnp.maximum(place - 1, 0)]
     below = strips[jnp.minimum(place + 1, row_devices - 1)]
     own = tokens.transpose(1, 0, 2)
@@ -269,22 +293,24 @@
     first = [i for i in range(1, col_devices, 2)]
     pairs = [(i, (i + 1) % col_devices) for i in first]
     odd = lax.ppermute(
-        jnp.where(parity == 0, facing_west, facing_east), "cols", pairs + [(b, a) for a, b in pairs]
+        jnp.where(parity == 0, facing_west, facing_east), COLS, pairs + [(b, a) for a, b in pairs]
     )
     even = lax.all_gather(
         jnp.where(parity == 0, facing_east, facing_west),
-        "cols",
+        COLS,
         axis=0,
         axis_index_groups=[[i, i + 1] for i in range(0, col_devices, 2)],
     )
     cells = col_count * SPAN
+    lines = lax.axis_size("x")
+    group = col_devices // lines
     whole = pl.BlockSpec(memory_space=pltpu.VMEM)
     scalars = pl.BlockSpec(memory_space=pltpu.SMEM)
     token_grad, chunks = pl.pallas_call(
         block_kernel,
         out_shape=(
             jax.ShapeDtypeStruct((cells, width), BF16),
-            jax.ShapeDtypeStruct((width, 4 * width + LANES), BF16),
+            jax.ShapeDtypeStruct((2 * lines, 8 * group + TAIL, LANES), BF16),
         ),
         in_specs=[scalars, scalars] + [whole] * 7,
         out_specs=(whole,) * 2,
@@ -294,6 +320,7 @@
             pltpu.VMEM((cells, width), F32),
             pltpu.VMEM((cells, width), F32),
             pltpu.VMEM((width // LANES, 3 * width, LANES), F32),
+            pltpu.VMEM((width // LANES, width, LANES), F32),
         ],
         compiler_params=pltpu.CompilerParams(vmem_limit_bytes=40 * 2**20),
     )(
@@ -308,36 +335,44 @@
         out_weight,
     )
     token_grad = token_grad.reshape(col_count, SPAN, width)[:, :row_count].transpose(1, 0, 2)
-    share = width // col_devices
-    chunks = lax.all_to_all(chunks.reshape(col_devices, share, -1), "cols", 0, 0)
-    part = jnp.sum(chunks.astype(F32), axis=0).reshape(-1, LANES)
-    part = jnp.pad(part, ((0, -part.shape[0] % 8), (0, 0)))
+    chunks = lax.all_to_all(chunks, ("x", "c"), 0, 0)
+    halves = lax.axis_size("h")
+    part = pl.pallas_call(
+        middle_kernel,
+        out_shape=jax.ShapeDtypeStruct((halves * group, TAIL, LANES), BF16),
+        in_specs=[whole],
+        out_specs=whole,
+        scratch_shapes=[pltpu.VMEM((8 * group, LANES), F32)],
+    )(chunks)
+    part = jnp.sum(lax.all_to_all(part, ("l", "y", "h"), 0, 0).astype(F32), axis=0)
     qkv_grad, proj_grad, gain_grad = pl.pallas_call(
         functools.partial(final_kernel, grad_scale),
         out_shape=(
-            jax.ShapeDtypeStruct((3 * share, width), F32),
-            jax.ShapeDtypeStruct((share, width), F32),
-            jax.ShapeDtypeStruct((1, share), F32),
+            jax.ShapeDtypeStruct((6, width), F32),
+            jax.ShapeDtypeStruct((2, width), F32),
+            jax.ShapeDtypeStruct((1, 2), F32),
         ),
-        in_specs=[whole],
+        in_specs=[scalars, whole],
         out_specs=(whole,) * 3,
-    )(lax.all_gather(part, "rows", axis=0, tiled=True))
-    return token_grad, qkv_grad.T, proj_grad.T, gain_grad.reshape(share)
+    )(lax.axis_index(COLS)[None].astype(jnp.int32), lax.all_gather(part, "c", axis=0, tiled=True))
+    return token_grad, qkv_grad.T, proj_grad.T, gain_grad.reshape(2)
 
 
 def solution(mesh):
+    parts = SPLIT + (2, 2)
+    fine = jax.sharding.Mesh(mesh.devices.reshape(parts), COLS + ROWS)
     return jax.shard_map(
         on_device,
-        mesh=mesh,
+        mesh=fine,
         in_specs=(
-            P("rows", "cols", None),
-            P(None, None, "cols", None),
-            P("rows", "cols", None),
+            P(ROWS, COLS, None),
+            P(None, None, COLS, None),
+            P(ROWS, COLS, None),
             P(),
             P(),
             P(),
             P(),
         ),
-        out_specs=(P("rows", "cols", None), P(None, "cols"), P(None, "cols"), P("cols")),
+        out_specs=(P(ROWS, COLS, None), P(None, COLS), P(None, COLS), P(COLS)),
         check_vma=False,
     )

time: 86.7 us -> 84.3 us (0.972)
  waiting for transfers between devices: 19.9 us -> 12.8 us
  blocking collectives: 34.6 us -> 41.2 us
  local copies, waits for them, and re-layouts: 5.99 us -> 3.87 us
  Pallas kernels: 6.39 us -> 8.18 us
  starting transfers between devices: 17.5 us -> 16.4 us
    all_to_all x0 -> x1, blocking collectives: none -> 14.6 us  [on_device(): chunks = lax.all_to_all(chunks, ('x', 'c'), 0, 0)]
    all_gather x3, blocking collectives: 34.6 us -> 26.7 us  [the longest x1 16.5 us: on_device(): strips = lax.all_gather(strips, ROWS, axis=0).transpose(0, 2, 1, 3)]
    all_to_all x1, waiting for transfers between devices: 19.9 us -> 12.8 us  [on_device(): lax.all_to_all(part, ('l', 'y', 'h'), 0, 0).astype(F32)]
    pallas_call x0 -> x1, Pallas kernels: none -> 1.92 us  [on_device(): pl.pallas_call(middle_kernel, out_shape=jax.ShapeDtypeStruct((halves * gr...]
    reshape x2 -> x0, local copies, waits for them, and re-layouts: 1.05 us -> none  [the longest x1 1.04 us: on_device(): chunks.reshape(col_devices, share, -1)]
    all_to_all x1, starting transfers between devices: 9.02 us -> 8.07 us  [on_device(): lax.all_to_all(part, ('l', 'y', 'h'), 0, 0).astype(F32)]
    unnamed x12 -> x18, local copies, waits for them, and re-layouts: 3.13 us -> 2.76 us
where the time goes in v4:
time: 84.3 us; the launch traced here: 83.7 us
  blocking collectives  41.2 us (49%)
  starting transfers between devices  16.4 us (19%)
  waiting for transfers between devices  12.8 us (15%)
  Pallas kernels  8.18 us (10%)
  local copies, waits for them, and re-layouts  3.87 us (5%)
  between operations  0.86 us (1%)
    all_gather x1, blocking collectives, on_device(): strips = lax.all_gather(strips, ROWS, axis=0).transpose(0, 2, 1, 3)  16.5 us
    all_to_all x1, blocking collectives, on_device(): chunks = lax.all_to_all(chunks, ('x', 'c'), 0, 0)  14.6 us
    all_to_all x1, waiting for transfers between devices, on_device(): lax.all_to_all(part, ('l', 'y', 'h'), 0, 0).astype(F32)  12.8 us
    ppermute x1, starting transfers between devices, on_device(): lax.ppermute(jnp.where(parity == 0, facing_west, facing_east), COLS, pair...  8.3 us
    all_to_all x1, starting transfers between devices, on_device(): lax.all_to_all(part, ('l', 'y', 'h'), 0, 0).astype(F32)  8.07 us
    all_gather x1, blocking collectives, on_device(): lax.all_gather(jnp.where(parity == 0, facing_east, facing_west), COLS, ax...  5.79 us
    pallas_call x1, Pallas kernels, on_device(): pl.pallas_call(block_kernel, out_shape=(jax.ShapeDtypeStruct((cells, widt...  4.93 us
    all_gather x1, blocking collectives, on_device(): lax.all_gather(part, 'c', axis=0, tiled=True)  4.38 us
  transfers between devices with their start and end apart: 2, of which 1 were waited for; matrix products, arithmetic and copies ran while one was open for 1% of the time, Pallas kernels for 0%

profile of v4, /device:TPU:1, one launch (start us, length us, event | category | flops | bytes accessed | tf_op | source)
XLA Modules:
  0.0 83.7 jit_solution(4456919469413721267)
XLA Ops:
  0.6 0.0 copy-start.4
  0.6 0.8 fusion
  1.4 0.0 copy-done.4
  1.5 0.0 copy-start.5
  1.5 0.8 copy-done.5
  2.3 0.0 copy-start.6
  2.4 0.1 pad.16.clone
  2.5 0.1 pad.12.clone
  2.5 0.5 copy-done.6
  3.1 16.5 %all-gather = bf16[72,8,256]{2,1,0:T(8,128)(2,1)S(1)} all-gather(bf16[18,8,256]{2,1,0:T(8,128)(2,1)S(1)} %pad_maximum_fusion.2), channel_id=2, replica_groups=mesh['x'=4,'l'=4,'y'=8,'h'=2,'c'=2] {'h','c'}, dimensions={0}, use_global_device_ids=true | all-gather | bytes 368640 | tf_op jit(solution)/shard_map/all_gather | solution.py:266
  19.7 0.1 pad_maximum_fusion.1
  19.9 0.1 pad_maximum_fusion
  20.1 8.3 %collective-permute-start = (bf16[9,32,256]{2,1,0:T(8,128)(2,1)S(1)}, bf16[9,32,256]{2,1,0:T(8,128)(2,1)S(1)}, u32[]{:S(2)}, u32[]{:S(2)}) collective-permute-start(bf16[9,32,256]{2,1,0:T(8,128)(2,1)S(1)} %maximum_select_fusion), channel_id=1, source_target_pairs={{4,8},{12,16},{20,24},{28,32},{36,40},{44,48},{52,56},{60,64},{68,... | collective-permute-start | bytes 442376 | tf_op jit(solution)/shard_map/ppermute | solution.py:295
  28.4 0.0 copy-start
  28.4 0.0 copy-start.1
  28.5 5.8 %all_gather.15 = bf16[2,9,32,256]{3,2,1,0:T(8,128)(2,1)S(1)} all-gather(bf16[1,9,32,256]{3,2,1,0:T(8,128)(2,1)S(1)} %maximum_select_fusion.1), channel_id=1, replica_groups={{0,4},{8,12},{16,20},{24,28},{32,36},{40,44},{48,52},{56,60},{64,68},{7..., dimensions={0}, use_global_device_ids=true | all-gather | bytes 442368 | tf_op jit(solution)/shard_map/all_gather | solution.py:298
  34.2 0.1 pad_add_fusion.place_ref
  34.3 0.0 collective-permute-done
  34.3 0.0 copy-start.2
  34.3 0.0 copy-done
  34.3 0.0 copy-done.1
  34.3 0.7 copy-done.2
  35.0 0.0 copy-done.3
  35.0 4.9 %shard_map.102 = (bf16[256,256]{1,0:T(8,128)(2,1)S(1)}, bf16[8,272,128]{2,1,0:T(8,128)(2,1)S(1)}) custom-call(s32[3]{0:T(128)S(1)} %pad_add_fusion.place_ref, f32[4]{0:T(128)S(1)} %copy-done.3, bf16[256,256]{1,0:T(8,128)(2,1)S(1)} %bitcast.45, bf16[256,256]{1,0:T(8,128)(2,1)S(1)} %bitcast.47, bf16[288,256]{1,0:T(8,128)(2,1)S(1)} %bitcast.48, ...), custom_call_target="tpu_custom_call" | custom-call | tf_op jit(solution)/shard_map/pallas_call | solution.py:309
  39.9 14.6 %all_to_all.10.chunk_ref = bf16[8,272,128]{2,1,0:T(8,128)(2,1)} all-to-all(bf16[8,272,128]{2,1,0:T(8,128)(2,1)S(1)} %get-tuple-element.10), channel_id=1, replica_groups=mesh['x'=4,'l'=4,'y'=8,'h'=2,'c'=2] {'x','c'}, dimensions={0} | all-to-all | bytes 1114112 | tf_op jit(solution)/shard_map/all_to_all | solution.py:338
  54.5 1.9 %shard_map.103 = bf16[64,16,128]{2,1,0:T(8,128)(2,1)} custom-call(bf16[8,272,128]{2,1,0:T(8,128)(2,1)} %all_to_all.10.chunk_ref), custom_call_target="tpu_custom_call" | custom-call | tf_op jit(solution)/shard_map/pallas_call | solution.py:340
  56.4 8.1 %all-to-all-start.1 = ((bf16[64,16,128]{2,1,0:T(8,128)(2,1)}), bf16[64,16,128]{2,1,0:T(8,128)(2,1)S(1)}, u32[]{:S(2)}, u32[]{:S(2)}) async-start(bf16[64,16,128]{2,1,0:T(8,128)(2,1)} %shard_map.103), calls=%async_computation.1 | async-start | bytes 524288 | tf_op jit(solution)/shard_map/all_to_all | solution.py:347
  64.5 0.7 copy.31
  65.2 12.8 %all-to-all-done.1 = bf16[64,16,128]{2,1,0:T(8,128)(2,1)S(1)} async-done(((bf16[64,16,128]{2,1,0:T(8,128)(2,1)}), bf16[64,16,128]{2,1,0:T(8,128)(2,1)S(1)}, u32[]{:S(2)}, u32[]{:S(2)}) %all-to-all-start.1) | async-done | bytes 262176 | tf_op jit(solution)/shard_map/all_to_all | solution.py:347
  78.0 0.1 convert_reduce_fusion
  78.0 4.4 %all_gather.16.parts_ref = f32[32,128]{1,0:T(8,128)} all-gather(f32[16,128]{1,0:T(8,128)S(1)} %convert_reduce_fusion), channel_id=1, replica_groups=mesh['x'=4,'l'=4,'y'=8,'h'=2,'c'=2] {'c'}, dimensions={0}, use_global_device_ids=true | all-gather | bytes 24576 | tf_op jit(solution)/shard_map/all_gather | solution.py:357
  82.4 1.3 %shard_map.104 = (f32[6,256]{1,0:T(8,128)}, f32[2,256]{1,0:T(2,128)}, f32[1,2]{1,0:T(1,128)}) custom-call(s32[1]{0:T(128)} %bitcast.25.place_ref, f32[32,128]{1,0:T(8,128)} %all_gather.16.parts_ref), custom_call_target="tpu_custom_call" | custom-call | tf_op jit(solution)/shard_map/pallas_call | solution.py:348
  (20 shorter events, 0.3 us)
Async XLA Ops:
  0.6 0.8 %copy-start.4 = (bf16[16,8,256]{2,1,0:T(8,128)(2,1)S(1)}, bf16[16,8,256]{2,1,0:T(8,128)(2,1)}, u32[]{:S(2)}) copy-start(bf16[16,8,256]{2,1,0:T(8,128)(2,1)} %param.7) | copy-start | bytes 196612
  1.5 0.8 %copy-start.5 = (bf16[16,8,256]{2,1,0:T(8,128)(2,1)S(1)}, bf16[16,8,256]{2,1,0:T(8,128)(2,1)}, u32[]{:S(2)}) copy-start(bf16[16,8,256]{2,1,0:T(8,128)(2,1)} %param.9) | copy-start | bytes 196612
  2.3 0.7 copy-start.6
  20.1 14.2 %collective-permute-start = (bf16[9,32,256]{2,1,0:T(8,128)(2,1)S(1)}, bf16[9,32,256]{2,1,0:T(8,128)(2,1)S(1)}, u32[]{:S(2)}, u32[]{:S(2)}) collective-permute-start(bf16[9,32,256]{2,1,0:T(8,128)(2,1)S(1)} %maximum_select_fusion), channel_id=1, source_target_pairs={{4,8},{12,16},{20,24},{28,32},{36,40},{44,48},{52,56},{60,64},{68,... | collective-permute-start | bytes 442376 | tf_op jit(solution)/shard_map/ppermute | solution.py:295
  28.4 5.9 %copy-start = (bf16[256,768]{1,0:T(8,128)(2,1)S(1)}, bf16[256,768]{1,0:T(8,128)(2,1)}, u32[]{:S(2)}) copy-start(bf16[256,768]{1,0:T(8,128)(2,1)} %qkv_ref.1) | copy-start | bytes 1179652
  28.4 5.9 %copy-start.1 = (bf16[256,256]{1,0:T(8,128)(2,1)S(1)}, bf16[256,256]{1,0:T(8,128)(2,1)}, u32[]{:S(2)}) copy-start(bf16[256,256]{1,0:T(8,128)(2,1)} %out_ref.1) | copy-start | bytes 393220
  34.3 0.7 copy-start.2
  34.3 0.7 copy-start.3
  56.4 21.5 %all-to-all-start.1 = ((bf16[64,16,128]{2,1,0:T(8,128)(2,1)}), bf16[64,16,128]{2,1,0:T(8,128)(2,1)S(1)}, u32[]{:S(2)}, u32[]{:S(2)}) async-start(bf16[64,16,128]{2,1,0:T(8,128)(2,1)} %shard_map.103), calls=%async_computation.1 | async-start | bytes 524288 | tf_op jit(solution)/shard_map/all_to_all | solution.py:347

commit v5 on v4

--- a/solution.py
+++ b/solution.py
@@ -1,4 +1,5 @@
 import functools
+import math
 
 import jax
 import jax.numpy as jnp
@@ -52,13 +53,47 @@
     return reciprocal * (grad - hat * head_mean(grad * hat, group))
 
 
+def head_group(width):
+    head = lax.broadcasted_iota(jnp.int32, (width, width), 0) // HEAD_DIM
+    return (head == lax.broadcasted_iota(jnp.int32, (width, width), 1) // HEAD_DIM).astype(BF16)
+
+
+def own_kernel(
+    head_ref, own_ref, own_grad_ref, gain_ref, qkv_ref, out_ref,
+    factor_ref, unit_ref, scale_ref, normed_ref, key_ref, key_recip_ref, key_b_ref, value_b_ref, query_ref, query_recip_ref, up_ref,
+):
+    width = own_ref.shape[1]
+    lane = lax.broadcasted_iota(jnp.int32, (1, width), 1) // HEAD_DIM
+    factor_ref[...] = jnp.zeros_like(factor_ref)
+    for head in range(HEADS):
+        factor = jnp.broadcast_to(head_ref[:, head : head + 1] * (1.0 / HEAD_DIM), (1, width))
+        factor_ref[:1] = jnp.where(lane == head, factor, factor_ref[:1])
+    weight = qkv_ref[...]
+    group = head_group(width)
+    unit, reciprocal = unit_norm(own_ref[...])
+    normed = (unit * gain_ref[...]).astype(BF16)
+    keys, key_recip = head_norm(dot(normed, weight[:, width : 2 * width]), group)
+    queries, query_recip = head_norm(dot(normed, weight[:, :width]), group)
+    unit_ref[...] = unit
+    scale_ref[...] = jnp.broadcast_to(reciprocal, scale_ref.shape)
+    normed_ref[...] = normed
+    key_ref[...] = keys
+    key_recip_ref[...] = key_recip
+    key_b_ref[...] = keys.astype(BF16)
+    value_b_ref[...] = dot(normed, weight[:, 2 * width :]).astype(BF16)
+    query_ref[...] = queries
+    query_recip_ref[...] = query_recip
+    up_ref[...] = dot(own_grad_ref[...], out_ref[...], 1, 1)
+
+
 def block_kernel(
-    place_ref, scale_ref, own_ref, own_grad_ref, odd_ref, even_ref, gain_ref, qkv_ref, out_ref,
+    place_ref, own_grad_ref, odd_ref, even_ref, gain_ref, qkv_ref, out_ref,
+    factor_ref, own_unit_ref, own_scale_ref, own_normed_ref, own_key_ref, own_key_recip_ref, own_key_b_ref, own_value_b_ref,
+    own_query_ref, own_query_recip_ref, own_up_ref,
     token_ref, chunk_ref,
     key_ref, value_ref, key_grad_ref, value_grad_ref, weight_grad_ref, proj_grad_ref,
 ):
-    width = own_ref.shape[1]
-    own_count = own_ref.shape[0]
+    own_count, width = own_grad_ref.shape
     strip = REACH * SPAN
     top = place_ref[0] == 0
     bottom = place_ref[0] == place_ref[1] - 1
@@ -68,8 +103,7 @@
     east = jnp.where(parity == 0, even_strip, odd_strip)
     gain = gain_ref[...]
     weight = qkv_ref[...]
-    lane_head = lax.broadcasted_iota(jnp.int32, (width, width), 0) // HEAD_DIM
-    group = (lane_head == lax.broadcasted_iota(jnp.int32, (width, width), 1) // HEAD_DIM).astype(BF16)
+    group = head_group(width)
 
     def row_in(count):
         return lax.broadcasted_iota(jnp.int32, (count, 1), 0) & (SPAN - 1)
@@ -88,22 +122,23 @@
         values = dot(normed, weight[:, 2 * width :])
         key_ref[start : start + cells.shape[0]] = keys.astype(BF16)
         value_ref[start : start + cells.shape[0]] = values.astype(BF16)
-        return unit, reciprocal, normed, keys, key_recip
+        return normed
 
     def queries_of(normed):
         return head_norm(dot(normed, weight[:, :width]), group)
 
-    unit, reciprocal, normed, keys, key_recip = keys_of(own_ref[...], strip)
-    queries, query_recip = queries_of(normed)
-    west_normed = keys_of(west[:strip], 0)[2]
-    east_normed = keys_of(east[:strip], strip + own_count)[2]
+    key_ref[strip : strip + own_count] = own_key_b_ref[...]
+    value_ref[strip : strip + own_count] = own_value_b_ref[...]
+    queries = own_query_ref[...]
+    west_normed = keys_of(west[:strip], 0)
+    east_normed = keys_of(east[:strip], strip + own_count)
     band = BAND * SPAN
     west_query = queries_of(west_normed[strip - band :])[0]
     east_query = queries_of(east_normed[:band])[0]
 
     own_grad = own_grad_ref[...]
     out_weight = out_ref[...]
-    own_up = dot(own_grad, out_weight, 1, 1)
+    own_up = own_up_ref[...]
     west_up = dot(west[strip:], out_weight, 1, 1)
     east_up = dot(east[strip:], out_weight, 1, 1)
     empty = jnp.zeros((SPAN, width), F32)
@@ -132,9 +167,14 @@
     inside = (col_gap >= 0) & (col_gap <= REACH) & (row_gap <= REACH)
     bias = jnp.where(inside, 0.0, LOWEST)
     bias = jnp.concatenate([bias] * HEADS, axis=1)
+    head_factor = factor_ref[:1]
     factor = jnp.concatenate(
-        [jnp.full((1, band), scale_ref[head] * (1.0 / HEAD_DIM), F32) for head in range(HEADS)], axis=1
-    )
+        [
+            jnp.broadcast_to(head_factor[:, head * HEAD_DIM : head * HEAD_DIM + 1], (1, band))
+            for head in range(HEADS)
+        ],
+        axis=1,
+    ) * math.log2(math.e)
 
     def merge(stacked):
         half = width // 2
@@ -161,11 +201,11 @@
         key_band = key_ref[lower:upper]
         value_band = value_ref[lower:upper]
         scores = dot(key_band, query_big, 1, 1) * factor + bias[lower - first : upper - first]
-        exponent = jnp.exp(scores - jnp.max(scores, axis=0, keepdims=True))
+        exponent = jnp.exp2(scores - jnp.max(scores, axis=0, keepdims=True))
         prob = exponent * (1.0 / jnp.sum(exponent, axis=0, keepdims=True))
         dots = dot(value_band, up_big, 1, 1)
         mean_dot = jnp.sum(prob * dots, axis=0, keepdims=True)
-        weighted = (prob * (dots - mean_dot) * factor).astype(BF16)
+        weighted = (prob * (dots - mean_dot)).astype(BF16)
         prob = prob.astype(BF16)
         near, far = max(lower, strip), min(upper, own_end)
         key_grad_ref[near - strip : far - strip] += dot(weighted[near - lower : far - lower], query_big)
@@ -177,9 +217,9 @@
     row = row_in(own_count)
     own_rows = row < 16
     key_rows = own_rows | (top & (row >= SPAN - RADIUS)) | (bottom & (row >= 16) & (row < 16 + RADIUS))
-    query_grad = jnp.concatenate(query_grads, axis=0)
-    raw_query = head_back(query_grad, queries, query_recip, group)
-    raw_key = head_back(key_grad_ref[...], keys, key_recip, group)
+    query_grad = jnp.concatenate(query_grads, axis=0) * head_factor
+    raw_query = head_back(query_grad, queries, own_query_recip_ref[...], group)
+    raw_key = head_back(key_grad_ref[...] * head_factor, own_key_ref[...], own_key_recip_ref[...], group)
     projected_grad = jnp.concatenate(
         [
             jnp.where(own_rows, raw_query, 0.0),
@@ -188,6 +228,8 @@
         ],
         axis=1,
     ).astype(BF16)
+    unit, normed = own_unit_ref[...], own_normed_ref[...]
+    reciprocal = own_scale_ref[:, :1]
     normed_grad = dot(projected_grad, weight, 1, 1)
     gain_grad = jnp.sum(normed_grad * unit, axis=0, keepdims=True)
     scaled = normed_grad * gain
@@ -263,7 +305,8 @@
         ],
         axis=0,
     )
-    strips = lax.all_gather(strips, ROWS, axis=0).transpose(0, 2, 1, 3)
+    strips, edge_tokens = lax.optimization_barrier((lax.all_gather(strips, ROWS, axis=0), edge_tokens))
+    strips = strips.transpose(0, 2, 1, 3)
     above = strips[jnp.maximum(place - 1, 0)]
     below = strips[jnp.minimum(place + 1, row_devices - 1)]
     own = tokens.transpose(1, 0, 2)
@@ -306,13 +349,42 @@
     group = col_devices // lines
     whole = pl.BlockSpec(memory_space=pltpu.VMEM)
     scalars = pl.BlockSpec(memory_space=pltpu.SMEM)
+    even, slab, grad_slab = lax.optimization_barrier((even, slab, grad_slab))
+    wide = jax.ShapeDtypeStruct((cells, width), F32)
+    narrow = jax.ShapeDtypeStruct((cells, width), BF16)
+    own_parts = pl.pallas_call(
+        own_kernel,
+        out_shape=(
+            jax.ShapeDtypeStruct((8, width), F32),
+            wide,
+            jax.ShapeDtypeStruct((cells, LANES), F32),
+            narrow,
+            wide,
+            wide,
+            narrow,
+            narrow,
+            wide,
+            wide,
+            wide,
+        ),
+        in_specs=[whole] * 6,
+        out_specs=(whole,) * 11,
+        compiler_params=pltpu.CompilerParams(vmem_limit_bytes=16 * 2**20),
+    )(
+        head_scale[None, :],
+        slab.reshape(cells, width),
+        grad_slab.reshape(cells, width),
+        norm_gain[None, :],
+        qkv_weight,
+        out_weight,
+    )
     token_grad, chunks = pl.pallas_call(
         block_kernel,
         out_shape=(
             jax.ShapeDtypeStruct((cells, width), BF16),
             jax.ShapeDtypeStruct((2 * lines, 8 * group + TAIL, LANES), BF16),
         ),
-        in_specs=[scalars, scalars] + [whole] * 7,
+        in_specs=[scalars] + [whole] * 17,
         out_specs=(whole,) * 2,
         scratch_shapes=[
             pltpu.VMEM((cells + 2 * REACH * SPAN, width), BF16),
@@ -325,14 +397,13 @@
         compiler_params=pltpu.CompilerParams(vmem_limit_bytes=40 * 2**20),
     )(
         jnp.stack([place, row_devices, parity]).astype(jnp.int32),
-        head_scale,
-        slab.reshape(cells, width),
         grad_slab.reshape(cells, width),
         odd.reshape(-1, width),
         even.reshape(2, -1, width),
         norm_gain[None, :],
         qkv_weight,
         out_weight,
+        *own_parts,
     )
     token_grad = token_grad.reshape(col_count, SPAN, width)[:, :row_count].transpose(1, 0, 2)
     chunks = lax.all_to_all(chunks, ("x", "c"), 0, 0)
@@ -343,6 +414,7 @@
         in_specs=[whole],
         out_specs=whole,
         scratch_shapes=[pltpu.VMEM((8 * group, LANES), F32)],
+        compiler_params=pltpu.CompilerParams(vmem_limit_bytes=8 * 2**20),
     )(chunks)
     part = jnp.sum(lax.all_to_all(part, ("l", "y", "h"), 0, 0).astype(F32), axis=0)
     qkv_grad, proj_grad, gain_grad = pl.pallas_call(
@@ -354,6 +426,7 @@
         ),
         in_specs=[scalars, whole],
         out_specs=(whole,) * 3,
+        compiler_params=pltpu.CompilerParams(vmem_limit_bytes=4 * 2**20),
     )(lax.axis_index(COLS)[None].astype(jnp.int32), lax.all_gather(part, "c", axis=0, tiled=True))
     return token_grad, qkv_grad.T, proj_grad.T, gain_grad.reshape(2)
 

time: 84.3 us -> 80.9 us (0.960)
  Pallas kernels: 8.18 us -> 6.56 us
    pallas_call x1, Pallas kernels: 1.92 us -> 0.85 us  [on_device(): pl.pallas_call(middle_kernel, out_shape=jax.ShapeDtypeStruct((halves * gr...]
    unnamed x18 -> x17, local copies, waits for them, and re-layouts: 2.76 us -> 2.22 us
  transfers between devices with their start and end apart: 2 -> 2, of which waited for: 1 -> 1; matrix products, arithmetic and copies ran while one was open for 1% -> 1% of each run, Pallas kernels for 0% -> 1%
where the time goes in v5:
time: 80.9 us; the launch traced here: 80.5 us
  blocking collectives  40.4 us (50%)
  starting transfers between devices  16.1 us (20%)
  waiting for transfers between devices  12.8 us (16%)
  Pallas kernels  6.56 us (8%)
  local copies, waits for them, and re-layouts  3.39 us (4%)
  between operations  0.85 us (1%)
    all_gather x1, blocking collectives, on_device(): lax.all_gather(strips, ROWS, axis=0)  16.5 us
    all_to_all x1, blocking collectives, on_device(): chunks = lax.all_to_all(chunks, ('x', 'c'), 0, 0)  13.8 us
    all_to_all x1, waiting for transfers between devices, on_device(): lax.all_to_all(part, ('l', 'y', 'h'), 0, 0).astype(F32)  12.8 us
    ppermute x1, starting transfers between devices, on_device(): lax.ppermute(jnp.where(parity == 0, facing_west, facing_east), COLS, pair...  8.3 us
    all_to_all x1, starting transfers between devices, on_device(): lax.all_to_all(part, ('l', 'y', 'h'), 0, 0).astype(F32)  7.75 us
    all_gather x1, blocking collectives, on_device(): lax.all_gather(jnp.where(parity == 0, facing_east, facing_west), COLS, ax...  5.79 us
    pallas_call x1, Pallas kernels, on_device(): pl.pallas_call(block_kernel, out_shape=(jax.ShapeDtypeStruct((cells, widt...  4.49 us
    all_gather x1, blocking collectives, on_device(): lax.all_gather(part, 'c', axis=0, tiled=True)  4.25 us
  transfers between devices with their start and end apart: 2, of which 1 were waited for; matrix products, arithmetic and copies ran while one was open for 1% of the time, Pallas kernels for 1%

profile of v5, /device:TPU:1, one launch (start us, length us, event | category | flops | bytes accessed | tf_op | source)
XLA Modules:
  0.0 80.5 jit_solution(12352600876273145186)
XLA Ops:
  0.6 0.0 copy-start.4
  0.6 0.8 fusion.2
  1.4 0.0 copy-done.4
  1.5 0.8 %copy-done.5 = bf16[16,8,256]{2,1,0:T(8,128)(2,1)S(1)} copy-done((bf16[16,8,256]{2,1,0:T(8,128)(2,1)S(1)}, bf16[16,8,256]{2,1,0:T(8,128)(2,1)}, u32[]{:S(2)}) %copy-start.5) | copy-done | bytes 65560
  2.4 0.1 pad.16.clone
  2.4 0.1 pad.12.clone
  2.5 0.0 copy-start.6
  2.6 16.5 %all-gather = bf16[72,8,256]{2,1,0:T(8,128)(2,1)S(1)} all-gather(bf16[18,8,256]{2,1,0:T(8,128)(2,1)S(1)} %pad_maximum_fusion.2), channel_id=2, replica_groups=mesh['x'=4,'l'=4,'y'=8,'h'=2,'c'=2] {'h','c'}, dimensions={0}, use_global_device_ids=true | all-gather | bytes 368640 | tf_op jit(solution)/shard_map/all_gather | solution.py:308
  19.1 0.0 copy-done.6
  19.1 0.1 copy.18
  19.3 0.1 pad_maximum_fusion.1
  19.4 0.1 pad_maximum_fusion
  19.6 8.3 %collective-permute-start = (bf16[9,32,256]{2,1,0:T(8,128)(2,1)S(1)}, bf16[9,32,256]{2,1,0:T(8,128)(2,1)S(1)}, u32[]{:S(2)}, u32[]{:S(2)}) collective-permute-start(bf16[9,32,256]{2,1,0:T(8,128)(2,1)S(1)} %maximum_select_fusion.1), channel_id=1, source_target_pairs={{4,8},{12,16},{20,24},{28,32},{36,40},{44,48},{52,56},{60,64},{68,... | collective-permute-start | bytes 442376 | tf_op jit(solution)/shard_map/ppermute | solution.py:338
  27.9 0.0 copy-start
  27.9 0.0 copy-start.1
  28.0 5.8 %all_gather.15 = bf16[2,9,32,256]{3,2,1,0:T(8,128)(2,1)S(1)} all-gather(bf16[1,9,32,256]{3,2,1,0:T(8,128)(2,1)S(1)} %maximum_select_fusion), channel_id=1, replica_groups={{0,4},{8,12},{16,20},{24,28},{32,36},{40,44},{48,52},{56,60},{64,68},{7..., dimensions={0}, use_global_device_ids=true | all-gather | bytes 442368 | tf_op jit(solution)/shard_map/all_gather | solution.py:341
  33.7 0.0 copy-done
  33.8 0.0 copy-done.1
  33.8 0.7 copy-done.2
  34.4 0.0 copy-done.3
  34.4 0.6 shard_map.102
  35.0 0.1 pad_add_fusion.place_ref
  35.1 0.0 collective-permute-done
  35.1 4.5 %shard_map.103 = (bf16[256,256]{1,0:T(8,128)(2,1)S(1)}, bf16[8,272,128]{2,1,0:T(8,128)(2,1)S(1)}) custom-call(s32[3]{0:T(128)S(1)} %pad_add_fusion.place_ref, bf16[256,256]{1,0:T(8,128)(2,1)S(1)} %bitcast.47, bf16[288,256]{1,0:T(8,128)(2,1)S(1)} %bitcast.50, bf16[2,288,256]{2,1,0:T(8,128)(2,1)S(1)} %bitcast.49, f32[1,256]{1,0:T(1,128)S(1)} %bitcast.53, ...), custom_call_target="tpu_custom_call" | custom-call | tf_op jit(solution)/shard_map/pallas_call | solution.py:381
  39.6 13.8 %all_to_all.10.chunk_ref = bf16[8,272,128]{2,1,0:T(8,128)(2,1)S(1)} all-to-all(bf16[8,272,128]{2,1,0:T(8,128)(2,1)S(1)} %get-tuple-element.42), channel_id=1, replica_groups=mesh['x'=4,'l'=4,'y'=8,'h'=2,'c'=2] {'x','c'}, dimensions={0} | all-to-all | bytes 1114112 | tf_op jit(solution)/shard_map/all_to_all | solution.py:409
  53.4 0.9 %shard_map.104 = bf16[64,16,128]{2,1,0:T(8,128)(2,1)} custom-call(bf16[8,272,128]{2,1,0:T(8,128)(2,1)S(1)} %all_to_all.10.chunk_ref), custom_call_target="tpu_custom_call" | custom-call | tf_op jit(solution)/shard_map/pallas_call | solution.py:411
  54.3 7.7 %all-to-all-start.1 = ((bf16[64,16,128]{2,1,0:T(8,128)(2,1)}), bf16[64,16,128]{2,1,0:T(8,128)(2,1)S(1)}, u32[]{:S(2)}, u32[]{:S(2)}) async-start(bf16[64,16,128]{2,1,0:T(8,128)(2,1)} %shard_map.104), calls=%async_computation.1 | async-start | bytes 524288 | tf_op jit(solution)/shard_map/all_to_all | solution.py:419
  62.1 0.7 copy.27
  62.7 12.8 %all-to-all-done.1 = bf16[64,16,128]{2,1,0:T(8,128)(2,1)S(1)} async-done(((bf16[64,16,128]{2,1,0:T(8,128)(2,1)}), bf16[64,16,128]{2,1,0:T(8,128)(2,1)S(1)}, u32[]{:S(2)}, u32[]{:S(2)}) %all-to-all-start.1) | async-done | bytes 262176 | tf_op jit(solution)/shard_map/all_to_all | solution.py:419
  75.5 0.1 convert_reduce_fusion
  75.6 4.3 %all_gather.16.parts_ref = f32[32,128]{1,0:T(8,128)S(1)} all-gather(f32[16,128]{1,0:T(8,128)S(1)} %convert_reduce_fusion), channel_id=1, replica_groups=mesh['x'=4,'l'=4,'y'=8,'h'=2,'c'=2] {'c'}, dimensions={0}, use_global_device_ids=true | all-gather | bytes 24576 | tf_op jit(solution)/shard_map/all_gather | solution.py:430
  79.9 0.6 shard_map.105
  (20 shorter events, 0.3 us)
Async XLA Ops:
  0.6 0.8 %copy-start.4 = (bf16[16,8,256]{2,1,0:T(8,128)(2,1)S(1)}, bf16[16,8,256]{2,1,0:T(8,128)(2,1)}, u32[]{:S(2)}) copy-start(bf16[16,8,256]{2,1,0:T(8,128)(2,1)} %param.7) | copy-start | bytes 196612
  1.5 0.8 %copy-start.5 = (bf16[16,8,256]{2,1,0:T(8,128)(2,1)S(1)}, bf16[16,8,256]{2,1,0:T(8,128)(2,1)}, u32[]{:S(2)}) copy-start(bf16[16,8,256]{2,1,0:T(8,128)(2,1)} %param.9) | copy-start | bytes 196612
  2.5 16.5 %copy-start.6 = (bf16[2,3,8,256]{3,2,1,0:T(8,128)(2,1)S(1)}, bf16[2,3,8,256]{3,2,1,0:T(8,128)(2,1)}, u32[]{:S(2)}) copy-start(bf16[2,3,8,256]{3,2,1,0:T(8,128)(2,1)} %param.8) | copy-start | bytes 73732
  19.6 15.5 %collective-permute-start = (bf16[9,32,256]{2,1,0:T(8,128)(2,1)S(1)}, bf16[9,32,256]{2,1,0:T(8,128)(2,1)S(1)}, u32[]{:S(2)}, u32[]{:S(2)}) collective-permute-start(bf16[9,32,256]{2,1,0:T(8,128)(2,1)S(1)} %maximum_select_fusion.1), channel_id=1, source_target_pairs={{4,8},{12,16},{20,24},{28,32},{36,40},{44,48},{52,56},{60,64},{68,... | collective-permute-start | bytes 442376 | tf_op jit(solution)/shard_map/ppermute | solution.py:338
  27.9 5.9 %copy-start = (bf16[256,768]{1,0:T(8,128)(2,1)S(1)}, bf16[256,768]{1,0:T(8,128)(2,1)}, u32[]{:S(2)}) copy-start(bf16[256,768]{1,0:T(8,128)(2,1)} %qkv_ref.3) | copy-start | bytes 1179652
  27.9 5.8 %copy-start.1 = (bf16[256,256]{1,0:T(8,128)(2,1)S(1)}, bf16[256,256]{1,0:T(8,128)(2,1)}, u32[]{:S(2)}) copy-start(bf16[256,256]{1,0:T(8,128)(2,1)} %out_ref.3) | copy-start | bytes 393220
  33.7 0.7 copy-start.2
  33.7 0.7 copy-start.3
  54.3 21.2 %all-to-all-start.1 = ((bf16[64,16,128]{2,1,0:T(8,128)(2,1)}), bf16[64,16,128]{2,1,0:T(8,128)(2,1)S(1)}, u32[]{:S(2)}, u32[]{:S(2)}) async-start(bf16[64,16,128]{2,1,0:T(8,128)(2,1)} %shard_map.104), calls=%async_computation.1 | async-start | bytes 524288 | tf_op jit(solution)/shard_map/all_to_all | solution.py:419

commit v6 on v5

--- a/solution.py
+++ b/solution.py
@@ -18,9 +18,9 @@
 BAND = 4
 LANES = 128
 TAIL = 16
-COLS = ("x", "l", "y")
+COLS = ("x", "l", "u", "v")
 ROWS = ("h", "c")
-SPLIT = (4, 4, 8)
+SPLIT = (4, 4, 4, 2)
 LOWEST = -1e30
 F32 = jnp.float32
 BF16 = jnp.bfloat16
@@ -87,6 +87,7 @@
 
 
 def block_kernel(
+    lowers,
     place_ref, own_grad_ref, odd_ref, even_ref, gain_ref, qkv_ref, out_ref,
     factor_ref, own_unit_ref, own_scale_ref, own_normed_ref, own_key_ref, own_key_recip_ref, own_key_b_ref, own_value_b_ref,
     own_query_ref, own_query_recip_ref, own_up_ref,
@@ -242,21 +243,21 @@
         at = slice(block * LANES, (block + 1) * LANES)
         weight_grad_ref[block] = weight_grad[:, at]
         proj_grad_ref[block] = proj_grad[:, at]
-    blocks, rows = chunk_ref.shape[:2]
+    peers, rows = chunk_ref.shape[:2]
     group = (rows - TAIL) // 8
-    for peer in range(blocks):
-        line, side = peer // 2, peer % 2
+    for peer in range(peers):
+        line, lower, side = peer // (2 * lowers), peer // 2 % lowers, peer % 2
+        column = line * group * lowers + lower
         for part in range(4):
             for block in range(width // LANES):
                 if part < 3:
-                    start = 6 * group * line + 3 * side + part
-                    cells = weight_grad_ref.at[block][pl.ds(start, group, stride=6), :]
+                    cells_ref, start, stride = weight_grad_ref, 6 * column + 3 * side + part, 6 * lowers
                 else:
-                    start = 2 * group * line + side
-                    cells = proj_grad_ref.at[block][pl.ds(start, group, stride=2), :]
+                    cells_ref, start, stride = proj_grad_ref, 2 * column + side, 2 * lowers
                 at = (2 * part + block) * group
+                cells = cells_ref.at[block][pl.ds(start, group, stride=stride), :]
                 chunk_ref[peer, at : at + group] = cells.astype(BF16)
-        lanes = gain_grad[:, 2 * group * line // LANES * LANES :][:, :LANES]
+        lanes = gain_grad[:, 2 * column // LANES * LANES :][:, :LANES]
         chunk_ref[peer, rows - TAIL :] = jnp.broadcast_to(lanes, (TAIL, LANES)).astype(BF16)
 
 
@@ -345,8 +346,9 @@
         axis_index_groups=[[i, i + 1] for i in range(0, col_devices, 2)],
     )
     cells = col_count * SPAN
-    lines = lax.axis_size("x")
-    group = col_devices // lines
+    lowers = lax.axis_size("v")
+    peers = 2 * lax.axis_size("x") * lowers
+    group = 2 * col_devices // peers
     whole = pl.BlockSpec(memory_space=pltpu.VMEM)
     scalars = pl.BlockSpec(memory_space=pltpu.SMEM)
     even, slab, grad_slab = lax.optimization_barrier((even, slab, grad_slab))
@@ -379,10 +381,10 @@
         out_weight,
     )
     token_grad, chunks = pl.pallas_call(
-        block_kernel,
+        functools.partial(block_kernel, lowers),
         out_shape=(
             jax.ShapeDtypeStruct((cells, width), BF16),
-            jax.ShapeDtypeStruct((2 * lines, 8 * group + TAIL, LANES), BF16),
+            jax.ShapeDtypeStruct((peers, 8 * group + TAIL, LANES), BF16),
         ),
         in_specs=[scalars] + [whole] * 17,
         out_specs=(whole,) * 2,
@@ -406,7 +408,7 @@
         *own_parts,
     )
     token_grad = token_grad.reshape(col_count, SPAN, width)[:, :row_count].transpose(1, 0, 2)
-    chunks = lax.all_to_all(chunks, ("x", "c"), 0, 0)
+    chunks = lax.all_to_all(chunks, ("x", "v", "c"), 0, 0)
     halves = lax.axis_size("h")
     part = pl.pallas_call(
         middle_kernel,
@@ -416,7 +418,7 @@
         scratch_shapes=[pltpu.VMEM((8 * group, LANES), F32)],
         compiler_params=pltpu.CompilerParams(vmem_limit_bytes=8 * 2**20),
     )(chunks)
-    part = jnp.sum(lax.all_to_all(part, ("l", "y", "h"), 0, 0).astype(F32), axis=0)
+    part = jnp.sum(lax.all_to_all(part, ("l", "u", "h"), 0, 0).astype(F32), axis=0)
     qkv_grad, proj_grad, gain_grad = pl.pallas_call(
         functools.partial(final_kernel, grad_scale),
         out_shape=(

time: 80.9 us -> 78.8 us (0.974)
  waiting for transfers between devices: 12.8 us -> 10.5 us
    all_to_all x1, waiting for transfers between devices: 12.8 us -> 10.5 us  [on_device(): lax.all_to_all(part, ('l', 'u', 'h'), 0, 0).astype(F32)]
    all_to_all x1, blocking collectives: 13.8 us -> 15 us  [on_device(): chunks = lax.all_to_all(chunks, ('x', 'v', 'c'), 0, 0)]
where the time goes in v6:
time: 78.8 us; the launch traced here: 78.4 us
  blocking collectives  40.9 us (52%)
  starting transfers between devices  15.9 us (20%)
  waiting for transfers between devices  10.5 us (13%)
  Pallas kernels  6.45 us (8%)
  local copies, waits for them, and re-layouts  3.39 us (4%)
  between operations  0.85 us (1%)
    all_gather x1, blocking collectives, on_device(): lax.all_gather(strips, ROWS, axis=0)  16.5 us
    all_to_all x1, blocking collectives, on_device(): chunks = lax.all_to_all(chunks, ('x', 'v', 'c'), 0, 0)  15 us
    all_to_all x1, waiting for transfers between devices, on_device(): lax.all_to_all(part, ('l', 'u', 'h'), 0, 0).astype(F32)  10.5 us
    ppermute x1, starting transfers between devices, on_device(): lax.ppermute(jnp.where(parity == 0, facing_west, facing_east), COLS, pair...  8.3 us
    all_to_all x1, starting transfers between devices, on_device(): lax.all_to_all(part, ('l', 'u', 'h'), 0, 0).astype(F32)  7.59 us
    all_gather x1, blocking collectives, on_device(): lax.all_gather(jnp.where(parity == 0, facing_east, facing_west), COLS, ax...  5.79 us
    pallas_call x1, Pallas kernels, on_device(): pl.pallas_call(functools.partial(block_kernel, lowers), out_shape=(jax.Sh...  4.48 us
    all_gather x1, blocking collectives, on_device(): lax.all_gather(part, 'c', axis=0, tiled=True)  3.59 us
  transfers between devices with their start and end apart: 2, of which 1 were waited for; matrix products, arithmetic and copies ran while one was open for 1% of the time, Pallas kernels for 1%

profile of v6, /device:TPU:1, one launch (start us, length us, event | category | flops | bytes accessed | tf_op | source)
XLA Modules:
  0.0 78.4 jit_solution(5954815052299010954)
XLA Ops:
  0.6 0.0 copy-start.4
  0.6 0.8 %fusion.2 = (bf16[6,8,256]{2,1,0:T(8,128)(2,1)S(1)}, bf16[6,8,256]{2,1,0:T(8,128)(2,1)S(1)}) fusion(bf16[16,8,256]{2,1,0:T(8,128)(2,1)} %param.7), kind=kLoop, calls=%fused_computation.23 | loop fusion | bytes 98304 | tf_op jit(solution)/shard_map/slice | solution.py:302
  1.4 0.0 copy-done.4
  1.5 0.0 copy-start.5
  1.5 0.8 %copy-done.5 = bf16[16,8,256]{2,1,0:T(8,128)(2,1)S(1)} copy-done((bf16[16,8,256]{2,1,0:T(8,128)(2,1)S(1)}, bf16[16,8,256]{2,1,0:T(8,128)(2,1)}, u32[]{:S(2)}) %copy-start.5) | copy-done | bytes 65560
  2.4 0.1 pad.16.clone
  2.5 0.1 pad.12.clone
  2.5 0.0 copy-start.6
  2.6 16.5 %all-gather = bf16[72,8,256]{2,1,0:T(8,128)(2,1)S(1)} all-gather(bf16[18,8,256]{2,1,0:T(8,128)(2,1)S(1)} %pad_maximum_fusion.2), channel_id=2, replica_groups=mesh['x'=4,'l'=4,'u'=4,'v'=2,'h'=2,'c'=2] {'h','c'}, dimensions={0}, use_global_device_ids=true | all-gather | bytes 368640 | tf_op jit(solution)/shard_map/all_gather | solution.py:309
  19.1 0.0 copy-done.6
  19.1 0.1 copy.18
  19.3 0.1 pad_maximum_fusion.1
  19.4 0.1 pad_maximum_fusion
  19.6 8.3 %collective-permute-start = (bf16[9,32,256]{2,1,0:T(8,128)(2,1)S(1)}, bf16[9,32,256]{2,1,0:T(8,128)(2,1)S(1)}, u32[]{:S(2)}, u32[]{:S(2)}) collective-permute-start(bf16[9,32,256]{2,1,0:T(8,128)(2,1)S(1)} %maximum_select_fusion.1), channel_id=1, source_target_pairs={{4,8},{12,16},{20,24},{28,32},{36,40},{44,48},{52,56},{60,64},{68,... | collective-permute-start | bytes 442376 | tf_op jit(solution)/shard_map/ppermute | solution.py:339
  27.9 0.0 copy-start
  27.9 0.0 copy-start.1
  28.0 5.8 %all_gather.15 = bf16[2,9,32,256]{3,2,1,0:T(8,128)(2,1)S(1)} all-gather(bf16[1,9,32,256]{3,2,1,0:T(8,128)(2,1)S(1)} %maximum_select_fusion), channel_id=1, replica_groups={{0,4},{8,12},{16,20},{24,28},{32,36},{40,44},{48,52},{56,60},{64,68},{7..., dimensions={0}, use_global_device_ids=true | all-gather | bytes 442368 | tf_op jit(solution)/shard_map/all_gather | solution.py:342
  33.7 0.0 copy-done
  33.8 0.0 copy-done.1
  33.8 0.7 copy-done.2
  34.4 0.0 copy-done.3
  34.4 0.6 shard_map.102
  35.0 0.1 pad_add_fusion.place_ref
  35.1 0.0 collective-permute-done
  35.1 4.5 %shard_map.103 = (bf16[256,256]{1,0:T(8,128)(2,1)S(1)}, bf16[16,144,128]{2,1,0:T(8,128)(2,1)S(1)}) custom-call(s32[3]{0:T(128)S(1)} %pad_add_fusion.place_ref, bf16[256,256]{1,0:T(8,128)(2,1)S(1)} %bitcast.47, bf16[288,256]{1,0:T(8,128)(2,1)S(1)} %bitcast.50, bf16[2,288,256]{2,1,0:T(8,128)(2,1)S(1)} %bitcast.49, f32[1,256]{1,0:T(1,128)S(1)} %bitcast.53, ...), custom_call_target="tpu_custom_call" | custom-call | tf_op jit(solution)/shard_map/pallas_call | solution.py:383
  39.6 15.0 %all_to_all.10.chunk_ref = bf16[16,144,128]{2,1,0:T(8,128)(2,1)S(1)} all-to-all(bf16[16,144,128]{2,1,0:T(8,128)(2,1)S(1)} %get-tuple-element.42), channel_id=1, replica_groups=mesh['x'=4,'l'=4,'u'=4,'v'=2,'h'=2,'c'=2] {'x','v','c'}, dimensions={0} | all-to-all | bytes 1179648 | tf_op jit(solution)/shard_map/all_to_all | solution.py:411
  54.6 0.8 shard_map.104
  55.4 7.6 %all-to-all-start.1 = ((bf16[32,16,128]{2,1,0:T(8,128)(2,1)}), bf16[32,16,128]{2,1,0:T(8,128)(2,1)S(1)}, u32[]{:S(2)}, u32[]{:S(2)}) async-start(bf16[32,16,128]{2,1,0:T(8,128)(2,1)} %shard_map.104), calls=%async_computation.1 | async-start | bytes 262144 | tf_op jit(solution)/shard_map/all_to_all | solution.py:421
  63.0 0.7 copy.27
  63.6 10.5 %all-to-all-done.1 = bf16[32,16,128]{2,1,0:T(8,128)(2,1)S(1)} async-done(((bf16[32,16,128]{2,1,0:T(8,128)(2,1)}), bf16[32,16,128]{2,1,0:T(8,128)(2,1)S(1)}, u32[]{:S(2)}, u32[]{:S(2)}) %all-to-all-start.1) | async-done | bytes 131104 | tf_op jit(solution)/shard_map/all_to_all | solution.py:421
  74.2 3.6 %all_gather.16.parts_ref = f32[32,128]{1,0:T(8,128)S(1)} all-gather(f32[16,128]{1,0:T(8,128)S(1)} %convert_reduce_fusion), channel_id=1, replica_groups=mesh['x'=4,'l'=4,'u'=4,'v'=2,'h'=2,'c'=2] {'c'}, dimensions={0}, use_global_device_ids=true | all-gather | bytes 24576 | tf_op jit(solution)/shard_map/all_gather | solution.py:432
  77.8 0.6 shard_map.105
  (20 shorter events, 0.3 us)
Async XLA Ops:
  0.6 0.8 %copy-start.4 = (bf16[16,8,256]{2,1,0:T(8,128)(2,1)S(1)}, bf16[16,8,256]{2,1,0:T(8,128)(2,1)}, u32[]{:S(2)}) copy-start(bf16[16,8,256]{2,1,0:T(8,128)(2,1)} %param.7) | copy-start | bytes 196612
  1.5 0.8 %copy-start.5 = (bf16[16,8,256]{2,1,0:T(8,128)(2,1)S(1)}, bf16[16,8,256]{2,1,0:T(8,128)(2,1)}, u32[]{:S(2)}) copy-start(bf16[16,8,256]{2,1,0:T(8,128)(2,1)} %param.9) | copy-start | bytes 196612
  2.5 16.5 %copy-start.6 = (bf16[2,3,8,256]{3,2,1,0:T(8,128)(2,1)S(1)}, bf16[2,3,8,256]{3,2,1,0:T(8,128)(2,1)}, u32[]{:S(2)}) copy-start(bf16[2,3,8,256]{3,2,1,0:T(8,128)(2,1)} %param.8) | copy-start | bytes 73732
  19.6 15.5 %collective-permute-start = (bf16[9,32,256]{2,1,0:T(8,128)(2,1)S(1)}, bf16[9,32,256]{2,1,0:T(8,128)(2,1)S(1)}, u32[]{:S(2)}, u32[]{:S(2)}) collective-permute-start(bf16[9,32,256]{2,1,0:T(8,128)(2,1)S(1)} %maximum_select_fusion.1), channel_id=1, source_target_pairs={{4,8},{12,16},{20,24},{28,32},{36,40},{44,48},{52,56},{60,64},{68,... | collective-permute-start | bytes 442376 | tf_op jit(solution)/shard_map/ppermute | solution.py:339
  27.9 5.9 %copy-start = (bf16[256,768]{1,0:T(8,128)(2,1)S(1)}, bf16[256,768]{1,0:T(8,128)(2,1)}, u32[]{:S(2)}) copy-start(bf16[256,768]{1,0:T(8,128)(2,1)} %qkv_ref.3) | copy-start | bytes 1179652
  27.9 5.8 %copy-start.1 = (bf16[256,256]{1,0:T(8,128)(2,1)S(1)}, bf16[256,256]{1,0:T(8,128)(2,1)}, u32[]{:S(2)}) copy-start(bf16[256,256]{1,0:T(8,128)(2,1)} %out_ref.3) | copy-start | bytes 393220
  33.7 0.7 copy-start.2
  33.7 0.7 copy-start.3
  55.4 18.8 %all-to-all-start.1 = ((bf16[32,16,128]{2,1,0:T(8,128)(2,1)}), bf16[32,16,128]{2,1,0:T(8,128)(2,1)S(1)}, u32[]{:S(2)}, u32[]{:S(2)}) async-start(bf16[32,16,128]{2,1,0:T(8,128)(2,1)} %shard_map.104), calls=%async_computation.1 | async-start | bytes 262144 | tf_op jit(solution)/shard_map/all_to_all | solution.py:421

commit v7 on v6

--- a/solution.py
+++ b/solution.py
@@ -38,6 +38,13 @@
     return (dot(high, group) + dot(low, group)) * (1.0 / HEAD_DIM)
 
 
+def high_low(values, count, first):
+    high = values.astype(BF16).astype(F32)
+    row = lax.broadcasted_iota(jnp.int32, (count, values.shape[1]), 0)
+    low = jnp.where(row == first + 1, values - high, 0.0)
+    return jnp.where(row == first, high, low).astype(BF16)
+
+
 def unit_norm(cells):
     rows = cells.astype(F32)
     reciprocal = lax.rsqrt(jnp.mean(rows * rows, axis=-1, keepdims=True) + EPSILON)
@@ -59,19 +66,14 @@
 
 
 def own_kernel(
-    head_ref, own_ref, own_grad_ref, gain_ref, qkv_ref, out_ref,
-    factor_ref, unit_ref, scale_ref, normed_ref, key_ref, key_recip_ref, key_b_ref, value_b_ref, query_ref, query_recip_ref, up_ref,
+    own_ref, own_grad_ref, gain_ref, qkv_ref, out_ref,
+    unit_ref, scale_ref, normed_ref, key_ref, key_recip_ref, key_b_ref, value_b_ref, query_ref, query_recip_ref, up_ref,
 ):
     width = own_ref.shape[1]
-    lane = lax.broadcasted_iota(jnp.int32, (1, width), 1) // HEAD_DIM
-    factor_ref[...] = jnp.zeros_like(factor_ref)
-    for head in range(HEADS):
-        factor = jnp.broadcast_to(head_ref[:, head : head + 1] * (1.0 / HEAD_DIM), (1, width))
-        factor_ref[:1] = jnp.where(lane == head, factor, factor_ref[:1])
     weight = qkv_ref[...]
     group = head_group(width)
     unit, reciprocal = unit_norm(own_ref[...])
-    normed = (unit * gain_ref[...]).astype(BF16)
+    normed = (unit * gain_ref[:, :width]).astype(BF16)
     keys, key_recip = head_norm(dot(normed, weight[:, width : 2 * width]), group)
     queries, query_recip = head_norm(dot(normed, weight[:, :width]), group)
     unit_ref[...] = unit
@@ -89,7 +91,7 @@
 def block_kernel(
     lowers,
     place_ref, own_grad_ref, odd_ref, even_ref, gain_ref, qkv_ref, out_ref,
-    factor_ref, own_unit_ref, own_scale_ref, own_normed_ref, own_key_ref, own_key_recip_ref, own_key_b_ref, own_value_b_ref,
+    own_unit_ref, own_scale_ref, own_normed_ref, own_key_ref, own_key_recip_ref, own_key_b_ref, own_value_b_ref,
     own_query_ref, own_query_recip_ref, own_up_ref,
     token_ref, chunk_ref,
     key_ref, value_ref, key_grad_ref, value_grad_ref, weight_grad_ref, proj_grad_ref,
@@ -102,7 +104,7 @@
     odd_strip, even_strip = odd_ref[...], even_ref[1 - parity]
     west = jnp.where(parity == 0, odd_strip, even_strip)
     east = jnp.where(parity == 0, even_strip, odd_strip)
-    gain = gain_ref[...]
+    gain = gain_ref[:, :width]
     weight = qkv_ref[...]
     group = head_group(width)
 
@@ -168,11 +170,13 @@
     inside = (col_gap >= 0) & (col_gap <= REACH) & (row_gap <= REACH)
     bias = jnp.where(inside, 0.0, LOWEST)
     bias = jnp.concatenate([bias] * HEADS, axis=1)
-    head_factor = factor_ref[:1]
+    lane_factors = [gain_ref[:, width + head : width + head + 1] * (1.0 / HEAD_DIM) for head in range(HEADS)]
+    head_factor = jnp.zeros((1, width), F32)
+    for head in range(HEADS):
+        head_factor = jnp.where(lane == head, jnp.broadcast_to(lane_factors[head], (1, width)), head_factor)
     factor = jnp.concatenate(
         [
-            jnp.broadcast_to(head_factor[:, head * HEAD_DIM : head * HEAD_DIM + 1], (1, band))
-            for head in range(HEADS)
+            jnp.broadcast_to(lane_factors[head], (1, band)) for head in range(HEADS)
         ],
         axis=1,
     ) * math.log2(math.e)
@@ -228,25 +232,29 @@
             jnp.where(key_rows, value_grad_ref[...], 0.0),
         ],
         axis=1,
-    ).astype(BF16)
+    )
+    projected_high = projected_grad.astype(BF16)
+    projected_low = (projected_grad - projected_high.astype(F32)).astype(BF16)
     unit, normed = own_unit_ref[...], own_normed_ref[...]
     reciprocal = own_scale_ref[:, :1]
-    normed_grad = dot(projected_grad, weight, 1, 1)
+    normed_grad = dot(projected_high, weight, 1, 1) + dot(projected_low, weight, 1, 1)
     gain_grad = jnp.sum(normed_grad * unit, axis=0, keepdims=True)
     scaled = normed_grad * gain
     token_part = reciprocal * (scaled - unit * jnp.mean(scaled * unit, axis=-1, keepdims=True))
     token_ref[...] = (own_grad.astype(F32) + token_part).astype(BF16)
     attended = jnp.where(own_rows, jnp.concatenate(attended, axis=0), 0.0).astype(BF16)
-    weight_grad = dot(projected_grad, normed, 0, 0)
+    weight_grad = dot(projected_high, normed, 0, 0)
     proj_grad = dot(own_grad, attended, 0, 0)
     for block in range(width // LANES):
         at = slice(block * LANES, (block + 1) * LANES)
         weight_grad_ref[block] = weight_grad[:, at]
         proj_grad_ref[block] = proj_grad[:, at]
-    peers, rows = chunk_ref.shape[:2]
+    peers, rows = chunk_ref.shape[1:3]
     group = (rows - TAIL) // 8
-    for peer in range(peers):
-        line, lower, side = peer // (2 * lowers), peer // 2 % lowers, peer % 2
+    for index in range(2 * peers):
+        peer, side = index // 2, index % 2
+        line, lower = peer // lowers, peer % lowers
+        half = (place_ref[0] + side) % 2
         column = line * group * lowers + lower
         for part in range(4):
             for block in range(width // LANES):
@@ -256,9 +264,9 @@
                     cells_ref, start, stride = proj_grad_ref, 2 * column + side, 2 * lowers
                 at = (2 * part + block) * group
                 cells = cells_ref.at[block][pl.ds(start, group, stride=stride), :]
-                chunk_ref[peer, at : at + group] = cells.astype(BF16)
+                chunk_ref[half, peer, at : at + group] = cells.astype(BF16)
         lanes = gain_grad[:, 2 * column // LANES * LANES :][:, :LANES]
-        chunk_ref[peer, rows - TAIL :] = jnp.broadcast_to(lanes, (TAIL, LANES)).astype(BF16)
+        chunk_ref[half, peer, rows - TAIL :] = high_low(lanes, TAIL, 2 * half)
 
 
 def middle_kernel(chunk_ref, part_ref, sum_ref):
@@ -266,7 +274,7 @@
     copies = part_ref.shape[0] // group
     total = sum(chunk_ref[peer].astype(F32) for peer in range(chunk_ref.shape[0]))
     sum_ref[...] = total[: 8 * group]
-    gains = total[8 * group : 8 * group + TAIL - 8]
+    gains = high_low(jnp.sum(total[8 * group :], axis=0, keepdims=True), TAIL - 8, 0).astype(F32)
     for column in range(group):
         rows = jnp.concatenate([sum_ref[pl.ds(column, 8, stride=group), :], gains], axis=0).astype(BF16)
         for copy in range(copies):
@@ -286,7 +294,7 @@
             else:
                 proj_ref[side : side + 1, :] = row
         here = lane == 2 * place_ref[0] % LANES + side
-        gains.append(jnp.sum(jnp.where(here, total[at + 2 : at + 3], 0.0), axis=1, keepdims=True))
+        gains.append(jnp.sum(jnp.where(here, total[at + 2 : at + 3] + total[at + 3 : at + 4], 0.0), axis=1, keepdims=True))
     gain_ref[...] = jnp.concatenate(gains, axis=1)
 
 
@@ -297,6 +305,8 @@
     place = lax.axis_index(ROWS)
     grad_scale = (row_count * row_devices * col_count * col_devices) ** (-0.5)
     parity = lax.axis_index(COLS) & 1
+    gains = jnp.concatenate([norm_gain, head_scale, jnp.zeros((LANES - HEADS,), F32)])[None, :]
+    gains, tokens, output_grad = lax.optimization_barrier((gains, tokens, output_grad))
     strips = jnp.concatenate(
         [
             tokens[:REACH],
@@ -306,7 +316,9 @@
         ],
         axis=0,
     )
-    strips, edge_tokens = lax.optimization_barrier((lax.all_gather(strips, ROWS, axis=0), edge_tokens))
+    strips, edge_tokens, tokens, output_grad = lax.optimization_barrier(
+        (lax.all_gather(strips, ROWS, axis=0), edge_tokens, tokens, output_grad)
+    )
     strips = strips.transpose(0, 2, 1, 3)
     above = strips[jnp.maximum(place - 1, 0)]
     below = strips[jnp.minimum(place + 1, row_devices - 1)]
@@ -347,8 +359,8 @@
     )
     cells = col_count * SPAN
     lowers = lax.axis_size("v")
-    peers = 2 * lax.axis_size("x") * lowers
-    group = 2 * col_devices // peers
+    peers = lax.axis_size("x") * lowers
+    group = col_devices // peers
     whole = pl.BlockSpec(memory_space=pltpu.VMEM)
     scalars = pl.BlockSpec(memory_space=pltpu.SMEM)
     even, slab, grad_slab = lax.optimization_barrier((even, slab, grad_slab))
@@ -357,7 +369,6 @@
     own_parts = pl.pallas_call(
         own_kernel,
         out_shape=(
-            jax.ShapeDtypeStruct((8, width), F32),
             wide,
             jax.ShapeDtypeStruct((cells, LANES), F32),
             narrow,
@@ -369,14 +380,13 @@
             wide,
             wide,
         ),
-        in_specs=[whole] * 6,
-        out_specs=(whole,) * 11,
+        in_specs=[whole] * 5,
+        out_specs=(whole,) * 10,
         compiler_params=pltpu.CompilerParams(vmem_limit_bytes=16 * 2**20),
     )(
-        head_scale[None, :],
         slab.reshape(cells, width),
         grad_slab.reshape(cells, width),
-        norm_gain[None, :],
+        gains,
         qkv_weight,
         out_weight,
     )
@@ -384,9 +394,9 @@
         functools.partial(block_kernel, lowers),
         out_shape=(
             jax.ShapeDtypeStruct((cells, width), BF16),
-            jax.ShapeDtypeStruct((peers, 8 * group + TAIL, LANES), BF16),
+            jax.ShapeDtypeStruct((2, peers, 8 * group + TAIL, LANES), BF16),
         ),
-        in_specs=[scalars] + [whole] * 17,
+        in_specs=[scalars] + [whole] * 16,
         out_specs=(whole,) * 2,
         scratch_shapes=[
             pltpu.VMEM((cells + 2 * REACH * SPAN, width), BF16),
@@ -402,13 +412,15 @@
         grad_slab.reshape(cells, width),
         odd.reshape(-1, width),
         even.reshape(2, -1, width),
-        norm_gain[None, :],
+        gains,
         qkv_weight,
         out_weight,
         *own_parts,
     )
     token_grad = token_grad.reshape(col_count, SPAN, width)[:, :row_count].transpose(1, 0, 2)
-    chunks = lax.all_to_all(chunks, ("x", "v", "c"), 0, 0)
+    received = lax.all_gather(chunks[1].reshape(-1, LANES), "c", axis=0)[1 - lax.axis_index("c")]
+    chunks = (chunks[0].astype(F32) + received.reshape(chunks.shape[1:]).astype(F32)).astype(BF16)
+    chunks = lax.all_to_all(chunks, ("x", "v"), 0, 0)
     halves = lax.axis_size("h")
     part = pl.pallas_call(
         middle_kernel,

time: 78.8 us -> 76.7 us (0.973)
  local copies, waits for them, and re-layouts: 3.39 us -> 1.73 us
  blocking collectives: 40.9 us -> 39.9 us
    all_to_all x1, blocking collectives: 15 us -> 9.87 us  [on_device(): chunks = lax.all_to_all(chunks, ('x', 'v'), 0, 0)]
    all_gather x0 -> x1, blocking collectives: none -> 3.14 us  [on_device(): lax.all_gather(chunks[1].reshape(-1, LANES), 'c', axis=0)]
    all_gather x1, blocking collectives: 3.59 us -> 4.61 us  [on_device(): lax.all_gather(part, 'c', axis=0, tiled=True)]
    unnamed x17 -> x15, local copies, waits for them, and re-layouts: 2.22 us -> 1.28 us
    slice x1, local copies, waits for them, and re-layouts: 0.8 us -> 0.01 us  [on_device(): tokens[:REACH]]
where the time goes in v7:
time: 76.7 us; the launch traced here: 76.3 us
  blocking collectives  39.9 us (52%)
  starting transfers between devices  16 us (21%)
  waiting for transfers between devices  10.6 us (14%)
  Pallas kernels  6.64 us (9%)
  local copies, waits for them, and re-layouts  1.73 us (2%)
  between operations  0.89 us (1%)
    all_gather x1, blocking collectives, on_device(): lax.all_gather(strips, ROWS, axis=0)  16.5 us
    all_to_all x1, waiting for transfers between devices, on_device(): lax.all_to_all(part, ('l', 'u', 'h'), 0, 0).astype(F32)  10.6 us
    all_to_all x1, blocking collectives, on_device(): chunks = lax.all_to_all(chunks, ('x', 'v'), 0, 0)  9.87 us
    ppermute x1, starting transfers between devices, on_device(): lax.ppermute(jnp.where(parity == 0, facing_west, facing_east), COLS, pair...  8.3 us
    all_to_all x1, starting transfers between devices, on_device(): lax.all_to_all(part, ('l', 'u', 'h'), 0, 0).astype(F32)  7.74 us
    all_gather x1, blocking collectives, on_device(): lax.all_gather(jnp.where(parity == 0, facing_east, facing_west), COLS, ax...  5.79 us
    pallas_call x1, Pallas kernels, on_device(): pl.pallas_call(functools.partial(block_kernel, lowers), out_shape=(jax.Sh...  4.68 us
    all_gather x1, blocking collectives, on_device(): lax.all_gather(part, 'c', axis=0, tiled=True)  4.61 us
  transfers between devices with their start and end apart: 2, of which 1 were waited for; matrix products, arithmetic and copies ran while one was open for 1% of the time, Pallas kernels for 1%

profile of v7, /device:TPU:1, one launch (start us, length us, event | category | flops | bytes accessed | tf_op | source)
XLA Modules:
  0.0 76.3 jit_solution(16245999896078155313)
XLA Ops:
  0.6 0.0 copy-start.3
  0.6 0.0 copy-start.5
  0.7 0.0 copy-start.6
  0.7 0.1 pad.16.clone
  0.8 0.1 pad.12.clone
  0.9 0.5 copy-done.5
  1.4 0.0 copy-done.6
  1.4 0.1 pad_maximum_fusion.3
  1.4 0.0 copy-done.3
  1.5 0.1 copy-done.2
  1.6 0.0 copy-start.4
  1.6 16.5 %all-gather = bf16[72,8,256]{2,1,0:T(8,128)(2,1)S(1)} all-gather(bf16[18,8,256]{2,1,0:T(8,128)(2,1)S(1)} %pad_maximum_fusion.2), channel_id=2, replica_groups=mesh['x'=4,'l'=4,'u'=4,'v'=2,'h'=2,'c'=2] {'h','c'}, dimensions={0}, use_global_device_ids=true | all-gather | bytes 368640 | tf_op jit(solution)/shard_map/all_gather | solution.py:320
  18.1 0.1 copy.18
  18.3 0.1 pad_maximum_fusion.1
  18.5 0.1 pad_maximum_fusion
  18.7 8.3 %collective-permute-start = (bf16[9,32,256]{2,1,0:T(8,128)(2,1)S(1)}, bf16[9,32,256]{2,1,0:T(8,128)(2,1)S(1)}, u32[]{:S(2)}, u32[]{:S(2)}) collective-permute-start(bf16[9,32,256]{2,1,0:T(8,128)(2,1)S(1)} %maximum_select_fusion.1), channel_id=1, source_target_pairs={{4,8},{12,16},{20,24},{28,32},{36,40},{44,48},{52,56},{60,64},{68,... | collective-permute-start | bytes 442376 | tf_op jit(solution)/shard_map/ppermute | solution.py:351
  27.0 0.0 copy-start
  27.0 0.0 copy-start.1
  27.0 5.8 %all_gather.18 = bf16[2,9,32,256]{3,2,1,0:T(8,128)(2,1)S(1)} all-gather(bf16[1,9,32,256]{3,2,1,0:T(8,128)(2,1)S(1)} %maximum_select_fusion), channel_id=1, replica_groups={{0,4},{8,12},{16,20},{24,28},{32,36},{40,44},{48,52},{56,60},{64,68},{7..., dimensions={0}, use_global_device_ids=true | all-gather | bytes 442368 | tf_op jit(solution)/shard_map/all_gather | solution.py:354
  32.8 0.6 shard_map.102
  33.4 0.1 pad_add_fusion.place_ref
  33.5 0.0 collective-permute-done
  33.5 4.7 %shard_map.103 = (bf16[256,256]{1,0:T(8,128)(2,1)S(1)}, bf16[2,8,144,128]{3,2,1,0:T(8,128)(2,1)S(1)}) custom-call(s32[3]{0:T(128)S(1)} %pad_add_fusion.place_ref, bf16[256,256]{1,0:T(8,128)(2,1)S(1)} %bitcast.49, bf16[288,256]{1,0:T(8,128)(2,1)S(1)} %bitcast.52, bf16[2,288,256]{2,1,0:T(8,128)(2,1)S(1)} %bitcast.51, f32[1,384]{1,0:T(1,128)S(1)} %broadcast_in_dim.17.gain_ref, ...), custom_call_target="tpu_custom_call" | custom-call | tf_op jit(solution)/shard_map/pallas_call | solution.py:393
  38.2 3.1 %all_gather.19 = bf16[2,1152,128]{2,1,0:T(8,128)(2,1)S(1)} all-gather(bf16[1,1152,128]{2,1,0:T(8,128)(2,1)S(1)} %bitcast.55), channel_id=1, replica_groups=mesh['x'=4,'l'=4,'u'=4,'v'=2,'h'=2,'c'=2] {'c'}, dimensions={0}, use_global_device_ids=true | all-gather | bytes 884736 | tf_op jit(solution)/shard_map/all_gather | solution.py:421
  41.4 0.1 fusion
  41.5 9.9 %all_to_all.10.chunk_ref = bf16[8,144,128]{2,1,0:T(8,128)(2,1)S(1)} all-to-all(bf16[8,144,128]{2,1,0:T(8,128)(2,1)S(1)} %fusion), channel_id=1, replica_groups=mesh['x'=4,'l'=4,'u'=4,'v'=2,'h'=2,'c'=2] {'x','v'}, dimensions={0} | all-to-all | bytes 589824 | tf_op jit(solution)/shard_map/all_to_all | solution.py:423
  51.3 0.7 shard_map.104
  52.1 7.7 %all-to-all-start.1 = ((bf16[32,16,128]{2,1,0:T(8,128)(2,1)}), bf16[32,16,128]{2,1,0:T(8,128)(2,1)S(1)}, u32[]{:S(2)}, u32[]{:S(2)}) async-start(bf16[32,16,128]{2,1,0:T(8,128)(2,1)} %shard_map.104), calls=%async_computation.1 | async-start | bytes 262144 | tf_op jit(solution)/shard_map/all_to_all | solution.py:433
  59.8 0.7 copy.27
  60.5 10.6 %all-to-all-done.1 = bf16[32,16,128]{2,1,0:T(8,128)(2,1)S(1)} async-done(((bf16[32,16,128]{2,1,0:T(8,128)(2,1)}), bf16[32,16,128]{2,1,0:T(8,128)(2,1)S(1)}, u32[]{:S(2)}, u32[]{:S(2)}) %all-to-all-start.1) | async-done | bytes 131104 | tf_op jit(solution)/shard_map/all_to_all | solution.py:433
  71.1 4.6 %all_gather.20.parts_ref = f32[32,128]{1,0:T(8,128)S(1)} all-gather(f32[16,128]{1,0:T(8,128)S(1)} %convert_reduce_fusion), channel_id=1, replica_groups=mesh['x'=4,'l'=4,'u'=4,'v'=2,'h'=2,'c'=2] {'c'}, dimensions={0}, use_global_device_ids=true | all-gather | bytes 24576 | tf_op jit(solution)/shard_map/all_gather | solution.py:444
  75.7 0.6 shard_map.105
  (26 shorter events, 0.4 us)
Async XLA Ops:
  0.6 0.8 %copy-start.3 = (bf16[16,8,256]{2,1,0:T(8,128)(2,1)S(1)}, bf16[16,8,256]{2,1,0:T(8,128)(2,1)}, u32[]{:S(2)}) copy-start(bf16[16,8,256]{2,1,0:T(8,128)(2,1)} %param.9) | copy-start | bytes 196612
  0.6 0.7 copy-start.5
  0.7 0.7 copy-start.6
  0.7 0.9 %copy-start.2 = (bf16[16,8,256]{2,1,0:T(8,128)(2,1)S(1)}, bf16[16,8,256]{2,1,0:T(8,128)(2,1)}, u32[]{:S(2)}) copy-start(bf16[16,8,256]{2,1,0:T(8,128)(2,1)} %param.7) | copy-start | bytes 196612
  1.6 16.5 %copy-start.4 = (bf16[2,3,8,256]{3,2,1,0:T(8,128)(2,1)S(1)}, bf16[2,3,8,256]{3,2,1,0:T(8,128)(2,1)}, u32[]{:S(2)}) copy-start(bf16[2,3,8,256]{3,2,1,0:T(8,128)(2,1)} %param.8) | copy-start | bytes 73732
  18.7 14.9 %collective-permute-start = (bf16[9,32,256]{2,1,0:T(8,128)(2,1)S(1)}, bf16[9,32,256]{2,1,0:T(8,128)(2,1)S(1)}, u32[]{:S(2)}, u32[]{:S(2)}) collective-permute-start(bf16[9,32,256]{2,1,0:T(8,128)(2,1)S(1)} %maximum_select_fusion.1), channel_id=1, source_target_pairs={{4,8},{12,16},{20,24},{28,32},{36,40},{44,48},{52,56},{60,64},{68,... | collective-permute-start | bytes 442376 | tf_op jit(solution)/shard_map/ppermute | solution.py:351
  27.0 5.8 %copy-start = (bf16[256,768]{1,0:T(8,128)(2,1)S(1)}, bf16[256,768]{1,0:T(8,128)(2,1)}, u32[]{:S(2)}) copy-start(bf16[256,768]{1,0:T(8,128)(2,1)} %qkv_ref.3) | copy-start | bytes 1179652
  27.0 5.8 %copy-start.1 = (bf16[256,256]{1,0:T(8,128)(2,1)S(1)}, bf16[256,256]{1,0:T(8,128)(2,1)}, u32[]{:S(2)}) copy-start(bf16[256,256]{1,0:T(8,128)(2,1)} %out_ref.3) | copy-start | bytes 393220
  52.1 19.0 %all-to-all-start.1 = ((bf16[32,16,128]{2,1,0:T(8,128)(2,1)}), bf16[32,16,128]{2,1,0:T(8,128)(2,1)S(1)}, u32[]{:S(2)}, u32[]{:S(2)}) async-start(bf16[32,16,128]{2,1,0:T(8,128)(2,1)} %shard_map.104), calls=%async_computation.1 | async-start | bytes 262144 | tf_op jit(solution)/shard_map/all_to_all | solution.py:433

commit v8 on v7

--- a/solution.py
+++ b/solution.py
@@ -91,9 +91,9 @@
 def block_kernel(
     lowers,
     place_ref, own_grad_ref, odd_ref, even_ref, gain_ref, qkv_ref, out_ref,
-    own_unit_ref, own_scale_ref, own_normed_ref, own_key_ref, own_key_recip_ref, own_key_b_ref, own_value_b_ref,
+    own_unit_ref, own_normed_ref, own_key_ref, own_key_recip_ref, own_key_b_ref, own_value_b_ref,
     own_query_ref, own_query_recip_ref, own_up_ref,
-    token_ref, chunk_ref,
+    normed_grad_ref, chunk_ref,
     key_ref, value_ref, key_grad_ref, value_grad_ref, weight_grad_ref, proj_grad_ref,
 ):
     own_count, width = own_grad_ref.shape
@@ -236,12 +236,9 @@
     projected_high = projected_grad.astype(BF16)
     projected_low = (projected_grad - projected_high.astype(F32)).astype(BF16)
     unit, normed = own_unit_ref[...], own_normed_ref[...]
-    reciprocal = own_scale_ref[:, :1]
     normed_grad = dot(projected_high, weight, 1, 1) + dot(projected_low, weight, 1, 1)
     gain_grad = jnp.sum(normed_grad * unit, axis=0, keepdims=True)
-    scaled = normed_grad * gain
-    token_part = reciprocal * (scaled - unit * jnp.mean(scaled * unit, axis=-1, keepdims=True))
-    token_ref[...] = (own_grad.astype(F32) + token_part).astype(BF16)
+    normed_grad_ref[...] = normed_grad
     attended = jnp.where(own_rows, jnp.concatenate(attended, axis=0), 0.0).astype(BF16)
     weight_grad = dot(projected_high, normed, 0, 0)
     proj_grad = dot(own_grad, attended, 0, 0)
@@ -269,6 +266,13 @@
         chunk_ref[half, peer, rows - TAIL :] = high_low(lanes, TAIL, 2 * half)
 
 
+def token_kernel(normed_grad_ref, unit_ref, scale_ref, own_grad_ref, gain_ref, token_ref):
+    unit = unit_ref[...]
+    scaled = normed_grad_ref[...] * gain_ref[:, : unit.shape[1]]
+    token_part = scale_ref[:, :1] * (scaled - unit * jnp.mean(scaled * unit, axis=-1, keepdims=True))
+    token_ref[...] = (own_grad_ref[...].astype(F32) + token_part).astype(BF16)
+
+
 def middle_kernel(chunk_ref, part_ref, sum_ref):
     group = sum_ref.shape[0] // 8
     copies = part_ref.shape[0] // group
@@ -390,13 +394,14 @@
         qkv_weight,
         out_weight,
     )
-    token_grad, chunks = pl.pallas_call(
+    unit, reciprocal, *own_parts = own_parts
+    normed_grad, chunks = pl.pallas_call(
         functools.partial(block_kernel, lowers),
         out_shape=(
-            jax.ShapeDtypeStruct((cells, width), BF16),
+            jax.ShapeDtypeStruct((cells, width), F32),
             jax.ShapeDtypeStruct((2, peers, 8 * group + TAIL, LANES), BF16),
         ),
-        in_specs=[scalars] + [whole] * 16,
+        in_specs=[scalars] + [whole] * 15,
         out_specs=(whole,) * 2,
         scratch_shapes=[
             pltpu.VMEM((cells + 2 * REACH * SPAN, width), BF16),
@@ -415,8 +420,17 @@
         gains,
         qkv_weight,
         out_weight,
+        unit,
         *own_parts,
     )
+    token_grad = pl.pallas_call(
+        token_kernel,
+        out_shape=jax.ShapeDtypeStruct((cells, width), BF16),
+        in_specs=[whole] * 5,
+        out_specs=whole,
+        compiler_params=pltpu.CompilerParams(vmem_limit_bytes=8 * 2**20),
+        cost_estimate=pl.CostEstimate(flops=16 * cells * width, bytes_accessed=8 * cells * width, transcendentals=0),
+    )(normed_grad, unit, reciprocal, grad_slab.reshape(cells, width), gains)
     token_grad = token_grad.reshape(col_count, SPAN, width)[:, :row_count].transpose(1, 0, 2)
     received = lax.all_gather(chunks[1].reshape(-1, LANES), "c", axis=0)[1 - lax.axis_index("c")]
     chunks = (chunks[0].astype(F32) + received.reshape(chunks.shape[1:]).astype(F32)).astype(BF16)

time: 76.7 us -> 76.6 us (level)
  no operation moved by 1% of the time
where the time goes in v8:
time: 76.6 us; the launch traced here: 76.2 us
  blocking collectives  39.9 us (52%)
  starting transfers between devices  16 us (21%)
  waiting for transfers between devices  10.4 us (14%)
  Pallas kernels  6.73 us (9%)
  local copies, waits for them, and re-layouts  1.73 us (2%)
  between operations  0.9 us (1%)
    all_gather x1, blocking collectives, on_device(): lax.all_gather(strips, ROWS, axis=0)  16.5 us
    all_to_all x1, waiting for transfers between devices, on_device(): lax.all_to_all(part, ('l', 'u', 'h'), 0, 0).astype(F32)  10.4 us
    all_to_all x1, blocking collectives, on_device(): chunks = lax.all_to_all(chunks, ('x', 'v'), 0, 0)  9.87 us
    ppermute x1, starting transfers between devices, on_device(): lax.ppermute(jnp.where(parity == 0, facing_west, facing_east), COLS, pair...  8.3 us
    all_to_all x1, starting transfers between devices, on_device(): lax.all_to_all(part, ('l', 'u', 'h'), 0, 0).astype(F32)  7.74 us
    all_gather x1, blocking collectives, on_device(): lax.all_gather(jnp.where(parity == 0, facing_east, facing_west), COLS, ax...  5.79 us
    all_gather x1, blocking collectives, on_device(): lax.all_gather(part, 'c', axis=0, tiled=True)  4.61 us
    pallas_call x1, Pallas kernels, on_device(): pl.pallas_call(functools.partial(block_kernel, lowers), out_shape=(jax.Sh...  4.6 us
  transfers between devices with their start and end apart: 2, of which 1 were waited for; matrix products, arithmetic and copies ran while one was open for 1% of the time, Pallas kernels for 1%

profile of v8, /device:TPU:1, one launch (start us, length us, event | category | flops | bytes accessed | tf_op | source)
XLA Modules:
  0.0 76.2 jit_solution(440857163594782072)
XLA Ops:
  0.6 0.0 copy-start.3
  0.7 0.1 pad.16.clone
  0.8 0.1 pad.12.clone
  0.9 0.5 copy-done.5
  1.4 0.0 copy-done.6
  1.4 0.1 pad_maximum_fusion.3
  1.4 0.0 copy-done.3
  1.5 0.1 copy-done.2
  1.6 0.0 copy-start.4
  1.6 16.5 %all-gather = bf16[72,8,256]{2,1,0:T(8,128)(2,1)S(1)} all-gather(bf16[18,8,256]{2,1,0:T(8,128)(2,1)S(1)} %pad_maximum_fusion.2), channel_id=2, replica_groups=mesh['x'=4,'l'=4,'u'=4,'v'=2,'h'=2,'c'=2] {'h','c'}, dimensions={0}, use_global_device_ids=true | all-gather | bytes 368640 | tf_op jit(solution)/shard_map/all_gather | solution.py:324
  18.1 0.1 copy.18
  18.3 0.1 pad_maximum_fusion.1
  18.5 0.1 pad_maximum_fusion
  18.7 8.3 %collective-permute-start = (bf16[9,32,256]{2,1,0:T(8,128)(2,1)S(1)}, bf16[9,32,256]{2,1,0:T(8,128)(2,1)S(1)}, u32[]{:S(2)}, u32[]{:S(2)}) collective-permute-start(bf16[9,32,256]{2,1,0:T(8,128)(2,1)S(1)} %maximum_select_fusion.1), channel_id=1, source_target_pairs={{4,8},{12,16},{20,24},{28,32},{36,40},{44,48},{52,56},{60,64},{68,... | collective-permute-start | bytes 442376 | tf_op jit(solution)/shard_map/ppermute | solution.py:355
  27.0 0.0 copy-start
  27.0 0.0 copy-start.1
  27.0 5.8 %all_gather.18 = bf16[2,9,32,256]{3,2,1,0:T(8,128)(2,1)S(1)} all-gather(bf16[1,9,32,256]{3,2,1,0:T(8,128)(2,1)S(1)} %maximum_select_fusion), channel_id=1, replica_groups={{0,4},{8,12},{16,20},{24,28},{32,36},{40,44},{48,52},{56,60},{64,68},{7..., dimensions={0}, use_global_device_ids=true | all-gather | bytes 442368 | tf_op jit(solution)/shard_map/all_gather | solution.py:358
  32.8 0.0 copy-done
  32.8 0.6 shard_map.102
  33.4 0.1 pad_add_fusion.place_ref
  33.5 0.0 collective-permute-done
  33.5 4.6 %shard_map.103 = (f32[256,256]{1,0:T(8,128)S(1)}, bf16[2,8,144,128]{3,2,1,0:T(8,128)(2,1)S(1)}) custom-call(s32[3]{0:T(128)S(1)} %pad_add_fusion.place_ref, bf16[256,256]{1,0:T(8,128)(2,1)S(1)} %bitcast.49, bf16[288,256]{1,0:T(8,128)(2,1)S(1)} %bitcast.54, bf16[2,288,256]{2,1,0:T(8,128)(2,1)S(1)} %bitcast.52, f32[1,384]{1,0:T(1,128)S(1)} %broadcast_in_dim.17.gain_ref, ...), custom_call_target="tpu_custom_call" | custom-call | tf_op jit(solution)/shard_map/pallas_call | solution.py:398
  38.1 3.1 %all_gather.19 = bf16[2,1152,128]{2,1,0:T(8,128)(2,1)S(1)} all-gather(bf16[1,1152,128]{2,1,0:T(8,128)(2,1)S(1)} %bitcast.56), channel_id=1, replica_groups=mesh['x'=4,'l'=4,'u'=4,'v'=2,'h'=2,'c'=2] {'c'}, dimensions={0}, use_global_device_ids=true | all-gather | bytes 884736 | tf_op jit(solution)/shard_map/all_gather | solution.py:435
  41.3 0.1 fusion
  41.4 9.9 %all_to_all.10.chunk_ref = bf16[8,144,128]{2,1,0:T(8,128)(2,1)S(1)} all-to-all(bf16[8,144,128]{2,1,0:T(8,128)(2,1)S(1)} %fusion), channel_id=1, replica_groups=mesh['x'=4,'l'=4,'u'=4,'v'=2,'h'=2,'c'=2] {'x','v'}, dimensions={0} | all-to-all | bytes 589824 | tf_op jit(solution)/shard_map/all_to_all | solution.py:437
  51.3 0.7 shard_map.105
  52.0 7.7 %all-to-all-start.1 = ((bf16[32,16,128]{2,1,0:T(8,128)(2,1)}), bf16[32,16,128]{2,1,0:T(8,128)(2,1)S(1)}, u32[]{:S(2)}, u32[]{:S(2)}) async-start(bf16[32,16,128]{2,1,0:T(8,128)(2,1)} %shard_map.105), calls=%async_computation.1 | async-start | bytes 262144 | tf_op jit(solution)/shard_map/all_to_all | solution.py:447
  59.8 0.2 shard_map.104
  59.9 0.7 copy.27
  60.6 10.4 %all-to-all-done.1 = bf16[32,16,128]{2,1,0:T(8,128)(2,1)S(1)} async-done(((bf16[32,16,128]{2,1,0:T(8,128)(2,1)}), bf16[32,16,128]{2,1,0:T(8,128)(2,1)S(1)}, u32[]{:S(2)}, u32[]{:S(2)}) %all-to-all-start.1) | async-done | bytes 131104 | tf_op jit(solution)/shard_map/all_to_all | solution.py:447
  71.0 4.6 %all_gather.20.parts_ref = f32[32,128]{1,0:T(8,128)S(1)} all-gather(f32[16,128]{1,0:T(8,128)S(1)} %convert_reduce_fusion), channel_id=1, replica_groups=mesh['x'=4,'l'=4,'u'=4,'v'=2,'h'=2,'c'=2] {'c'}, dimensions={0}, use_global_device_ids=true | all-gather | bytes 24576 | tf_op jit(solution)/shard_map/all_gather | solution.py:458
  75.6 0.6 shard_map.106
  (27 shorter events, 0.4 us)
Async XLA Ops:
  0.6 0.8 %copy-start.3 = (bf16[16,8,256]{2,1,0:T(8,128)(2,1)S(1)}, bf16[16,8,256]{2,1,0:T(8,128)(2,1)}, u32[]{:S(2)}) copy-start(bf16[16,8,256]{2,1,0:T(8,128)(2,1)} %param.9) | copy-start | bytes 196612
  0.6 0.7 copy-start.5
  0.7 0.7 copy-start.6
  0.7 0.9 %copy-start.2 = (bf16[16,8,256]{2,1,0:T(8,128)(2,1)S(1)}, bf16[16,8,256]{2,1,0:T(8,128)(2,1)}, u32[]{:S(2)}) copy-start(bf16[16,8,256]{2,1,0:T(8,128)(2,1)} %param.7) | copy-start | bytes 196612
  1.6 16.5 %copy-start.4 = (bf16[2,3,8,256]{3,2,1,0:T(8,128)(2,1)S(1)}, bf16[2,3,8,256]{3,2,1,0:T(8,128)(2,1)}, u32[]{:S(2)}) copy-start(bf16[2,3,8,256]{3,2,1,0:T(8,128)(2,1)} %param.8) | copy-start | bytes 73732
  18.7 14.9 %collective-permute-start = (bf16[9,32,256]{2,1,0:T(8,128)(2,1)S(1)}, bf16[9,32,256]{2,1,0:T(8,128)(2,1)S(1)}, u32[]{:S(2)}, u32[]{:S(2)}) collective-permute-start(bf16[9,32,256]{2,1,0:T(8,128)(2,1)S(1)} %maximum_select_fusion.1), channel_id=1, source_target_pairs={{4,8},{12,16},{20,24},{28,32},{36,40},{44,48},{52,56},{60,64},{68,... | collective-permute-start | bytes 442376 | tf_op jit(solution)/shard_map/ppermute | solution.py:355
  27.0 5.8 %copy-start = (bf16[256,768]{1,0:T(8,128)(2,1)S(1)}, bf16[256,768]{1,0:T(8,128)(2,1)}, u32[]{:S(2)}) copy-start(bf16[256,768]{1,0:T(8,128)(2,1)} %qkv_ref.3) | copy-start | bytes 1179652
  27.0 5.8 %copy-start.1 = (bf16[256,256]{1,0:T(8,128)(2,1)S(1)}, bf16[256,256]{1,0:T(8,128)(2,1)}, u32[]{:S(2)}) copy-start(bf16[256,256]{1,0:T(8,128)(2,1)} %out_ref.3) | copy-start | bytes 393220
  52.0 19.0 %all-to-all-start.1 = ((bf16[32,16,128]{2,1,0:T(8,128)(2,1)}), bf16[32,16,128]{2,1,0:T(8,128)(2,1)S(1)}, u32[]{:S(2)}, u32[]{:S(2)}) async-start(bf16[32,16,128]{2,1,0:T(8,128)(2,1)} %shard_map.105), calls=%async_computation.1 | async-start | bytes 262144 | tf_op jit(solution)/shard_map/all_to_all | solution.py:447
